TPU v7x, 32 devices: a whole 2x2x4 slice. The times are simulated.
32 devices in a mesh: seq: 8 (over z, x), tp: 4 (over y, core).
Axes of the slice: x: 2, y: 2, z: 4, core: 2. Of those that a mesh axis runs over, the one named last changes fastest.
Arguments:
- tokens: bfloat16 [4096, 2048], P('seq', 'tp'), may hold values from -6 to 6
- w_first: bfloat16 [8, 512, 512], P('seq'), may hold values from -0.25 to 0.25
- second_factor_weight: bfloat16 [512, 8, 8], P('seq'), may hold values from -2 to 2
- w_up: bfloat16 [64, 2, 128, 128], P('tp'), may hold values from -0.375 to 0.375
- w_self: bfloat16 [6, 64, 128, 128], P(None, 'tp'), may hold values from -0.375 to 0.375
- w_cross: bfloat16 [6, 64, 128, 128], P(None, 'tp'), may hold values from -0.375 to 0.375
- w_down: bfloat16 [64, 2, 128, 128], P('tp'), may hold values from -0.1875 to 0.1875
- block_pairs: int32 [64, 2], P('tp'), may hold values from 0 to 15, all different within a row
- cotangent: bfloat16 [4096, 2048], P('seq', 'tp'), may hold values from -6 to 6
Outputs:
- layer_out: bfloat16 [4096, 2048], P('seq', 'tp')
- grad_tokens: bfloat16 [4096, 2048], P('seq', 'tp')
- grad_first: float32 [8, 512, 512], P('seq')
- gradient_second_factor: float32 [512, 8, 8], P('seq')
- grad_self: float32 [6, 64, 128, 128], P(None, 'tp', 'seq')
- grad_cross: float32 [6, 64, 128, 128], P(None, 'tp', 'seq')
Inputs may be any that keep to these rules, and one draw needn't show every extreme that they name: `block_pairs`: each row names two different input blocks, and every one of the 16 input blocks is named by some row.
All inputs are finite; a program needn't handle non-finite values.
Results may differ from a plain program's by a relative error of at most 0.019.
Values may be sent and summed in bfloat16 or wider, within the bound.
A program may use at most 128 MiB of HBM per device.

v0:
```python
import math

import jax
import jax.numpy as jnp
from jax import lax
from jax.sharding import PartitionSpec as P


def partner_2(value, axis, bit):
    mask = 2**bit
    pairs = [(source, source ^ mask) for source in range(lax.axis_size(axis))]
    return lax.ppermute(value, axis, pairs)


def gelu_tanh(value):
    return jax.nn.gelu(value, approximate=True)


def swap_local(state, level):
    span = 2**level
    shape = state.shape
    folded = state.reshape(shape[0], shape[1] // (2 * span), 2, span, shape[2])
    return jnp.flip(folded, axis=2).reshape(shape)


def apply_blocks(state, weight):
    return jnp.einsum("rjc,jce->rje", state, weight, preferred_element_type=jnp.float32)


def apply_transposed(state, weight):
    return jnp.einsum("rje,jce->rjc", state, weight, preferred_element_type=jnp.float32)


def outer_blocks(left, right):
    return jnp.einsum("rjc,rje->jce", left, right, preferred_element_type=jnp.float32)


def per_device(
    tokens, w_first, second_factor_weight, w_up, w_self, w_cross, w_down, block_pairs, cotangent
):
    seq_len, width_local = tokens.shape
    group_count, block_len, _ = w_first.shape
    levels = w_self.shape[0]
    slots = w_self.shape[1]
    block_width = w_self.shape[2]
    model_width = width_local * lax.axis_size("tp")
    in_blocks = model_width // block_width
    local_bits = slots.bit_length() - 1
    total_tokens = seq_len * lax.axis_size("seq")
    token_scale = 1.0 / math.sqrt(total_tokens)
    model_width_scale = 1.0 / math.sqrt(model_width)
    grouped = tokens.reshape(group_count, block_len, width_local)
    first_factor_output = jnp.einsum(
        "acb,abd->acd", w_first, grouped, preferred_element_type=jnp.float32
    ).astype(jnp.bfloat16)
    received_rows = lax.all_to_all(
        first_factor_output, "seq", split_axis=1, concat_axis=0, tiled=True
    )
    mixed_part = jnp.einsum(
        "vyi,ivz->yvz", second_factor_weight, received_rows, preferred_element_type=jnp.float32
    ).astype(jnp.bfloat16)
    returned = lax.all_to_all(mixed_part, "seq", split_axis=0, concat_axis=1, tiled=True)
    mixed_tokens = returned
    first_factor_shifted = received_rows
    hidden_in = (
        tokens.astype(jnp.float32) + mixed_tokens.reshape(seq_len, width_local).astype(jnp.float32)
    ).astype(jnp.bfloat16)
    hidden_all, cotangent_all = (
        lax.all_gather(hidden_in, "tp", axis=1, tiled=True),
        lax.all_gather(cotangent, "tp", axis=1, tiled=True),
    )
    flat_pairs = block_pairs.reshape(-1)
    chosen = (
        block_pairs[:, :, None] == jnp.arange(in_blocks, dtype=jnp.int32)[None, None, :]
    ).astype(jnp.float32)
    picked = jnp.take(
        hidden_all.reshape(seq_len, in_blocks, block_width), flat_pairs, axis=1
    ).reshape(seq_len, slots, 2, block_width)
    state = jnp.einsum("rjkc,jkce->rje", picked, w_up, preferred_element_type=jnp.float32).astype(
        jnp.bfloat16
    )
    states = [state]
    partners = [None] * levels
    for level_at in range(levels):
        if level_at < local_bits:
            partner = swap_local(state, level_at)
        else:
            partner = partner_2(state, "tp", level_at - local_bits)
        partners[level_at] = partner
        state = (
            apply_blocks(state, w_self[level_at]) + apply_blocks(partner, w_cross[level_at])
        ).astype(jnp.bfloat16)
        states.append(state)
    top = state.astype(jnp.float32)
    activated = gelu_tanh(top).astype(jnp.bfloat16)
    pieces = jnp.einsum("rjc,jkce->rjke", activated, w_down, preferred_element_type=jnp.float32)
    down_term = jnp.einsum(
        "rjke,jki->rie", pieces, chosen, precision=lax.Precision.HIGHEST
    ).reshape(seq_len, model_width)
    down_part = lax.psum_scatter(down_term, "tp", scatter_dimension=1, tiled=True)
    layer_out = (hidden_in.astype(jnp.float32) + down_part).astype(jnp.bfloat16)
    grad_picked = jnp.take(
        cotangent_all.reshape(seq_len, in_blocks, block_width), flat_pairs, axis=1
    ).reshape(seq_len, slots, 2, block_width)
    grad_act = jnp.einsum("rjke,jkce->rjc", grad_picked, w_down, preferred_element_type=jnp.float32)
    _, pull = jax.vjp(gelu_tanh, top)
    grad_state = pull(grad_act)[0].astype(jnp.bfloat16)
    self_terms = [None] * levels
    cross_terms = [None] * levels
    for level_at in reversed(range(levels)):
        below = states[level_at]
        self_terms[level_at] = outer_blocks(below, grad_state)
        swap_bit = level_at - local_bits
        if level_at < local_bits:
            cross_terms[level_at] = outer_blocks(partners[level_at], grad_state)
            incoming = swap_local(apply_transposed(grad_state, w_cross[level_at]), level_at)
        else:
            other_grad, other_weight = partner_2((grad_state, w_cross[level_at]), "tp", swap_bit)
            incoming = apply_transposed(other_grad, other_weight)
            cross_terms[level_at] = partner_2(
                outer_blocks(below, other_grad).astype(jnp.bfloat16), "tp", swap_bit
            ).astype(jnp.float32)
        grad_state = (apply_transposed(grad_state, w_self[level_at]) + incoming).astype(
            jnp.bfloat16
        )
    back_pieces = jnp.einsum("rje,jkce->rjkc", grad_state, w_up, preferred_element_type=jnp.float32)
    spread = jnp.einsum(
        "rjkc,jki->ric", back_pieces, chosen, precision=lax.Precision.HIGHEST
    ).reshape(seq_len, model_width)
    spread_part = lax.psum_scatter(spread, "tp", scatter_dimension=1, tiled=True)
    grad_hidden = (cotangent.astype(jnp.float32) + spread_part).astype(jnp.bfloat16)
    level_self, level_cross = (
        lax.psum_scatter(jnp.stack(self_terms), "seq", scatter_dimension=2, tiled=True),
        lax.psum_scatter(jnp.stack(cross_terms), "seq", scatter_dimension=2, tiled=True),
    )
    received_rows = lax.all_to_all(
        grad_hidden.reshape(group_count, block_len, width_local),
        "seq",
        split_axis=1,
        concat_axis=0,
        tiled=True,
    )
    moved_back = jnp.einsum(
        "emj,meg->jeg", second_factor_weight, received_rows, preferred_element_type=jnp.float32
    ).astype(jnp.bfloat16)
    returned = lax.all_to_all(moved_back, "seq", split_axis=0, concat_axis=1, tiled=True)
    second_part = jnp.einsum(
        "tfm,lfm->ftl", received_rows, first_factor_shifted, preferred_element_type=jnp.float32
    )
    first_part = jnp.einsum("acd,abd->acb", returned, grouped, preferred_element_type=jnp.float32)
    second_sum, first_sum = lax.psum((second_part, first_part), "tp")
    grad_mix = jnp.einsum(
        "acb,acd->abd", w_first, returned, preferred_element_type=jnp.float32
    ).reshape(seq_len, width_local)
    grad_tokens = (grad_hidden.astype(jnp.float32) + grad_mix).astype(jnp.bfloat16)
    return (
        layer_out,
        grad_tokens,
        first_sum * model_width_scale,
        second_sum * model_width_scale,
        level_self * token_scale,
        level_cross * token_scale,
    )


def solution(mesh):
    in_specs = (
        P("seq", "tp"),
        P("seq", None, None),
        P("seq", None, None),
        P("tp", None, None, None),
        P(None, "tp", None, None),
        P(None, "tp", None, None),
        P("tp", None, None, None),
        P("tp", None),
        P("seq", "tp"),
    )
    out_specs = (
        P("seq", "tp"),
        P("seq", "tp"),
        P("seq", None, None),
        P("seq", None, None),
        P(None, "tp", "seq", None),
        P(None, "tp", "seq", None),
    )
    return jax.shard_map(
        per_device, mesh=mesh, in_specs=in_specs, out_specs=out_specs, check_vma=False
    )
```

profile of v0, /device:TPU:0, one launch (start us, length us, event | category | flops | bytes accessed | tf_op | source)
XLA Modules:
  0.0 734.1 jit_solution(11716601679448760789)
XLA Ops:
  7.2 2.1 copy.159
  12.4 3.8 reduce
  17.4 7.3 all-to-all-start
  24.8 14.3 %all-to-all-done = bf16[8,2,16384]{2,1,0:T(2,128)(2,1)S(1)} async-done(((bf16[8,2,16384]{2,1,0:T(2,128)(2,1)}), bf16[8,2,16384]{2,1,0:T(2,128)(2,1)S(1)}, u32[]{:S(2)}, u32[]{:S(2)}) %all-to-all-start) | async-done | bytes 524320 | tf_op jit(solution)/shard_map/all_to_all | solution.py:56
  41.2 18.1 %all_to_all.42 = bf16[8,64,512]{2,1,0:T(8,128)(2,1)S(1)} all-to-all(bf16[8,64,512]{2,1,0:T(8,128)(2,1)S(1)} %copy.146), channel_id=1, replica_groups=mesh['seq'=8,'tp'=4] {'seq'}, dimensions={0} | all-to-all | bytes 1048576 | tf_op jit(solution)/shard_map/all_to_all | solution.py:62
  60.6 3.0 copy.161
  63.6 3.1 gather_fusion.1
  66.7 15.4 %all-gather.3.cloned.1.call-done = bf16[512,2048]{1,0:T(8,128)(2,1)} async-done(((bf16[512,512]{1,0:T(8,128)(2,1)}), bf16[512,2048]{1,0:T(8,128)(2,1)}) %all-gather.3.cloned.1.call-update) | async-done | bytes 2097168 | tf_op jit(solution)/shard_map/all_gather | solution.py:69
  82.1 4.0 copy.148
  86.1 3.0 copy.149
  89.1 3.1 gather_fusion
  92.2 5.5 broadcast_select_fusion
  100.6 1.9 fusion.45
  104.3 4.1 fusion.41
  109.9 3.7 add_convert_fusion.6
  113.6 4.1 fusion.37
  119.2 3.7 add_convert_fusion.5
  123.0 4.1 fusion.33
  128.6 3.8 fusion.51
  133.9 2.8 collective-permute-done
  138.7 46.5 %collective-permute-done.1 = bf16[512,16,128]{2,0,1:T(8,128)(2,1)S(1)} collective-permute-done((bf16[512,16,128]{2,0,1:T(8,128)(2,1)S(1)}, bf16[512,16,128]{2,0,1:T(8,128)(2,1)S(1)}, u32[]{:S(2)}, u32[]{:S(2)}) %collective-permute-start.1) | collective-permute-done | bytes 2097184 | tf_op jit(solution)/shard_map/ppermute | solution.py:12
  187.2 14.8 %fusion.10 = bf16[512,16,128]{2,0,1:T(8,128)(2,1)S(1)} fusion(bf16[16,512,128]{2,1,0:T(8,128)(2,1)S(1)} %add_convert_fusion.2, bf16[512,16,2,128]{3,0,2,1:T(8,128)(2,1)S(1)} %bitcast.396, bf16[16,2,128,128]{3,2,1,0:T(8,128)(2,1)S(1)} %copy-done.41), kind=kOutput, calls=%fused_computation.14 | convolution fusion | flops 558891008 | bytes 9437184 | tf_op jit(solution)/shard_map/rjke,jkce->rjc/dot_general | solution.py:105
  205.0 55.3 %collective-permute-done.3 = bf16[16,128,128]{2,1,0:T(8,128)(2,1)S(1)} collective-permute-done((bf16[16,128,128]{2,1,0:T(8,128)(2,1)S(1)}, bf16[16,128,128]{2,1,0:T(8,128)(2,1)S(1)}, u32[]{:S(2)}, u32[]{:S(2)}) %collective-permute-start.3) | collective-permute-done | bytes 524320 | tf_op jit(solution)/shard_map/ppermute | solution.py:12
  263.0 3.5 collective-permute-done.5
  267.9 2.7 fusion.29
  270.6 4.6 rev.36
  275.2 3.1 fusion.14
  278.2 4.1 fusion.111
  282.3 4.6 rev.37
  286.9 3.7 fusion.13
  290.7 4.1 fusion.116
  294.8 4.6 rev.38
  299.4 3.7 fusion.12
  303.1 4.1 fusion.121
  307.2 4.6 rev.39
  311.8 3.7 fusion.11
  316.8 11.6 %fusion.19 = f32[512,16,128]{2,1,0:T(8,128)} fusion(f32[512,16,2,128]{3,0,2,1:T(8,128)S(1)} %convolution_bitcast_fusion, s32[16,2]{0,1:T(2,128)S(1)} %copy-done.40), kind=kOutput, calls=%fused_computation.44 | convolution fusion | flops 402653696 | bytes 12583040 | tf_op jit(solution)/shard_map/rjkc,jki->ric/dot_general | solution.py:127
  328.4 5.3 copy.206
  334.2 3.4 convolution_bitcast_fusion.1
  337.6 8.0 %fusion.2 = f32[16,512,128,1]{2,0,3,1:T(8,128)S(1)} fusion(f32[512,16,2,128]{3,0,2,1:T(8,128)S(1)} %convolution_bitcast_fusion.1, s32[16,2]{0,1:T(2,128)S(1)} %copy-done.40), kind=kOutput, calls=%fused_computation.4 | convolution fusion | flops 402653696 | bytes 12583040 | tf_op jit(solution)/shard_map/rjke,jki->rie/dot_general | solution.py:97
  345.6 3.9 copy.226
  349.6 28.8 %reduce-scatter.7.cloned.1.call-done = f32[512,512]{0,1:T(8,128)} async-done(((f32[512,2048]{0,1:T(8,128)}), f32[512,512]{0,1:T(8,128)}) %reduce-scatter.7.cloned.1.call-update) | async-done | bytes 1048592 | tf_op jit(solution)/shard_map/reduce_scatter | solution.py:130
  378.4 2.5 fusion.162
  380.9 3.6 copy.164
  384.4 5.7 reduce.1
  390.1 2.2 reshape.187
  392.4 5.5 all-to-all-start.2
  397.8 4.4 fusion.57
  402.3 10.2 %all-to-all-done.2 = bf16[8,2,16384]{2,1,0:T(2,128)(2,1)} async-done(((bf16[8,2,16384]{2,1,0:T(2,128)(2,1)}), bf16[8,2,16384]{2,1,0:T(2,128)(2,1)}, u32[]{:S(2)}, u32[]{:S(2)}) %all-to-all-start.2) | async-done | bytes 524320 | tf_op jit(solution)/shard_map/all_to_all | solution.py:136
  412.5 3.5 reshape.188
  419.5 4.1 all-to-all-start.3
  423.7 4.2 fusion.63
  431.4 6.5 all-to-all-done.3
  437.9 2.6 convolution_bitcast_fusion.7
  440.6 4.1 fusion.92
  446.8 3.2 convolution_convert_fusion.3
  461.2 4.7 collective-permute-done.7
  468.1 2.2 add_convert_fusion.9
  472.1 15.3 %psum.15 = f32[64,8,8]{2,1,0:T(8,128)S(1)} all-reduce(f32[64,8,8]{2,1,0:T(8,128)S(1)} %fusion.128), channel_id=1, replica_groups=mesh['seq'=8,'tp'=4] {'tp'}, use_global_device_ids=true, to_apply=%region_3.5 | all-reduce | flops 4096 | bytes 32768 | tf_op jit(solution)/shard_map/psum | solution.py:151
  490.9 2.4 broadcast_multiply_fusion
  493.3 110.0 %reduce-scatter.9.cloned.1.call-done = f32[6,16,16,128]{3,2,1,0:T(8,128)} async-done(((f32[6,16,128,128]{3,2,1,0:T(8,128)}), f32[6,16,16,128]{3,2,1,0:T(8,128)}) %reduce-scatter.9.cloned.1.call-update) | async-done | bytes 786448 | tf_op jit(solution)/shard_map/reduce_scatter | solution.py:133
  603.3 2.1 broadcast_multiply_fusion.2
  605.4 119.5 %reduce-scatter.11.cloned.1.call-done = f32[6,16,16,128]{3,2,1,0:T(8,128)} async-done(((f32[6,16,128,128]{3,2,1,0:T(8,128)}), f32[6,16,16,128]{3,2,1,0:T(8,128)}) %reduce-scatter.11.cloned.1.call-update) | async-done | bytes 786448 | tf_op jit(solution)/shard_map/reduce_scatter | solution.py:134
  724.9 2.1 broadcast_multiply_fusion.1
  (161 shorter events, 58.6 us)
Async XLA Ops:
  7.2 90.6 %copy-start = (bf16[16,2,128,128]{3,2,1,0:T(8,128)(2,1)S(1)}, bf16[16,2,128,128]{3,2,1,0:T(8,128)(2,1)}, u32[]{:S(2)}) copy-start(bf16[16,2,128,128]{3,2,1,0:T(8,128)(2,1)} %param.14) | copy-start | bytes 3145732
  7.2 53.4 %all-gather.5.cloned.1.call-start = ((), (), s32[]{:S(2)}) async-start(), calls=%async_computation.10 | async-start | bytes 2621440 | tf_op jit(solution)/shard_map/all_gather | solution.py:70
  9.4 15.3 %copy-start.39 = (bf16[64,8,8]{0,2,1:T(8,128)(2,1)S(1)}, bf16[64,8,8]{0,2,1:T(8,128)(2,1)}, u32[]{:S(2)}) copy-start(bf16[64,8,8]{0,2,1:T(8,128)(2,1)} %param.13) | copy-start | bytes 24580
  17.4 21.7 %all-to-all-start = ((bf16[8,2,16384]{2,1,0:T(2,128)(2,1)}), bf16[8,2,16384]{2,1,0:T(2,128)(2,1)S(1)}, u32[]{:S(2)}, u32[]{:S(2)}) async-start(bf16[8,2,16384]{2,1,0:T(2,128)(2,1)} %reshape.185), calls=%async_computation | async-start | bytes 1048576 | tf_op jit(solution)/shard_map/all_to_all | solution.py:56
  24.6 57.5 %all-gather.3.cloned.1.call-start = ((), (), s32[]{:S(2)}) async-start(), calls=%async_computation.8 | async-start | bytes 2621440 | tf_op jit(solution)/shard_map/all_gather | solution.py:69
  24.8 34.5 %copy-start.32 = (bf16[512,512]{1,0:T(8,128)(2,1)S(1)}, bf16[512,512]{1,0:T(8,128)(2,1)}, u32[]{:S(2)}) copy-start(bf16[512,512]{1,0:T(8,128)(2,1)} %param.11) | copy-start | bytes 1572868
  39.6 20.7 %copy-start.40 = (s32[16,2]{0,1:T(2,128)S(1)}, s32[16,2]{0,1:T(2,128)}, u32[]{:S(2)}) copy-start(s32[16,2]{0,1:T(2,128)} %param.18) | copy-start | bytes 388
  39.8 0.8 copy-start.37
  60.3 318.1 %reduce-scatter.7.cloned.1.call-start = ((), (), s32[]{:S(2)}) async-start(), calls=%async_computation.11 | async-start | bytes 5242880 | tf_op jit(solution)/shard_map/reduce_scatter | solution.py:130
  99.0 3.5 copy-start.17
  100.6 1.9 copy-start.18
  104.3 4.1 copy-start.12
  113.6 4.1 copy-start.13
  123.0 4.1 copy-start.15
  128.6 4.2 copy-start.25
  132.4 1.4 copy-start.8
  132.4 4.2 copy-start.24
  132.4 4.2 collective-permute-start
  137.4 1.3 copy-start.10
  137.4 47.8 %collective-permute-start.1 = (bf16[512,16,128]{2,0,1:T(8,128)(2,1)S(1)}, bf16[512,16,128]{2,0,1:T(8,128)(2,1)S(1)}, u32[]{:S(2)}, u32[]{:S(2)}) collective-permute-start(bf16[512,16,128]{2,0,1:T(8,128)(2,1)S(1)} %fusion.52), channel_id=1, source_target_pairs={{0,2},{1,3},{2,0},{3,1},{4,6},{5,7},{6,4},{7,5},{8,10},{9,11},{10,... | collective-permute-start | bytes 6291464 | tf_op jit(solution)/shard_map/ppermute | solution.py:12
  138.7 48.5 %copy-start.34 = (bf16[32,512,128]{2,1,0:T(8,128)(2,1)S(1)}, bf16[32,512,128]{2,1,0:T(8,128)(2,1)}, u32[]{:S(2)}) copy-start(bf16[32,512,128]{2,1,0:T(8,128)(2,1)} %get-tuple-element.39) | copy-start | bytes 12582916
  138.7 48.5 %copy-start.41 = (bf16[16,2,128,128]{3,2,1,0:T(8,128)(2,1)S(1)}, bf16[16,2,128,128]{3,2,1,0:T(8,128)(2,1)}, u32[]{:S(2)}) copy-start(bf16[16,2,128,128]{3,2,1,0:T(8,128)(2,1)} %param.17) | copy-start | bytes 3145732
  185.9 1.3 copy-start.36
  202.1 3.0 copy-start.29
  202.1 58.3 %collective-permute-start.2 = (bf16[512,16,128]{2,0,1:T(8,128)(2,1)S(1)}, bf16[512,16,128]{2,0,1:T(8,128)(2,1)S(1)}, u32[]{:S(2)}, u32[]{:S(2)}) collective-permute-start(bf16[512,16,128]{2,0,1:T(8,128)(2,1)S(1)} %fusion.10), channel_id=1, source_target_pairs={{0,2},{1,3},{2,0},{3,1},{4,6},{5,7},{6,4},{7,5},{8,10},{9,11},{10,... | collective-permute-start | bytes 6291464 | tf_op jit(solution)/shard_map/ppermute | solution.py:12
  202.5 57.8 %collective-permute-start.3 = (bf16[16,128,128]{2,1,0:T(8,128)(2,1)S(1)}, bf16[16,128,128]{2,1,0:T(8,128)(2,1)S(1)}, u32[]{:S(2)}, u32[]{:S(2)}) collective-permute-start(bf16[16,128,128]{2,1,0:T(8,128)(2,1)S(1)} %get-tuple-element.38), channel_id=1, source_target_pairs={{0,2},{1,3},{2,0},{3,1},{4,6},{5,7},{6,4},{7,5},{8,10},{9,11},{10,... | collective-permute-start | bytes 1572872 | tf_op jit(solution)/shard_map/ppermute | solution.py:12
  260.3 1.3 copy-start.26
  261.6 1.4 copy-start.23
  261.6 4.9 collective-permute-start.4
  261.7 4.9 collective-permute-start.5
  266.6 1.3 copy-start.27
  278.2 4.1 copy-start.1
  290.7 4.1 copy-start.4
  303.1 4.1 copy-start.6
  333.7 133.4 %reduce-scatter.5.cloned.1.call-start = ((), (), s32[]{:S(2)}) async-start(), calls=%async_computation.9 | async-start | bytes 5242880 | tf_op jit(solution)/shard_map/reduce_scatter | solution.py:100
  392.4 20.1 %all-to-all-start.2 = ((bf16[8,2,16384]{2,1,0:T(2,128)(2,1)}), bf16[8,2,16384]{2,1,0:T(2,128)(2,1)}, u32[]{:S(2)}, u32[]{:S(2)}) async-start(bf16[8,2,16384]{2,1,0:T(2,128)(2,1)} %reshape.187), calls=%async_computation.4 | async-start | bytes 1048576 | tf_op jit(solution)/shard_map/all_to_all | solution.py:136
  417.3 0.8 copy-start.38
  419.5 18.4 %all-to-all-start.3 = ((bf16[8,64,512]{2,1,0:T(8,128)(2,1)}), bf16[8,64,512]{2,1,0:T(8,128)(2,1)}, u32[]{:S(2)}, u32[]{:S(2)}) async-start(bf16[8,64,512]{2,1,0:T(8,128)(2,1)} %copy.167), calls=%async_computation.5 | async-start | bytes 1048576 | tf_op jit(solution)/shard_map/all_to_all | solution.py:146
  423.6 67.3 %all-reduce.2.cloned.1.call-start = ((), (), s32[]{:S(2)}) async-start(), calls=%async_computation.12 | async-start | bytes 2097152 | tf_op jit(solution)/shard_map/psum | solution.py:151
  423.7 4.2 copy-start.2
  423.7 4.2 copy-start.14
  427.9 1.7 copy-start.16
  440.6 162.7 %reduce-scatter.9.cloned.1.call-start = ((), (), s32[]{:S(2)}) async-start(), calls=%async_computation.13 | async-start | bytes 7077888 | tf_op jit(solution)/shard_map/reduce_scatter | solution.py:133
  440.6 4.1 copy-start.11
  440.6 4.1 copy-start.30
  446.5 278.4 %reduce-scatter.11.cloned.1.call-start = ((), (), s32[]{:S(2)}) async-start(), calls=%async_computation.14 | async-start | bytes 7077888 | tf_op jit(solution)/shard_map/reduce_scatter | solution.py:134
  446.8 3.7 copy-start.9
  446.8 3.7 copy-start.28
  450.0 1.7 copy-start.7
  450.0 2.3 copy-start.19
  450.0 15.8 %collective-permute-start.7 = (bf16[16,128,128]{2,1,0:T(8,128)(2,1)S(1)}, bf16[16,128,128]{2,1,0:T(8,128)(2,1)S(1)}, u32[]{:S(2)}, u32[]{:S(2)}) collective-permute-start(bf16[16,128,128]{2,1,0:T(8,128)(2,1)S(1)} %convolution_convert_fusion.3), channel_id=1, source_target_pairs={{0,2},{1,3},{2,0},{3,1},{4,6},{5,7},{6,4},{7,5},{8,10},{9,11},{10,... | collective-permute-start | bytes 1572872 | tf_op jit(solution)/shard_map/ppermute | solution.py:12
  451.3 2.7 copy-start.5
  451.3 2.7 copy-start.20
  451.3 8.8 %collective-permute-start.6 = (bf16[16,128,128]{2,1,0:T(8,128)(2,1)S(1)}, bf16[16,128,128]{2,1,0:T(8,128)(2,1)S(1)}, u32[]{:S(2)}, u32[]{:S(2)}) collective-permute-start(bf16[16,128,128]{2,1,0:T(8,128)(2,1)S(1)} %convolution_convert_fusion.4), channel_id=1, source_target_pairs={{0,1},{1,0},{2,3},{3,2},{4,5},{5,4},{6,7},{7,6},{8,9},{9,8},{10,11... | collective-permute-start | bytes 1572872 | tf_op jit(solution)/shard_map/ppermute | solution.py:12
  454.1 1.8 copy-start.3
  454.1 2.6 copy-start.21
  456.7 1.7 copy-start.22
  467.0 1.1 copy-start.33
  467.0 21.2 %copy-start.31 = (bf16[512,512]{0,1:T(8,128)(2,1)S(1)}, bf16[512,512]{0,1:T(8,128)(2,1)}, u32[]{:S(2)}) copy-start(bf16[512,512]{0,1:T(8,128)(2,1)} %copy.159) | copy-start | bytes 1572868
  467.0 21.2 %copy-start.35 = (f32[512,512]{0,1:T(8,128)S(1)}, f32[512,512]{0,1:T(8,128)}, u32[]{:S(2)}) copy-start(f32[512,512]{0,1:T(8,128)} %reduce-scatter.7.cloned.1.call-done) | copy-start | bytes 3145732
Sparse Core Ops, SparseCore 0:
  10.2 25.2 all-gather.4
  60.4 21.6 all-gather.2
  333.8 44.5 reduce-scatter.6
  380.9 44.5 reduce-scatter.4
  440.7 39.7 all-reduce.1
  484.4 118.8 reduce-scatter.8
  607.3 117.5 reduce-scatter.10
where the time goes:
time: 737 us; the launch traced here: 734 us
  waiting for transfers between devices  418 us (57%)
  matrix products  140 us (19%)
  local copies, waits for them, and re-layouts  76.7 us (10%)
  blocking collectives  33.4 us (5%)
  other arithmetic  29.5 us (4%)
  starting transfers between devices  21.7 us (3%)
  between operations  15 us (2%)
    reduce_scatter x1, waiting for transfers between devices, per_device(): lax.psum_scatter(jnp.stack(cross_terms), 'seq', scatter_dimension=2, tile...  119 us
    ppermute x8, waiting for transfers between devices, partner_2(): return lax.ppermute(value, axis, pairs)  113 us
    reduce_scatter x1, waiting for transfers between devices, per_device(): lax.psum_scatter(jnp.stack(self_terms), 'seq', scatter_dimension=2, tiled...  110 us
    dot_general x12, matrix products, apply_transposed(): jnp.einsum('rje,jce->rjc', state, weight, preferred_element_type=jnp.floa...  32 us
    dot_general x12, matrix products, apply_blocks(): jnp.einsum('rjc,jce->rje', state, weight, preferred_element_type=jnp.floa...  30 us
    dot_general x12, matrix products, outer_blocks(): jnp.einsum('rjc,rje->jce', left, right, preferred_element_type=jnp.float32)  28.9 us
    reduce_scatter x1, waiting for transfers between devices, per_device(): lax.psum_scatter(spread, 'tp', scatter_dimension=1, tiled=True)  28.8 us
    unnamed x97, local copies, waits for them, and re-layouts  25.1 us
  transfers between devices with their start and end apart: 18, of which 12 were waited for; matrix products, arithmetic and copies ran while one was open for 14% of the time, Pallas kernels for 0%

commit v1 on v0

v1 whole, which is shorter than its diff:
```python
import functools
import math

import jax
import jax.numpy as jnp
from jax import lax
from jax.experimental import pallas as pl
from jax.experimental.pallas import tpu as pltpu
from jax.sharding import PartitionSpec as P

BF = jnp.bfloat16
F32 = jnp.float32
VMEM_BYTES = 56 * 1024 * 1024


def dot(left, right, contract):
    return lax.dot_general(left, right, (contract, ((), ())), preferred_element_type=F32)


def dot_nn(left, right):
    return dot(left, right, ((1,), (0,)))


def dot_nt(left, right):
    return dot(left, right, ((1,), (1,)))


def dot_tn(left, right):
    return dot(left, right, ((0,), (0,)))


def partner_2(value, axis, bit):
    mask = 2**bit
    pairs = [(source, source ^ mask) for source in range(lax.axis_size(axis))]
    return lax.ppermute(value, axis, pairs)


def lanes(index, width):
    return pl.ds(pl.multiple_of(index * width, width), width)


def pair_of(index, level):
    low = 2**level
    first = (index // low) * (2 * low) + index % low
    return first, first + low


def pair_matrix(w_self, w_cross, first, second):
    top = jnp.concatenate([w_self[0, first], w_cross[0, second]], axis=1)
    bottom = jnp.concatenate([w_cross[0, first], w_self[0, second]], axis=1)
    return jnp.concatenate([top, bottom], axis=0)


def side_by_side(ref, first, second, width):
    return jnp.concatenate([ref[:, lanes(first, width)], ref[:, lanes(second, width)]], axis=1)


def up_kernel(levels, slots, width, pairs, hidden, w_up, *refs):
    w_self, w_cross, states = refs[:levels], refs[levels : 2 * levels], refs[2 * levels :]

    @pl.loop(0, slots)
    def _(j):
        both = side_by_side(hidden, pairs[j, 0], pairs[j, 1], width)
        matrix = jnp.concatenate([w_up[j, 0], w_up[j, 1]], axis=0)
        states[0][:, lanes(j, width)] = dot_nn(both, matrix).astype(BF)

    for level in range(levels):

        @pl.loop(0, slots // 2)
        def _(index):
            first, second = pair_of(index, level)
            both = side_by_side(states[level], first, second, width)
            result = dot_nn(both, pair_matrix(w_self[level], w_cross[level], first, second)).astype(BF)
            states[level + 1][:, lanes(first, width)] = result[:, :width]
            states[level + 1][:, lanes(second, width)] = result[:, width:]


def across_kernel(slots, width, state, partner, w_self, w_cross, out):
    @pl.loop(0, slots)
    def _(j):
        both = jnp.concatenate([state[:, lanes(j, width)], partner[:, lanes(j, width)]], axis=1)
        matrix = jnp.concatenate([w_self[0, j], w_cross[0, j]], axis=0)
        out[:, lanes(j, width)] = dot_nn(both, matrix).astype(BF)


def top_kernel(
    slots, width, pairs, state, partner, w_self, w_cross, w_down, cotangent, down, grad, send, total
):
    total[...] = jnp.zeros_like(total)

    @pl.loop(0, slots)
    def _(j):
        first, second = pairs[j, 0], pairs[j, 1]
        both = jnp.concatenate([state[:, lanes(j, width)], partner[:, lanes(j, width)]], axis=1)
        matrix = jnp.concatenate([w_self[0, j], w_cross[0, j]], axis=0)
        top = dot_nn(both, matrix).astype(BF).astype(F32)
        root = math.sqrt(2.0 / math.pi)
        square = top * top
        bend = jnp.tanh(root * (top + 0.044715 * (square * top)))
        active = (0.5 * top * (1.0 + bend)).astype(BF)
        slope = 0.5 * (1.0 + bend) + 0.5 * top * (1.0 - bend * bend) * (
            root * (1.0 + (3 * 0.044715) * square)
        )
        w_both = jnp.concatenate([w_down[j, 0], w_down[j, 1]], axis=1)
        pieces = dot_nn(active, w_both)
        total[:, lanes(first, width)] += pieces[:, :width]
        total[:, lanes(second, width)] += pieces[:, width:]
        grad_act = dot_nt(side_by_side(cotangent, first, second, width), w_both)
        grad_top = (grad_act * slope).astype(BF)
        grad[:, lanes(j, width)] = grad_top
        send[:, lanes(j, width)] = dot_nt(grad_top, w_cross[0, j]).astype(BF)

    down[...] = total[...].astype(BF)


def across_grad_kernel(slots, width, state, partner, grad, terms):
    @pl.loop(0, slots)
    def _(j):
        both = jnp.concatenate([state[:, lanes(j, width)], partner[:, lanes(j, width)]], axis=1)
        result = dot_tn(both, grad[:, lanes(j, width)]).astype(BF)
        terms[0, j] = result[:width]
        terms[1, j] = result[width:]


def middle_kernel(slots, width, grad, incoming, w_self, w_cross_below, out, send):
    @pl.loop(0, slots)
    def _(j):
        own = dot_nt(grad[:, lanes(j, width)], w_self[0, j])
        result = (own + incoming[:, lanes(j, width)].astype(F32)).astype(BF)
        out[:, lanes(j, width)] = result
        send[:, lanes(j, width)] = dot_nt(result, w_cross_below[0, j]).astype(BF)


def down_kernel(levels, slots, width, pairs, grad, incoming, w_self_above, w_up, *refs):
    w_self, w_cross = refs[:levels], refs[levels : 2 * levels]
    grads = refs[2 * levels : 3 * levels + 1]
    spread, total = refs[3 * levels + 1 :]

    @pl.loop(0, slots)
    def _(j):
        own = dot_nt(grad[:, lanes(j, width)], w_self_above[0, j])
        result = own + incoming[:, lanes(j, width)].astype(F32)
        grads[levels][:, lanes(j, width)] = result.astype(BF)

    for level in reversed(range(levels)):

        @pl.loop(0, slots // 2)
        def _(index):
            first, second = pair_of(index, level)
            both = side_by_side(grads[level + 1], first, second, width)
            result = dot_nt(both, pair_matrix(w_self[level], w_cross[level], first, second)).astype(BF)
            grads[level][:, lanes(first, width)] = result[:, :width]
            grads[level][:, lanes(second, width)] = result[:, width:]

    total[...] = jnp.zeros_like(total)

    @pl.loop(0, slots)
    def _(j):
        matrix = jnp.concatenate([w_up[j, 0], w_up[j, 1]], axis=0)
        pieces = dot_nt(grads[0][:, lanes(j, width)], matrix)
        total[:, lanes(pairs[j, 0], width)] += pieces[:, :width]
        total[:, lanes(pairs[j, 1], width)] += pieces[:, width:]

    spread[...] = total[...].astype(BF)


def pair_grad_kernel(level, slots, width, state, grad, terms):
    @pl.loop(0, slots // 2)
    def _(index):
        first, second = pair_of(index, level)
        result = dot_tn(
            side_by_side(state, first, second, width), side_by_side(grad, first, second, width)
        ).astype(BF)
        terms[0, first] = result[:width, :width]
        terms[1, second] = result[:width, width:]
        terms[1, first] = result[width:, :width]
        terms[0, second] = result[width:, width:]


def whole(array):
    return pl.BlockSpec(array.shape, lambda i: (0,) * array.ndim)


def level_of(array, level):
    return pl.BlockSpec((1,) + array.shape[1:], lambda i: (level, 0, 0, 0))


def rows_of(shape, tile):
    return pl.BlockSpec((tile, shape[1]), lambda i: (i, 0))


def call(kernel, steps, operands, in_specs, out_shapes, out_specs, flops, scratch=()):
    moved = sum(x.size * x.dtype.itemsize for x in operands[:4])
    moved += sum(math.prod(x.shape) * x.dtype.itemsize for x in out_shapes)
    return pl.pallas_call(
        kernel,
        grid=(steps,),
        in_specs=in_specs,
        out_specs=out_specs,
        out_shape=out_shapes,
        scratch_shapes=scratch,
        compiler_params=pltpu.CompilerParams(vmem_limit_bytes=VMEM_BYTES),
        cost_estimate=pl.CostEstimate(flops=flops, bytes_accessed=moved, transcendentals=0),
    )(*operands)


def per_device(
    tokens, w_first, second_factor_weight, w_up, w_self, w_cross, w_down, block_pairs, cotangent
):
    seq_len, width_local = tokens.shape
    levels, slots, width, _ = w_self.shape
    model_width = width_local * lax.axis_size("tp")
    local = slots.bit_length() - 1
    hidden_width = slots * width
    total_tokens = seq_len * lax.axis_size("seq")
    token_scale = 1.0 / math.sqrt(total_tokens)
    model_width_scale = 1.0 / math.sqrt(model_width)
    positions, groups, _ = second_factor_weight.shape
    tile = seq_len // 2
    steps = 2
    smem = pl.BlockSpec(memory_space=pltpu.SMEM)
    state_shape = jax.ShapeDtypeStruct((seq_len, hidden_width), BF)
    model_shape = jax.ShapeDtypeStruct((seq_len, model_width), BF)
    terms_shape = jax.ShapeDtypeStruct((2, slots, width, width), BF)
    row_state = rows_of(state_shape.shape, tile)
    row_model = rows_of(model_shape.shape, tile)
    unit = 2 * seq_len * hidden_width * width

    cotangent_all = lax.all_gather(cotangent, "tp", axis=1, tiled=True)

    same = jnp.eye(positions, dtype=BF)
    mixer = (
        second_factor_weight.transpose(1, 0, 2)[:, :, :, None] * same[None, :, None, :]
    ).reshape(groups * positions, groups * positions)

    first_factor = w_first[0]
    first_out = dot_nn(first_factor, tokens).astype(BF)
    first_rows = lax.all_to_all(first_out, "seq", split_axis=0, concat_axis=0, tiled=True)
    mixed_part = dot_nn(mixer, first_rows).astype(BF)
    mixed = lax.all_to_all(mixed_part, "seq", split_axis=0, concat_axis=0, tiled=True)
    hidden_in = (tokens.astype(F32) + mixed.astype(F32)).astype(BF)
    hidden_all = lax.all_gather(hidden_in, "tp", axis=1, tiled=True)

    local_self = [w_self] * local
    local_cross = [w_cross] * local
    local_specs = [level_of(w_self, level) for level in range(local)]
    states = call(
        functools.partial(up_kernel, local, slots, width),
        steps,
        [block_pairs, hidden_all, w_up, *local_self, *local_cross],
        [smem, row_model, whole(w_up), *local_specs, *local_specs],
        [state_shape] * (local + 1),
        [row_state] * (local + 1),
        (local + 1) * 2 * unit,
    )
    states = list(states)
    partners = [None] * levels
    for level in range(local, levels - 1):
        partners[level] = partner_2(states[level], "tp", level - local)
        (state,) = call(
            functools.partial(across_kernel, slots, width),
            steps,
            [states[level], partners[level], w_self, w_cross],
            [row_state, row_state, level_of(w_self, level), level_of(w_cross, level)],
            [state_shape],
            [row_state],
            2 * unit,
        )
        states.append(state)
    last = levels - 1
    partners[last] = partner_2(states[last], "tp", last - local)
    down_part, grad, send = call(
        functools.partial(top_kernel, slots, width),
        steps,
        [block_pairs, states[last], partners[last], w_self, w_cross, w_down, cotangent_all],
        [
            smem,
            row_state,
            row_state,
            level_of(w_self, last),
            level_of(w_cross, last),
            whole(w_down),
            row_model,
        ],
        [model_shape, state_shape, state_shape],
        [row_model, row_state, row_state],
        7 * unit,
        [pltpu.VMEM((tile, model_width), F32)],
    )
    terms = [None] * levels

    def across_terms(level, gradient):
        (result,) = call(
            functools.partial(across_grad_kernel, slots, width),
            1,
            [states[level], partners[level], gradient],
            [whole(states[level]), whole(states[level]), whole(gradient)],
            [terms_shape],
            [whole(terms_shape)],
            2 * unit,
        )
        return lax.psum_scatter(result, "seq", scatter_dimension=2, tiled=True)

    for level in range(last, local, -1):
        incoming = partner_2(send, "tp", level - local)
        terms[level] = across_terms(level, grad)
        grad, send = call(
            functools.partial(middle_kernel, slots, width),
            steps,
            [grad, incoming, w_self, w_cross],
            [row_state, row_state, level_of(w_self, level), level_of(w_cross, level - 1)],
            [state_shape, state_shape],
            [row_state, row_state],
            2 * unit,
        )
    incoming = partner_2(send, "tp", 0)
    terms[local] = across_terms(local, grad)
    *grads, spread = call(
        functools.partial(down_kernel, local, slots, width),
        steps,
        [block_pairs, grad, incoming, w_self, w_up, *local_self, *local_cross],
        [
            smem,
            row_state,
            row_state,
            level_of(w_self, local),
            whole(w_up),
            *local_specs,
            *local_specs,
        ],
        [state_shape] * (local + 1) + [model_shape],
        [row_state] * (local + 1) + [row_model],
        (2 * local + 3) * unit,
        [pltpu.VMEM((tile, model_width), F32)],
    )
    spread_part = lax.psum_scatter(spread, "tp", scatter_dimension=1, tiled=True)
    grad_hidden = (cotangent.astype(F32) + spread_part.astype(F32)).astype(BF)
    for level in reversed(range(local)):
        (result,) = call(
            functools.partial(pair_grad_kernel, level, slots, width),
            1,
            [states[level], grads[level + 1]],
            [whole(states[level]), whole(states[level])],
            [terms_shape],
            [whole(terms_shape)],
            2 * unit,
        )
        terms[level] = lax.psum_scatter(result, "seq", scatter_dimension=2, tiled=True)

    down_sum = lax.psum_scatter(down_part, "tp", scatter_dimension=1, tiled=True)
    layer_out = (hidden_in.astype(F32) + down_sum.astype(F32)).astype(BF)

    grad_rows = lax.all_to_all(grad_hidden, "seq", split_axis=0, concat_axis=0, tiled=True)
    moved_back = dot_tn(mixer, grad_rows).astype(BF)
    returned = lax.all_to_all(moved_back, "seq", split_axis=0, concat_axis=0, tiled=True)
    cross_rows = dot_nt(grad_rows, first_rows).reshape(groups, positions, groups, positions)
    second_part = jnp.sum(cross_rows * same.astype(F32)[None, :, None, :], axis=3).transpose(1, 0, 2)
    first_part = dot_nt(returned, tokens).astype(BF)
    second_sum, first_sum = lax.psum((second_part, first_part), "tp")
    grad_mix = dot_tn(first_factor, returned)
    grad_tokens = (grad_hidden.astype(F32) + grad_mix).astype(BF)
    level_terms = jnp.stack(terms, axis=1).astype(F32) * token_scale
    return (
        layer_out,
        grad_tokens,
        (first_sum.astype(F32) * model_width_scale)[None],
        second_sum * model_width_scale,
        level_terms[0],
        level_terms[1],
    )


def solution(mesh):
    in_specs = (
        P("seq", "tp"),
        P("seq", None, None),
        P("seq", None, None),
        P("tp", None, None, None),
        P(None, "tp", None, None),
        P(None, "tp", None, None),
        P("tp", None, None, None),
        P("tp", None),
        P("seq", "tp"),
    )
    out_specs = (
        P("seq", "tp"),
        P("seq", "tp"),
        P("seq", None, None),
        P("seq", None, None),
        P(None, "tp", "seq", None),
        P(None, "tp", "seq", None),
    )
    return jax.shard_map(
        per_device, mesh=mesh, in_specs=in_specs, out_specs=out_specs, check_vma=False
    )
```

time: 737 us -> 799 us (1.084)
  waiting for transfers between devices: 418 us -> 567 us
  Pallas kernels: 0 us -> 140 us
  matrix products: 140 us -> 8.29 us
  local copies, waits for them, and re-layouts: 76.7 us -> 14.7 us
  other arithmetic: 29.5 us -> 8.5 us
    pallas_call x0 -> x11, Pallas kernels: none -> 140 us  [call(): pl.pallas_call(kernel, grid=(steps,), in_specs=in_specs, out_specs=out_sp...]
    dot_general x48 -> x6, matrix products: 140 us -> 8.29 us  [dot(): lax.dot_general(left, right, (contract, ((), ())), preferred_element_type...]
    reduce_scatter x3 -> x7, waiting for transfers between devices: 229 us -> 349 us  [the longest x4 218 us: per_device(): lax.psum_scatter(result, 'seq', scatter_dimension=2, tiled=True)]
    psum x1, waiting for transfers between devices: 0.01 us -> 31.9 us  [per_device(): second_sum, first_sum = lax.psum((second_part, first_part), 'tp')]
    rev x8 -> x0, local copies, waits for them, and re-layouts: 24.5 us -> none  [swap_local(): return jnp.flip(folded, axis=2).reshape(shape)]
    all_gather x2, waiting for transfers between devices: 15.4 us -> 33.7 us  [the longest x1 21.1 us: per_device(): hidden_all = lax.all_gather(hidden_in, 'tp', axis=1, tiled=True)]
    all_to_all x3, waiting for transfers between devices: 31 us -> 12.9 us  [the longest x1 12.9 us: per_device(): lax.all_to_all(first_out, 'seq', split_axis=0, concat_axis=0, tiled=True)]
    reshape x5 -> x0, local copies, waits for them, and re-layouts: 15 us -> none  [the longest x1 5.29 us: per_device(): spread = jnp.einsum('rjkc,jki->ric', back_pieces, chosen, precision=lax.P...]
  transfers between devices with their start and end apart: 18 -> 18, of which waited for: 12 -> 15; matrix products, arithmetic and copies ran while one was open for 14% -> 2% of each run, Pallas kernels for 0% -> 12%
where the time goes in v1:
time: 799 us; the launch traced here: 798 us
  waiting for transfers between devices  567 us (71%)
  Pallas kernels  140 us (18%)
  blocking collectives  29 us (4%)
  starting transfers between devices  17.4 us (2%)
  local copies, waits for them, and re-layouts  14.7 us (2%)
  between operations  14.1 us (2%)
  other arithmetic  8.5 us (1%)
  matrix products  8.29 us (1%)
    reduce_scatter x4, waiting for transfers between devices, per_device(): lax.psum_scatter(result, 'seq', scatter_dimension=2, tiled=True)  218 us
    pallas_call x11, Pallas kernels, call(): pl.pallas_call(kernel, grid=(steps,), in_specs=in_specs, out_specs=out_sp...  140 us
    reduce_scatter x2, waiting for transfers between devices, across_terms(): return lax.psum_scatter(result, 'seq', scatter_dimension=2, tiled=True)  131 us
    ppermute x4, waiting for transfers between devices, partner_2(): return lax.ppermute(value, axis, pairs)  106 us
    reduce_scatter x1, waiting for transfers between devices, per_device(): lax.psum_scatter(spread, 'tp', scatter_dimension=1, tiled=True)  32.1 us
    psum x1, waiting for transfers between devices, per_device(): second_sum, first_sum = lax.psum((second_part, first_part), 'tp')  31.9 us
    all_gather x1, waiting for transfers between devices, per_device(): hidden_all = lax.all_gather(hidden_in, 'tp', axis=1, tiled=True)  21.1 us
    all_to_all x1, blocking collectives, per_device(): lax.all_to_all(mixed_part, 'seq', split_axis=0, concat_axis=0, tiled=True)  18.1 us
  transfers between devices with their start and end apart: 18, of which 15 were waited for; matrix products, arithmetic and copies ran while one was open for 2% of the time, Pallas kernels for 12%

profile of v1, /device:TPU:0, one launch (start us, length us, event | category | flops | bytes accessed | tf_op | source)
XLA Modules:
  0.0 798.3 jit_solution(11922482768996607868)
XLA Ops:
  7.2 1.0 copy-done
  8.2 2.3 convolution_convert_fusion.3
  10.5 7.3 all-to-all-start
  17.8 0.1 copy.16
  17.9 0.1 copy.15
  18.0 0.6 broadcast_multiply_fusion
  18.7 0.6 mul.56
  19.3 12.9 %all-to-all-done = bf16[8,64,512]{2,1,0:T(8,128)(2,1)S(1)} async-done(((bf16[8,64,512]{2,1,0:T(8,128)(2,1)}), bf16[8,64,512]{2,1,0:T(8,128)(2,1)S(1)}, u32[]{:S(2)}, u32[]{:S(2)}) %all-to-all-start) | async-done | bytes 524320 | tf_op jit(solution)/shard_map/all_to_all | solution.py:238
  32.2 0.4 convolution_convert_fusion.2
  32.7 18.1 %all_to_all.45 = bf16[8,64,512]{2,1,0:T(8,128)(2,1)S(1)} all-to-all(bf16[8,64,512]{2,1,0:T(8,128)(2,1)S(1)} %bitcast.62), channel_id=1, replica_groups=mesh['seq'=8,'tp'=4] {'seq'}, dimensions={0} | all-to-all | bytes 1048576 | tf_op jit(solution)/shard_map/all_to_all | solution.py:240
  50.8 1.0 fusion.2
  51.8 0.7 copy.18.pairs
  52.5 21.1 %all-gather.3.cloned.1.call-done.hidden = bf16[512,2048]{1,0:T(8,128)(2,1)} async-done(((bf16[512,512]{1,0:T(8,128)(2,1)}), bf16[512,2048]{1,0:T(8,128)(2,1)}) %all-gather.3.cloned.1.call-update) | async-done | bytes 2097168 | tf_op jit(solution)/shard_map/all_gather | solution.py:242
  73.6 24.0 %shard_map.136 = (bf16[512,2048]{1,0:T(8,128)(2,1)}, bf16[512,2048]{1,0:T(8,128)(2,1)}, bf16[512,2048]{1,0:T(8,128)(2,1)}, bf16[512,2048]{1,0:T(8,128)(2,1)}, bf16[512,2048]{1,0:T(8,128)(2,1)}) custom-call(s32[16,2]{1,0:T(8,128)} %copy.18.pairs, bf16[512,2048]{1,0:T(8,128)(2,1)} %all-gather.3.cloned.1.call-done.hidden, bf16[16,2,128,128]{3,2,1,0:T(8,128)(2,1)} %w_up.3, ...), custom_call_target="tpu_custom_call" | custom-call | flops 2684354560 | bytes 16777344 | tf_op jit(solution)/shard_map/pallas_call | solution.py:195
  97.6 0.2 collective-permute-start
  97.9 4.1 collective-permute-done.partner
  102.0 1.3 copy-done.1
  103.3 8.7 %shard_map.137.state = bf16[512,2048]{1,0:T(8,128)(2,1)} custom-call(bf16[512,2048]{1,0:T(8,128)(2,1)} %get-tuple-element.21.state, bf16[512,2048]{1,0:T(8,128)(2,1)} %copy-done.1, bf16[6,16,128,128]{3,2,1,0:T(8,128)(2,1)} %refs_3_.3, bf16[6,16,128,128]{3,2,1,0:T(8,128)(2,1)} %refs_7_.3), custom_call_target="tpu_custom_call" | custom-call | flops 536870912 | bytes 12582912 | tf_op jit(solution)/shard_map/pallas_call | solution.py:195
  112.0 0.1 collective-permute-start.1
  112.1 12.6 %all-gather.5.cloned.1.call-done.cotangent = bf16[512,2048]{1,0:T(8,128)(2,1)} async-done(((bf16[512,512]{1,0:T(8,128)(2,1)}), bf16[512,2048]{1,0:T(8,128)(2,1)}) %all-gather.5.cloned.1.call-update) | async-done | bytes 2097168 | tf_op jit(solution)/shard_map/all_gather | solution.py:229
  124.7 39.4 %collective-permute-done.1.partner = bf16[512,2048]{1,0:T(8,128)(2,1)S(1)} collective-permute-done((bf16[512,2048]{1,0:T(8,128)(2,1)}, bf16[512,2048]{1,0:T(8,128)(2,1)S(1)}, u32[]{:S(2)}, u32[]{:S(2)}) %collective-permute-start.1) | collective-permute-done | bytes 2097184 | tf_op jit(solution)/shard_map/ppermute | solution.py:35
  164.1 1.3 copy-done.2
  165.4 17.8 %shard_map.138 = (bf16[512,2048]{1,0:T(8,128)(2,1)}, bf16[512,2048]{1,0:T(8,128)(2,1)}, bf16[512,2048]{1,0:T(8,128)(2,1)}) custom-call(s32[16,2]{1,0:T(8,128)} %copy.18.pairs, bf16[512,2048]{1,0:T(8,128)(2,1)} %shard_map.137.state, bf16[512,2048]{1,0:T(8,128)(2,1)} %copy-done.2, bf16[6,16,128,128]{3,2,1,0:T(8,128)(2,1)} %refs_3_.3, ...), custom_call_target="tpu_custom_call" | custom-call | flops 1879048192 | bytes 13631616 | tf_op jit(solution)/shard_map/pallas_call | solution.py:195
  183.1 0.3 collective-permute-start.2
  183.5 58.5 %collective-permute-done.2.incoming = bf16[512,2048]{1,0:T(8,128)(2,1)S(1)} collective-permute-done((bf16[512,2048]{1,0:T(8,128)(2,1)}, bf16[512,2048]{1,0:T(8,128)(2,1)S(1)}, u32[]{:S(2)}, u32[]{:S(2)}) %collective-permute-start.2) | collective-permute-done | bytes 2097184 | tf_op jit(solution)/shard_map/ppermute | solution.py:35
  242.0 1.3 copy-done.5
  243.3 13.0 %shard_map.139 = (bf16[512,2048]{1,0:T(8,128)(2,1)}, bf16[512,2048]{1,0:T(8,128)(2,1)}) custom-call(bf16[512,2048]{1,0:T(8,128)(2,1)} %get-tuple-element.23.grad, bf16[512,2048]{1,0:T(8,128)(2,1)} %copy-done.5, bf16[6,16,128,128]{3,2,1,0:T(8,128)(2,1)} %refs_3_.3, bf16[6,16,128,128]{3,2,1,0:T(8,128)(2,1)} %refs_7_.3), custom_call_target="tpu_custom_call" | custom-call | flops 536870912 | bytes 14680064 | tf_op jit(solution)/shard_map/pallas_call | solution.py:195
  256.3 4.4 collective-permute-done.3.incoming
  260.7 1.3 copy-done.6
  261.9 34.0 %shard_map.140 = (bf16[512,2048]{1,0:T(8,128)(2,1)}, bf16[512,2048]{1,0:T(8,128)(2,1)}, bf16[512,2048]{1,0:T(8,128)(2,1)}, bf16[512,2048]{1,0:T(8,128)(2,1)}, bf...) custom-call(s32[16,2]{1,0:T(8,128)} %copy.18.pairs, bf16[512,2048]{1,0:T(8,128)(2,1)} %get-tuple-element.25.grad, ...), custom_call_target="tpu_custom_call" | custom-call | flops 2952790016 | bytes 19923072 | tf_op jit(solution)/shard_map/pallas_call | solution.py:195
  296.0 6.0 shard_map.141
  302.0 6.0 shard_map.142
  308.1 0.5 reduce-scatter.11.cloned.1.call-update
  308.7 6.2 shard_map.143
  314.9 6.1 shard_map.144
  321.1 9.0 %shard_map.145 = bf16[2,16,128,128]{3,2,1,0:T(8,128)(2,1)} custom-call(bf16[512,2048]{1,0:T(8,128)(2,1)} %get-tuple-element.21.state, bf16[512,2048]{1,0:T(8,128)(2,1)} %copy-done.1, bf16[512,2048]{1,0:T(8,128)(2,1)} %get-tuple-element.25.grad), custom_call_target="tpu_custom_call" | custom-call | flops 536870912 | bytes 7340032 | tf_op jit(solution)/shard_map/pallas_call | solution.py:195
  330.1 8.9 %shard_map.146 = bf16[2,16,128,128]{3,2,1,0:T(8,128)(2,1)} custom-call(bf16[512,2048]{1,0:T(8,128)(2,1)} %shard_map.137.state, bf16[512,2048]{1,0:T(8,128)(2,1)} %copy-done.2, bf16[512,2048]{1,0:T(8,128)(2,1)} %get-tuple-element.23.grad), custom_call_target="tpu_custom_call" | custom-call | flops 536870912 | bytes 7340032 | tf_op jit(solution)/shard_map/pallas_call | solution.py:195
  339.1 2.0 add_convert_fusion.1
  341.2 24.9 %reduce-scatter.13.cloned.1.call-done = bf16[2,16,16,128]{3,2,1,0:T(8,128)(2,1)} async-done(((bf16[2,16,128,128]{3,2,1,0:T(8,128)(2,1)}), bf16[2,16,16,128]{3,2,1,0:T(8,128)(2,1)}) %reduce-scatter.13.cloned.1.call-update) | async-done | bytes 131088 | tf_op jit(solution)/shard_map/reduce_scatter | solution.py:348
  366.1 0.9 bitcast_dynamic-update-slice_fusion.5
  367.0 65.3 %reduce-scatter.15.cloned.1.call-done = bf16[2,16,16,128]{3,2,1,0:T(8,128)(2,1)} async-done(((bf16[2,16,128,128]{3,2,1,0:T(8,128)(2,1)}), bf16[2,16,16,128]{3,2,1,0:T(8,128)(2,1)}) %reduce-scatter.15.cloned.1.call-update) | async-done | bytes 131088 | tf_op jit(solution)/shard_map/reduce_scatter | solution.py:348
  432.2 0.9 bitcast_dynamic-update-slice_fusion.4
  433.2 32.1 %reduce-scatter.11.cloned.1.call-done = bf16[512,512]{1,0:T(8,128)(2,1)} async-done(((bf16[512,2048]{1,0:T(8,128)(2,1)}), bf16[512,512]{1,0:T(8,128)(2,1)}) %reduce-scatter.11.cloned.1.call-update) | async-done | bytes 524304 | tf_op jit(solution)/shard_map/reduce_scatter | solution.py:336
  465.3 2.0 add_convert_fusion
  467.2 5.5 all-to-all-start.2
  472.8 62.0 %reduce-scatter.17.cloned.1.call-done = bf16[2,16,16,128]{3,2,1,0:T(8,128)(2,1)} async-done(((bf16[2,16,128,128]{3,2,1,0:T(8,128)(2,1)}), bf16[2,16,16,128]{3,2,1,0:T(8,128)(2,1)}) %reduce-scatter.17.cloned.1.call-update) | async-done | bytes 131088 | tf_op jit(solution)/shard_map/reduce_scatter | solution.py:348
  534.8 0.9 bitcast_dynamic-update-slice_fusion.3
  535.7 65.8 %reduce-scatter.19.cloned.1.call-done = bf16[2,16,16,128]{3,2,1,0:T(8,128)(2,1)} async-done(((bf16[2,16,128,128]{3,2,1,0:T(8,128)(2,1)}), bf16[2,16,16,128]{3,2,1,0:T(8,128)(2,1)}) %reduce-scatter.19.cloned.1.call-update) | async-done | bytes 131088 | tf_op jit(solution)/shard_map/reduce_scatter | solution.py:348
  601.5 0.9 bitcast_dynamic-update-slice_fusion.2
  602.4 65.4 %reduce-scatter.21.cloned.1.call-done = bf16[2,16,16,128]{3,2,1,0:T(8,128)(2,1)} async-done(((bf16[2,16,128,128]{3,2,1,0:T(8,128)(2,1)}), bf16[2,16,16,128]{3,2,1,0:T(8,128)(2,1)}) %reduce-scatter.21.cloned.1.call-update) | async-done | bytes 131088 | tf_op jit(solution)/shard_map/reduce_scatter | solution.py:302
  667.8 0.9 bitcast_dynamic-update-slice_fusion.1
  668.8 65.7 %reduce-scatter.23.cloned.1.call-done = bf16[2,16,16,128]{3,2,1,0:T(8,128)(2,1)} async-done(((bf16[2,16,128,128]{3,2,1,0:T(8,128)(2,1)}), bf16[2,16,16,128]{3,2,1,0:T(8,128)(2,1)}) %reduce-scatter.23.cloned.1.call-update) | async-done | bytes 131088 | tf_op jit(solution)/shard_map/reduce_scatter | solution.py:302
  734.5 0.9 bitcast_dynamic-update-slice_fusion
  735.4 1.3 convolution_convert_fusion.1
  736.7 3.6 all-to-all-start.3
  740.3 0.1 convert_multiply_fusion
  740.5 1.3 slice_bitcast_fusion
  741.8 0.7 multiply_reduce_fusion
  742.6 10.9 %psum.15 = f32[64,8,8]{0,2,1:T(8,128)S(1)} all-reduce(f32[64,8,8]{0,2,1:T(8,128)S(1)} %bitcast.64), channel_id=1, replica_groups=mesh['seq'=8,'tp'=4] {'tp'}, use_global_device_ids=true, to_apply=%region_4.0 | all-reduce | flops 4096 | bytes 32768 | tf_op jit(solution)/shard_map/psum | solution.py:359
  753.4 0.6 broadcast_multiply_fusion.1
  754.1 1.3 convolution_convert_fusion
  755.4 2.3 fusion.1
  757.7 31.9 %all-reduce.2.cloned.1.call-done = bf16[512,512]{1,0:T(8,128)(2,1)} async-done(((bf16[512,512]{1,0:T(8,128)(2,1)}), bf16[512,512]{1,0:T(8,128)(2,1)}) %all-reduce.2.cloned.1.call-update) | async-done | bytes 524304 | tf_op jit(solution)/shard_map/psum | solution.py:359
  789.6 2.2 multiply_bitcast_fusion
  (50 shorter events, 0.7 us)
Async XLA Ops:
  7.2 1.0 copy-start
  7.2 10.7 %copy-start.12 = (bf16[64,8,8]{0,2,1:T(8,128)(2,1)S(1)}, bf16[64,8,8]{0,2,1:T(8,128)(2,1)}, u32[]{:S(2)}) copy-start(bf16[64,8,8]{0,2,1:T(8,128)(2,1)} %param.11) | copy-start | bytes 24580
  10.5 21.7 %all-to-all-start = ((bf16[8,64,512]{2,1,0:T(8,128)(2,1)}), bf16[8,64,512]{2,1,0:T(8,128)(2,1)S(1)}, u32[]{:S(2)}, u32[]{:S(2)}) async-start(bf16[8,64,512]{2,1,0:T(8,128)(2,1)} %bitcast.2), calls=%async_computation | async-start | bytes 1048576 | tf_op jit(solution)/shard_map/all_to_all | solution.py:238
  17.7 55.9 %all-gather.3.cloned.1.call-start = ((), (), s32[]{:S(2)}) async-start(), calls=%async_computation.12 | async-start | bytes 2621440 | tf_op jit(solution)/shard_map/all_gather | solution.py:242
  18.6 32.1 %copy-start.3 = (bf16[512,512]{1,0:T(8,128)(2,1)S(1)}, bf16[512,512]{1,0:T(8,128)(2,1)}, u32[]{:S(2)}) copy-start(bf16[512,512]{1,0:T(8,128)(2,1)} %param.9) | copy-start | bytes 1572868
  19.3 32.5 %copy-start.7 = (bf16[512,512]{1,0:T(8,128)(2,1)}, bf16[512,512]{1,0:T(8,128)(2,1)S(1)}, u32[]{:S(2)}) copy-start(bf16[512,512]{1,0:T(8,128)(2,1)S(1)} %mul.56) | copy-start | bytes 1572868
  32.2 19.5 %copy-start.10 = (bf16[8,64,512]{2,1,0:T(8,128)(2,1)}, bf16[8,64,512]{2,1,0:T(8,128)(2,1)S(1)}, u32[]{:S(2)}) copy-start(bf16[8,64,512]{2,1,0:T(8,128)(2,1)S(1)} %all-to-all-done) | copy-start | bytes 1572868
  32.2 19.6 %copy-start.13 = (s32[16,2]{0,1:T(2,128)S(1)}, s32[16,2]{0,1:T(2,128)}, u32[]{:S(2)}) copy-start(s32[16,2]{0,1:T(2,128)} %param.16) | copy-start | bytes 388
  51.8 72.9 %all-gather.5.cloned.1.call-start = ((), (), s32[]{:S(2)}) async-start(), calls=%async_computation.13 | async-start | bytes 2621440 | tf_op jit(solution)/shard_map/all_gather | solution.py:229
  97.6 4.4 collective-permute-start
  97.8 241.3 %reduce-scatter.9.cloned.1.call-start = ((), (), s32[]{:S(2)}) async-start(), calls=%async_computation.14 | async-start | bytes 2621440 | tf_op jit(solution)/shard_map/reduce_scatter | solution.py:350
  102.0 1.3 copy-start.1
  112.0 52.1 %collective-permute-start.1 = (bf16[512,2048]{1,0:T(8,128)(2,1)}, bf16[512,2048]{1,0:T(8,128)(2,1)S(1)}, u32[]{:S(2)}, u32[]{:S(2)}) collective-permute-start(bf16[512,2048]{1,0:T(8,128)(2,1)} %shard_map.137.state), channel_id=1, source_target_pairs={{0,2},{1,3},{2,0},{3,1},{4,6},{5,7},{6,4},{7,5},{8,10},{9,11},{10,... | collective-permute-start | bytes 6291464 | tf_op jit(solution)/shard_map/ppermute | solution.py:35
  164.1 1.3 copy-start.2
  183.1 58.8 %collective-permute-start.2 = (bf16[512,2048]{1,0:T(8,128)(2,1)}, bf16[512,2048]{1,0:T(8,128)(2,1)S(1)}, u32[]{:S(2)}, u32[]{:S(2)}) collective-permute-start(bf16[512,2048]{1,0:T(8,128)(2,1)} %get-tuple-element.24), channel_id=1, source_target_pairs={{0,2},{1,3},{2,0},{3,1},{4,6},{5,7},{6,4},{7,5},{8,10},{9,11},{10,... | collective-permute-start | bytes 6291464 | tf_op jit(solution)/shard_map/ppermute | solution.py:35
  183.4 182.6 %reduce-scatter.13.cloned.1.call-start = ((), (), s32[]{:S(2)}) async-start(), calls=%async_computation.17 | async-start | bytes 1179648 | tf_op jit(solution)/shard_map/reduce_scatter | solution.py:348
  242.0 1.3 copy-start.5
  256.3 4.4 collective-permute-start.3
  260.7 1.3 copy-start.6
  302.0 130.3 %reduce-scatter.15.cloned.1.call-start = ((), (), s32[]{:S(2)}) async-start(), calls=%async_computation.18 | async-start | bytes 1179648 | tf_op jit(solution)/shard_map/reduce_scatter | solution.py:348
  308.1 157.2 %reduce-scatter.11.cloned.1.call-start = ((), (), s32[]{:S(2)}) async-start(), calls=%async_computation.15 | async-start | bytes 2621440 | tf_op jit(solution)/shard_map/reduce_scatter | solution.py:336
  308.6 226.2 %reduce-scatter.17.cloned.1.call-start = ((), (), s32[]{:S(2)}) async-start(), calls=%async_computation.19 | async-start | bytes 1179648 | tf_op jit(solution)/shard_map/reduce_scatter | solution.py:348
  314.9 286.6 %reduce-scatter.19.cloned.1.call-start = ((), (), s32[]{:S(2)}) async-start(), calls=%async_computation.20 | async-start | bytes 1179648 | tf_op jit(solution)/shard_map/reduce_scatter | solution.py:348
  321.0 346.8 %reduce-scatter.21.cloned.1.call-start = ((), (), s32[]{:S(2)}) async-start(), calls=%async_computation.21 | async-start | bytes 1179648 | tf_op jit(solution)/shard_map/reduce_scatter | solution.py:302
  330.1 9.1 %copy-start.4 = (bf16[512,512]{1,0:T(8,128)(2,1)S(1)}, bf16[512,512]{1,0:T(8,128)(2,1)}, u32[]{:S(2)}) copy-start(bf16[512,512]{1,0:T(8,128)(2,1)} %fusion.2) | copy-start | bytes 1572868
  330.1 404.4 %reduce-scatter.23.cloned.1.call-start = ((), (), s32[]{:S(2)}) async-start(), calls=%async_computation.22 | async-start | bytes 1179648 | tf_op jit(solution)/shard_map/reduce_scatter | solution.py:302
  339.1 126.2 %copy-start.9 = (bf16[512,512]{1,0:T(8,128)(2,1)S(1)}, bf16[512,512]{1,0:T(8,128)(2,1)}, u32[]{:S(2)}) copy-start(bf16[512,512]{1,0:T(8,128)(2,1)} %param.17) | copy-start | bytes 1572868
  341.2 394.3 %copy-start.8 = (bf16[512,512]{1,0:T(8,128)(2,1)S(1)}, bf16[512,512]{1,0:T(8,128)(2,1)}, u32[]{:S(2)}) copy-start(bf16[512,512]{1,0:T(8,128)(2,1)} %copy-done.7) | copy-start | bytes 1572868
  467.2 268.2 %all-to-all-start.2 = ((bf16[8,64,512]{2,1,0:T(8,128)(2,1)}), bf16[8,64,512]{2,1,0:T(8,128)(2,1)S(1)}, u32[]{:S(2)}, u32[]{:S(2)}) async-start(bf16[8,64,512]{2,1,0:T(8,128)(2,1)} %bitcast.6), calls=%async_computation.4 | async-start | bytes 1048576 | tf_op jit(solution)/shard_map/all_to_all | solution.py:353
  736.7 17.4 %all-to-all-start.3 = ((bf16[8,64,512]{2,1,0:T(8,128)(2,1)}), bf16[8,64,512]{2,1,0:T(8,128)(2,1)S(1)}, u32[]{:S(2)}, u32[]{:S(2)}) async-start(bf16[8,64,512]{2,1,0:T(8,128)(2,1)} %bitcast.8), calls=%async_computation.5 | async-start | bytes 1048576 | tf_op jit(solution)/shard_map/all_to_all | solution.py:355
  740.3 49.3 %all-reduce.2.cloned.1.call-start = ((), (), s32[]{:S(2)}) async-start(), calls=%async_computation.16 | async-start | bytes 1048576 | tf_op jit(solution)/shard_map/psum | solution.py:359
  740.5 1.3 copy-start.11
Sparse Core Ops, SparseCore 0:
  51.9 21.6 all-gather.2
  98.0 26.6 all-gather.4
  183.6 43.9 reduce-scatter.8
  302.1 63.9 reduce-scatter.12
  369.3 62.8 reduce-scatter.14
  434.8 30.4 reduce-scatter.10
  468.7 66.0 reduce-scatter.16
  538.6 62.8 reduce-scatter.18
  604.9 62.8 reduce-scatter.20
  671.5 62.9 reduce-scatter.22
  755.5 34.0 all-reduce.1

commit v2 on v1

--- a/solution.py
+++ b/solution.py
@@ -11,6 +11,7 @@
 BF = jnp.bfloat16
 F32 = jnp.float32
 VMEM_BYTES = 56 * 1024 * 1024
+UNROLL = 4
 
 
 def dot(left, right, contract):
@@ -35,6 +36,47 @@
     return lax.ppermute(value, axis, pairs)
 
 
+def bit_of(axis, bit):
+    return (lax.axis_index(axis) // 2**bit) % 2
+
+
+def bits_of(axis):
+    return lax.axis_size(axis).bit_length() - 1
+
+
+def halved_sum(value, axis, dim):
+    for bit in range(bits_of(axis)):
+        shape = value.shape
+        folded = value.reshape(shape[:dim] + (shape[dim] // 2, 2) + shape[dim + 1 :])
+        mine = bit_of(axis, bit)
+        keep = lax.dynamic_index_in_dim(folded, mine, dim + 1, keepdims=False)
+        give = lax.dynamic_index_in_dim(folded, 1 - mine, dim + 1, keepdims=False)
+        total = keep.astype(F32) + partner_2(give, axis, bit).astype(F32)
+        value = total.astype(BF)
+    return lax.squeeze(total, (dim,))
+
+
+def doubled_gather(value, axis):
+    shape = value.shape
+    count = 0
+    for bit in reversed(range(bits_of(axis))):
+        other = partner_2(value, axis, bit)
+        low = bit_of(axis, bit) == 0
+        value = jnp.stack(
+            [jnp.where(low, value, other), jnp.where(low, other, value)], axis=count
+        )
+        count += 1
+    return value.reshape((lax.axis_size(axis),) + shape)
+
+
+def exchanged_sum(value, axis):
+    kind = value.dtype
+    for bit in range(bits_of(axis)):
+        total = value.astype(F32) + partner_2(value, axis, bit).astype(F32)
+        value = total.astype(kind)
+    return total
+
+
 def lanes(index, width):
     return pl.ds(pl.multiple_of(index * width, width), width)
 
@@ -55,18 +97,31 @@
     return jnp.concatenate([ref[:, lanes(first, width)], ref[:, lanes(second, width)]], axis=1)
 
 
+def blocks_of(ref, first, second, width):
+    per = ref.shape[2] // width
+    return jnp.concatenate(
+        [ref[i // per, :, lanes(lax.rem(i, per), width)] for i in (first, second)], axis=1
+    )
+
+
+def put_chunks(out, total):
+    count, _, size = out.shape
+    for chunk in range(count):
+        out[chunk] = total[:, chunk * size : (chunk + 1) * size].astype(BF)
+
+
 def up_kernel(levels, slots, width, pairs, hidden, w_up, *refs):
     w_self, w_cross, states = refs[:levels], refs[levels : 2 * levels], refs[2 * levels :]
 
-    @pl.loop(0, slots)
-    def _(j):
-        both = side_by_side(hidden, pairs[j, 0], pairs[j, 1], width)
+    @pl.loop(0, slots, unroll=UNROLL)
+    def _(j):
+        both = blocks_of(hidden, pairs[j, 0], pairs[j, 1], width)
         matrix = jnp.concatenate([w_up[j, 0], w_up[j, 1]], axis=0)
         states[0][:, lanes(j, width)] = dot_nn(both, matrix).astype(BF)
 
     for level in range(levels):
 
-        @pl.loop(0, slots // 2)
+        @pl.loop(0, slots // 2, unroll=UNROLL)
         def _(index):
             first, second = pair_of(index, level)
             both = side_by_side(states[level], first, second, width)
@@ -76,7 +131,7 @@
 
 
 def across_kernel(slots, width, state, partner, w_self, w_cross, out):
-    @pl.loop(0, slots)
+    @pl.loop(0, slots, unroll=UNROLL)
     def _(j):
         both = jnp.concatenate([state[:, lanes(j, width)], partner[:, lanes(j, width)]], axis=1)
         matrix = jnp.concatenate([w_self[0, j], w_cross[0, j]], axis=0)
@@ -88,7 +143,7 @@
 ):
     total[...] = jnp.zeros_like(total)
 
-    @pl.loop(0, slots)
+    @pl.loop(0, slots, unroll=UNROLL)
     def _(j):
         first, second = pairs[j, 0], pairs[j, 1]
         both = jnp.concatenate([state[:, lanes(j, width)], partner[:, lanes(j, width)]], axis=1)
@@ -105,25 +160,25 @@
         pieces = dot_nn(active, w_both)
         total[:, lanes(first, width)] += pieces[:, :width]
         total[:, lanes(second, width)] += pieces[:, width:]
-        grad_act = dot_nt(side_by_side(cotangent, first, second, width), w_both)
+        grad_act = dot_nt(blocks_of(cotangent, first, second, width), w_both)
         grad_top = (grad_act * slope).astype(BF)
         grad[:, lanes(j, width)] = grad_top
         send[:, lanes(j, width)] = dot_nt(grad_top, w_cross[0, j]).astype(BF)
 
-    down[...] = total[...].astype(BF)
+    put_chunks(down, total)
 
 
 def across_grad_kernel(slots, width, state, partner, grad, terms):
-    @pl.loop(0, slots)
+    @pl.loop(0, slots, unroll=UNROLL)
     def _(j):
         both = jnp.concatenate([state[:, lanes(j, width)], partner[:, lanes(j, width)]], axis=1)
         result = dot_tn(both, grad[:, lanes(j, width)]).astype(BF)
-        terms[0, j] = result[:width]
-        terms[1, j] = result[width:]
+        terms[0, 0, j] = result[:width]
+        terms[0, 1, j] = result[width:]
 
 
 def middle_kernel(slots, width, grad, incoming, w_self, w_cross_below, out, send):
-    @pl.loop(0, slots)
+    @pl.loop(0, slots, unroll=UNROLL)
     def _(j):
         own = dot_nt(grad[:, lanes(j, width)], w_self[0, j])
         result = (own + incoming[:, lanes(j, width)].astype(F32)).astype(BF)
@@ -136,7 +191,7 @@
     grads = refs[2 * levels : 3 * levels + 1]
     spread, total = refs[3 * levels + 1 :]
 
-    @pl.loop(0, slots)
+    @pl.loop(0, slots, unroll=UNROLL)
     def _(j):
         own = dot_nt(grad[:, lanes(j, width)], w_self_above[0, j])
         result = own + incoming[:, lanes(j, width)].astype(F32)
@@ -144,7 +199,7 @@
 
     for level in reversed(range(levels)):
 
-        @pl.loop(0, slots // 2)
+        @pl.loop(0, slots // 2, unroll=UNROLL)
         def _(index):
             first, second = pair_of(index, level)
             both = side_by_side(grads[level + 1], first, second, width)
@@ -154,27 +209,32 @@
 
     total[...] = jnp.zeros_like(total)
 
-    @pl.loop(0, slots)
+    @pl.loop(0, slots, unroll=UNROLL)
     def _(j):
         matrix = jnp.concatenate([w_up[j, 0], w_up[j, 1]], axis=0)
         pieces = dot_nt(grads[0][:, lanes(j, width)], matrix)
         total[:, lanes(pairs[j, 0], width)] += pieces[:, :width]
         total[:, lanes(pairs[j, 1], width)] += pieces[:, width:]
 
-    spread[...] = total[...].astype(BF)
-
-
-def pair_grad_kernel(level, slots, width, state, grad, terms):
-    @pl.loop(0, slots // 2)
-    def _(index):
-        first, second = pair_of(index, level)
-        result = dot_tn(
-            side_by_side(state, first, second, width), side_by_side(grad, first, second, width)
-        ).astype(BF)
-        terms[0, first] = result[:width, :width]
-        terms[1, second] = result[:width, width:]
-        terms[1, first] = result[width:, :width]
-        terms[0, second] = result[width:, width:]
+    put_chunks(spread, total)
+
+
+def pair_grad_kernel(group, slots, width, *refs):
+    count = len(group)
+    states, grads, terms = refs[:count], refs[count : 2 * count], refs[2 * count]
+    for at, level in enumerate(group):
+
+        @pl.loop(0, slots // 2, unroll=UNROLL)
+        def _(index):
+            first, second = pair_of(index, level)
+            result = dot_tn(
+                side_by_side(states[at], first, second, width),
+                side_by_side(grads[at], first, second, width),
+            ).astype(BF)
+            terms[at, 0, first] = result[:width, :width]
+            terms[at, 1, second] = result[:width, width:]
+            terms[at, 1, first] = result[width:, :width]
+            terms[at, 0, second] = result[width:, width:]
 
 
 def whole(array):
@@ -187,6 +247,10 @@
 
 def rows_of(shape, tile):
     return pl.BlockSpec((tile, shape[1]), lambda i: (i, 0))
+
+
+def chunk_rows_of(shape, tile):
+    return pl.BlockSpec((shape[0], tile, shape[2]), lambda i: (0, i, 0))
 
 
 def call(kernel, steps, operands, in_specs, out_shapes, out_specs, flops, scratch=()):
@@ -220,13 +284,21 @@
     steps = 2
     smem = pl.BlockSpec(memory_space=pltpu.SMEM)
     state_shape = jax.ShapeDtypeStruct((seq_len, hidden_width), BF)
-    model_shape = jax.ShapeDtypeStruct((seq_len, model_width), BF)
-    terms_shape = jax.ShapeDtypeStruct((2, slots, width, width), BF)
+    model_shape = jax.ShapeDtypeStruct((lax.axis_size("tp"), seq_len, width_local), BF)
+    seq_size = lax.axis_size("seq")
+
+    def terms_of(count):
+        return jax.ShapeDtypeStruct((count, 2, slots, width, width), BF)
+
+    def summed(result):
+        chunked = result.reshape(result.shape[:3] + (seq_size, width // seq_size, width))
+        return halved_sum(chunked, "seq", 3)
+
     row_state = rows_of(state_shape.shape, tile)
-    row_model = rows_of(model_shape.shape, tile)
+    row_model = chunk_rows_of(model_shape.shape, tile)
     unit = 2 * seq_len * hidden_width * width
 
-    cotangent_all = lax.all_gather(cotangent, "tp", axis=1, tiled=True)
+    cotangent_all = doubled_gather(cotangent, "tp")
 
     same = jnp.eye(positions, dtype=BF)
     mixer = (
@@ -239,7 +311,7 @@
     mixed_part = dot_nn(mixer, first_rows).astype(BF)
     mixed = lax.all_to_all(mixed_part, "seq", split_axis=0, concat_axis=0, tiled=True)
     hidden_in = (tokens.astype(F32) + mixed.astype(F32)).astype(BF)
-    hidden_all = lax.all_gather(hidden_in, "tp", axis=1, tiled=True)
+    hidden_all = doubled_gather(hidden_in, "tp")
 
     local_self = [w_self] * local
     local_cross = [w_cross] * local
@@ -295,11 +367,11 @@
             1,
             [states[level], partners[level], gradient],
             [whole(states[level]), whole(states[level]), whole(gradient)],
-            [terms_shape],
-            [whole(terms_shape)],
+            [terms_of(1)],
+            [whole(terms_of(1))],
             2 * unit,
         )
-        return lax.psum_scatter(result, "seq", scatter_dimension=2, tiled=True)
+        return summed(result)[0]
 
     for level in range(last, local, -1):
         incoming = partner_2(send, "tp", level - local)
@@ -333,22 +405,25 @@
         (2 * local + 3) * unit,
         [pltpu.VMEM((tile, model_width), F32)],
     )
-    spread_part = lax.psum_scatter(spread, "tp", scatter_dimension=1, tiled=True)
-    grad_hidden = (cotangent.astype(F32) + spread_part.astype(F32)).astype(BF)
-    for level in reversed(range(local)):
+    spread_part = halved_sum(spread, "tp", 0)
+    grad_hidden = (cotangent.astype(F32) + spread_part).astype(BF)
+    for top in range(local, 0, -2):
+        group = list(range(max(top - 2, 0), top))
         (result,) = call(
-            functools.partial(pair_grad_kernel, level, slots, width),
+            functools.partial(pair_grad_kernel, group, slots, width),
             1,
-            [states[level], grads[level + 1]],
-            [whole(states[level]), whole(states[level])],
-            [terms_shape],
-            [whole(terms_shape)],
-            2 * unit,
-        )
-        terms[level] = lax.psum_scatter(result, "seq", scatter_dimension=2, tiled=True)
-
-    down_sum = lax.psum_scatter(down_part, "tp", scatter_dimension=1, tiled=True)
-    layer_out = (hidden_in.astype(F32) + down_sum.astype(F32)).astype(BF)
+            [states[level] for level in group] + [grads[level + 1] for level in group],
+            [whole(states[0])] * (2 * len(group)),
+            [terms_of(len(group))],
+            [whole(terms_of(len(group)))],
+            2 * len(group) * unit,
+        )
+        sums = summed(result)
+        for at, level in enumerate(group):
+            terms[level] = sums[at]
+
+    down_sum = halved_sum(down_part, "tp", 0)
+    layer_out = (hidden_in.astype(F32) + down_sum).astype(BF)
 
     grad_rows = lax.all_to_all(grad_hidden, "seq", split_axis=0, concat_axis=0, tiled=True)
     moved_back = dot_tn(mixer, grad_rows).astype(BF)
@@ -356,14 +431,15 @@
     cross_rows = dot_nt(grad_rows, first_rows).reshape(groups, positions, groups, positions)
     second_part = jnp.sum(cross_rows * same.astype(F32)[None, :, None, :], axis=3).transpose(1, 0, 2)
     first_part = dot_nt(returned, tokens).astype(BF)
-    second_sum, first_sum = lax.psum((second_part, first_part), "tp")
+    second_sum = exchanged_sum(second_part, "tp")
+    first_sum = exchanged_sum(first_part, "tp")
     grad_mix = dot_tn(first_factor, returned)
     grad_tokens = (grad_hidden.astype(F32) + grad_mix).astype(BF)
-    level_terms = jnp.stack(terms, axis=1).astype(F32) * token_scale
+    level_terms = jnp.stack(terms, axis=1) * token_scale
     return (
         layer_out,
         grad_tokens,
-        (first_sum.astype(F32) * model_width_scale)[None],
+        (first_sum * model_width_scale)[None],
         second_sum * model_width_scale,
         level_terms[0],
         level_terms[1],

time: 799 us -> 401 us (0.50)
  waiting for transfers between devices: 567 us -> 196 us
  Pallas kernels: 140 us -> 88 us
  starting transfers between devices: 17.4 us -> 48.9 us
  blocking collectives: 29 us -> 0 us
  local copies, waits for them, and re-layouts: 14.7 us -> 34.6 us
  other arithmetic: 8.5 us -> 21.4 us
  between operations: 14.1 us -> 1.26 us
    reduce_scatter x8 -> x0, waiting for transfers between devices: 381 us -> none  [the longest x4 218 us: per_device(): lax.psum_scatter(result, 'seq', scatter_dimension=2, tiled=True)]
    pallas_call x11 -> x9, Pallas kernels: 140 us -> 88 us  [call(): pl.pallas_call(kernel, grid=(steps,), in_specs=in_specs, out_specs=out_sp...]
    ppermute x4 -> x28, waiting for transfers between devices: 106 us -> 155 us  [partner_2(): return lax.ppermute(value, axis, pairs)]
    all_gather x2 -> x0, waiting for transfers between devices: 33.7 us -> none  [the longest x1 21.1 us: per_device(): hidden_all = lax.all_gather(hidden_in, 'tp', axis=1, tiled=True)]
    psum x1 -> x0, waiting for transfers between devices: 31.9 us -> none  [per_device(): second_sum, first_sum = lax.psum((second_part, first_part), 'tp')]
    ppermute x4 -> x28, starting transfers between devices: 0.62 us -> 29.8 us  [partner_2(): return lax.ppermute(value, axis, pairs)]
    all_to_all x1 -> x0, blocking collectives: 18.1 us -> none  [per_device(): lax.all_to_all(mixed_part, 'seq', split_axis=0, concat_axis=0, tiled=True)]
    all_to_all x0 -> x1, waiting for transfers between devices: none -> 13.1 us  [per_device(): lax.all_to_all(mixed_part, 'seq', split_axis=0, concat_axis=0, tiled=True)]
  transfers between devices with their start and end apart: 18 -> 32, of which waited for: 15 -> 17; matrix products, arithmetic and copies ran while one was open for 2% -> 12% of each run, Pallas kernels for 12% -> 14%
where the time goes in v2:
time: 401 us; the launch traced here: 399 us
  waiting for transfers between devices  196 us (49%)
  Pallas kernels  88 us (22%)
  starting transfers between devices  48.9 us (12%)
  local copies, waits for them, and re-layouts  34.6 us (9%)
  other arithmetic  21.4 us (5%)
  matrix products  9.71 us (2%)
    ppermute x28, waiting for transfers between devices, partner_2(): return lax.ppermute(value, axis, pairs)  155 us
    pallas_call x9, Pallas kernels, call(): pl.pallas_call(kernel, grid=(steps,), in_specs=in_specs, out_specs=out_sp...  88 us
    ppermute x28, starting transfers between devices, partner_2(): return lax.ppermute(value, axis, pairs)  29.8 us
    all_to_all x1, waiting for transfers between devices, per_device(): lax.all_to_all(mixed_part, 'seq', split_axis=0, concat_axis=0, tiled=True)  13.1 us
    all_to_all x1, waiting for transfers between devices, per_device(): lax.all_to_all(first_out, 'seq', split_axis=0, concat_axis=0, tiled=True)  13.1 us
    unnamed x68, local copies, waits for them, and re-layouts  12.8 us
    squeeze x12, local copies, waits for them, and re-layouts, halved_sum(): give = lax.dynamic_index_in_dim(folded, 1 - mine, dim + 1, keepdims=False)  12 us
    all_to_all x1, waiting for transfers between devices, per_device(): lax.all_to_all(moved_back, 'seq', split_axis=0, concat_axis=0, tiled=True)  10.8 us
  transfers between devices with their start and end apart: 32, of which 17 were waited for; matrix products, arithmetic and copies ran while one was open for 12% of the time, Pallas kernels for 14%

profile of v2, /device:TPU:0, one launch (start us, length us, event | category | flops | bytes accessed | tf_op | source)
XLA Modules:
  0.0 399.4 jit_solution(2887951881724409253)
XLA Ops:
  1.7 2.3 convolution_convert_fusion.3
  4.0 7.3 %all-to-all-start = ((bf16[8,64,512]{2,1,0:T(8,128)(2,1)}), bf16[8,64,512]{2,1,0:T(8,128)(2,1)}, u32[]{:S(2)}, u32[]{:S(2)}) async-start(bf16[8,64,512]{2,1,0:T(8,128)(2,1)} %bitcast.2), calls=%async_computation | async-start | bytes 1048576 | tf_op jit(solution)/shard_map/all_to_all | solution.py:310
  12.7 13.1 %all-to-all-done = bf16[8,64,512]{2,1,0:T(8,128)(2,1)} async-done(((bf16[8,64,512]{2,1,0:T(8,128)(2,1)}), bf16[8,64,512]{2,1,0:T(8,128)(2,1)}, u32[]{:S(2)}, u32[]{:S(2)}) %all-to-all-start) | async-done | bytes 524320 | tf_op jit(solution)/shard_map/all_to_all | solution.py:310
  25.8 2.3 convolution_convert_fusion.2
  28.1 3.6 all-to-all-start.1
  31.7 1.6 collective-permute-start.4
  33.3 13.1 %all-to-all-done.1 = bf16[8,64,512]{2,1,0:T(8,128)(2,1)S(1)} async-done(((bf16[8,64,512]{2,1,0:T(8,128)(2,1)}), bf16[8,64,512]{2,1,0:T(8,128)(2,1)S(1)}, u32[]{:S(2)}, u32[]{:S(2)}) %all-to-all-start.1) | async-done | bytes 524320 | tf_op jit(solution)/shard_map/all_to_all | solution.py:312
  46.6 1.6 collective-permute-start
  48.2 11.0 %collective-permute-done = bf16[512,512]{1,0:T(8,128)(2,1)} collective-permute-done((bf16[512,512]{1,0:T(8,128)(2,1)S(1)}, bf16[512,512]{1,0:T(8,128)(2,1)}, u32[]{:S(2)}, u32[]{:S(2)}) %collective-permute-start) | collective-permute-done | bytes 524320 | tf_op jit(solution)/shard_map/ppermute | solution.py:36
  59.1 2.3 select_bitcast_fusion.5
  63.2 2.3 collective-permute-done.1
  65.5 1.4 select_bitcast_fusion.3
  67.1 1.6 copy.32
  68.6 13.8 %shard_map.136 = (bf16[512,2048]{1,0:T(8,128)(2,1)}, bf16[512,2048]{1,0:T(8,128)(2,1)}, bf16[512,2048]{1,0:T(8,128)(2,1)}, bf16[512,2048]{1,0:T(8,128)(2,1)}, bf16[512,2048]{1,0:T(8,128)(2,1)}) custom-call(s32[16,2]{1,0:T(8,128)} %copy.35.pairs, bf16[4,512,512]{2,1,0:T(8,128)(2,1)} %bitcast.178, bf16[16,2,128,128]{3,2,1,0:T(8,128)(2,1)} %w_up.3, ...), custom_call_target="tpu_custom_call" | custom-call | flops 2684354560 | bytes 16777344 | tf_op jit(solution)/shard_map/pallas_call | solution.py:259
  82.7 4.2 %collective-permute-done.2.partner = bf16[512,2048]{1,0:T(8,128)(2,1)S(1)} collective-permute-done((bf16[512,2048]{1,0:T(8,128)(2,1)}, bf16[512,2048]{1,0:T(8,128)(2,1)S(1)}, u32[]{:S(2)}, u32[]{:S(2)}) %collective-permute-start.2) | collective-permute-done | bytes 2097184 | tf_op jit(solution)/shard_map/ppermute | solution.py:36
  86.9 1.4 copy-done.3
  88.4 5.4 %shard_map.137.state = bf16[512,2048]{1,0:T(8,128)(2,1)} custom-call(bf16[512,2048]{1,0:T(8,128)(2,1)} %get-tuple-element.21.state, bf16[512,2048]{1,0:T(8,128)(2,1)} %copy-done.3, bf16[6,16,128,128]{3,2,1,0:T(8,128)(2,1)} %refs_3_.3, bf16[6,16,128,128]{3,2,1,0:T(8,128)(2,1)} %refs_7_.3), custom_call_target="tpu_custom_call" | custom-call | flops 536870912 | bytes 12582912 | tf_op jit(solution)/shard_map/pallas_call | solution.py:259
  93.8 1.5 collective-permute-start.3
  95.5 2.6 collective-permute-done.5
  98.5 1.5 copy.34
  100.0 41.6 %collective-permute-done.3.partner = bf16[512,2048]{1,0:T(8,128)(2,1)S(1)} collective-permute-done((bf16[512,2048]{1,0:T(8,128)(2,1)}, bf16[512,2048]{1,0:T(8,128)(2,1)S(1)}, u32[]{:S(2)}, u32[]{:S(2)}) %collective-permute-start.3) | collective-permute-done | bytes 2097184 | tf_op jit(solution)/shard_map/ppermute | solution.py:36
  143.0 14.3 %shard_map.138 = (bf16[4,512,512]{2,1,0:T(8,128)(2,1)}, bf16[512,2048]{1,0:T(8,128)(2,1)}, bf16[512,2048]{1,0:T(8,128)(2,1)}) custom-call(s32[16,2]{1,0:T(8,128)} %copy.35.pairs, bf16[512,2048]{1,0:T(8,128)(2,1)} %shard_map.137.state, bf16[512,2048]{1,0:T(8,128)(2,1)} %copy-done.4, bf16[6,16,128,128]{3,2,1,0:T(8,128)(2,1)} %refs_3_.3, ...), custom_call_target="tpu_custom_call" | custom-call | flops 1879048192 | bytes 13631616 | tf_op jit(solution)/shard_map/pallas_call | solution.py:259
  157.3 1.5 collective-permute-start.8
  158.8 6.8 %shard_map.144 = bf16[1,2,16,128,128]{4,3,2,1,0:T(8,128)(2,1)} custom-call(bf16[512,2048]{1,0:T(8,128)(2,1)} %shard_map.137.state, bf16[512,2048]{1,0:T(8,128)(2,1)} %copy-done.4, bf16[512,2048]{1,0:T(8,128)(2,1)} %get-tuple-element.23.grad), custom_call_target="tpu_custom_call" | custom-call | flops 536870912 | bytes 7340032 | tf_op jit(solution)/shard_map/pallas_call | solution.py:259
  165.6 1.9 dynamic-slice_bitcast_fusion.3
  167.5 2.0 collective-permute-start.25
  169.5 34.9 %collective-permute-done.8.incoming = bf16[512,2048]{1,0:T(8,128)(2,1)S(1)} collective-permute-done((bf16[512,2048]{1,0:T(8,128)(2,1)}, bf16[512,2048]{1,0:T(8,128)(2,1)S(1)}, u32[]{:S(2)}, u32[]{:S(2)}) %collective-permute-start.8) | collective-permute-done | bytes 2097184 | tf_op jit(solution)/shard_map/ppermute | solution.py:36
  204.3 1.3 copy-done.13
  205.7 6.4 %shard_map.139 = (bf16[512,2048]{1,0:T(8,128)(2,1)}, bf16[512,2048]{1,0:T(8,128)(2,1)}) custom-call(bf16[512,2048]{1,0:T(8,128)(2,1)} %get-tuple-element.23.grad, bf16[512,2048]{1,0:T(8,128)(2,1)} %copy-done.13, bf16[6,16,128,128]{3,2,1,0:T(8,128)(2,1)} %refs_3_.3, bf16[6,16,128,128]{3,2,1,0:T(8,128)(2,1)} %refs_7_.3), custom_call_target="tpu_custom_call" | custom-call | flops 536870912 | bytes 14680064 | tf_op jit(solution)/shard_map/pallas_call | solution.py:259
  212.2 2.4 dynamic-slice_bitcast_fusion.2
  218.0 6.7 %shard_map.143 = bf16[1,2,16,128,128]{4,3,2,1,0:T(8,128)(2,1)} custom-call(bf16[512,2048]{1,0:T(8,128)(2,1)} %get-tuple-element.21.state, bf16[512,2048]{1,0:T(8,128)(2,1)} %copy-done.3, bf16[512,2048]{1,0:T(8,128)(2,1)} %get-tuple-element.25.grad), custom_call_target="tpu_custom_call" | custom-call | flops 536870912 | bytes 7340032 | tf_op jit(solution)/shard_map/pallas_call | solution.py:259
  225.9 2.1 collective-permute-start.22
  228.8 2.9 collective-permute-start.27
  231.8 1.5 fusion.3
  233.3 1.6 collective-permute-start.7
  234.9 5.3 %collective-permute-done.22 = bf16[1,2,16,4,16,128]{5,4,3,2,1,0:T(8,128)(2,1)S(1)} collective-permute-done((bf16[1,2,16,4,16,128]{5,4,3,2,1,0:T(8,128)(2,1)S(1)}, bf16[1,2,16,4,16,128]{5,4,3,2,1,0:T(8,128)(2,1)S(1)}, u32[]{:S(2)}, u32[]{:S(2)}) %collective-permute-start.22) | collective-permute-done | bytes 524320 | tf_op jit(solution)/shard_map/ppermute | solution.py:36
  240.4 18.8 %shard_map.140 = (bf16[512,2048]{1,0:T(8,128)(2,1)}, bf16[512,2048]{1,0:T(8,128)(2,1)}, bf16[512,2048]{1,0:T(8,128)(2,1)}, bf16[512,2048]{1,0:T(8,128)(2,1)}, bf...) custom-call(s32[16,2]{1,0:T(8,128)} %copy.35.pairs, bf16[512,2048]{1,0:T(8,128)(2,1)} %get-tuple-element.25.grad, ...), custom_call_target="tpu_custom_call" | custom-call | flops 2952790016 | bytes 19923072 | tf_op jit(solution)/shard_map/pallas_call | solution.py:259
  259.3 7.7 %shard_map.142 = bf16[2,2,16,128,128]{4,3,2,1,0:T(8,128)(2,1)} custom-call(bf16[512,2048]{1,0:T(8,128)(2,1)} %get-tuple-element.32.refs_0_, bf16[512,2048]{1,0:T(8,128)(2,1)} %get-tuple-element.33.refs_1_, bf16[512,2048]{1,0:T(8,128)(2,1)} %get-tuple-element.34.refs_2_, bf16[512,2048]{1,0:T(8,128)(2,1)} %get-tuple-element.35.refs_3_), custom_call_target="tpu_custom_call" | custom-call | flops 1073741824 | bytes 10485760 | tf_op jit(solution)/shard_map/pallas_call | solution.py:259
  267.0 2.5 dynamic-slice_bitcast_fusion
  269.5 1.7 collective-permute-start.19
  271.9 1.7 collective-permute-start.23
  273.7 7.9 %shard_map.141 = bf16[2,2,16,128,128]{4,3,2,1,0:T(8,128)(2,1)} custom-call(bf16[512,2048]{1,0:T(8,128)(2,1)} %get-tuple-element.28.refs_0_, bf16[512,2048]{1,0:T(8,128)(2,1)} %get-tuple-element.29.refs_1_, bf16[512,2048]{1,0:T(8,128)(2,1)} %get-tuple-element.30.refs_2_, bf16[512,2048]{1,0:T(8,128)(2,1)} %get-tuple-element.31.refs_3_), custom_call_target="tpu_custom_call" | custom-call | flops 1073741824 | bytes 10485760 | tf_op jit(solution)/shard_map/pallas_call | solution.py:259
  281.6 2.5 dynamic-slice_bitcast_fusion.1
  291.7 2.3 copy.56
  294.0 1.8 collective-permute-done.19
  295.9 1.6 fusion
  297.8 1.8 collective-permute-start.20
  299.6 17.4 %collective-permute-done.16 = bf16[2,2,16,4,16,128]{5,4,3,2,1,0:T(8,128)(2,1)} collective-permute-done((bf16[2,2,16,4,16,128]{5,4,3,2,1,0:T(8,128)(2,1)}, bf16[2,2,16,4,16,128]{5,4,3,2,1,0:T(8,128)(2,1)}, u32[]{:S(2)}, u32[]{:S(2)}) %collective-permute-start.16) | collective-permute-done | bytes 1048608 | tf_op jit(solution)/shard_map/ppermute | solution.py:36
  317.0 1.6 fusion.1
  318.6 1.4 collective-permute-start.17
  320.1 1.5 fusion.2
  321.7 1.5 collective-permute-start.11
  323.3 1.4 collective-permute-start.21
  324.7 12.2 %collective-permute-done.17 = bf16[2,2,16,2,16,128]{5,4,3,2,1,0:T(8,128)(2,1)S(1)} collective-permute-done((bf16[2,2,16,2,16,128]{5,4,3,2,1,0:T(8,128)(2,1)S(1)}, bf16[2,2,16,2,16,128]{5,4,3,2,1,0:T(8,128)(2,1)S(1)}, u32[]{:S(2)}, u32[]{:S(2)}) %collective-permute-start.17) | collective-permute-done | bytes 524320 | tf_op jit(solution)/shard_map/ppermute | solution.py:36
  338.5 4.7 %all-to-all-start.2 = ((bf16[8,64,512]{2,1,0:T(8,128)(2,1)}), bf16[8,64,512]{2,1,0:T(8,128)(2,1)}, u32[]{:S(2)}, u32[]{:S(2)}) async-start(bf16[8,64,512]{2,1,0:T(8,128)(2,1)} %bitcast.24), calls=%async_computation.2 | async-start | bytes 1048576 | tf_op jit(solution)/shard_map/all_to_all | solution.py:428
  343.2 12.1 %collective-permute-done.18 = bf16[2,2,16,1,16,128]{5,4,3,2,1,0:T(8,128)(2,1)S(1)} collective-permute-done((bf16[2,2,16,1,16,128]{5,4,3,2,1,0:T(8,128)(2,1)S(1)}, bf16[2,2,16,1,16,128]{5,4,3,2,1,0:T(8,128)(2,1)S(1)}, u32[]{:S(2)}, u32[]{:S(2)}) %collective-permute-start.18) | collective-permute-done | bytes 262176 | tf_op jit(solution)/shard_map/ppermute | solution.py:36
  357.4 3.6 all-to-all-done.2
  360.9 2.3 convolution_convert_fusion.1
  363.2 3.5 all-to-all-start.3
  368.8 1.9 multiply_reduce_fusion
  370.8 10.8 %all-to-all-done.3 = bf16[8,64,512]{2,1,0:T(8,128)(2,1)S(1)} async-done(((bf16[8,64,512]{2,1,0:T(8,128)(2,1)}), bf16[8,64,512]{2,1,0:T(8,128)(2,1)S(1)}, u32[]{:S(2)}, u32[]{:S(2)}) %all-to-all-start.3) | async-done | bytes 524320 | tf_op jit(solution)/shard_map/all_to_all | solution.py:430
  382.3 1.4 collective-permute-start.15
  384.2 1.4 collective-permute-start.13
  389.1 9.2 %collective-permute-done.13 = bf16[512,512]{1,0:T(8,128)(2,1)S(1)} collective-permute-done((bf16[512,512]{1,0:T(8,128)(2,1)S(1)}, bf16[512,512]{1,0:T(8,128)(2,1)S(1)}, u32[]{:S(2)}, u32[]{:S(2)}) %collective-permute-start.13) | collective-permute-done | bytes 524320 | tf_op jit(solution)/shard_map/ppermute | solution.py:36
  (142 shorter events, 32.5 us)
Async XLA Ops:
  0.6 1.0 copy-start
  0.6 10.7 %copy-start.28 = (bf16[64,8,8]{0,2,1:T(8,128)(2,1)S(1)}, bf16[64,8,8]{0,2,1:T(8,128)(2,1)}, u32[]{:S(2)}) copy-start(bf16[64,8,8]{0,2,1:T(8,128)(2,1)} %param.11) | copy-start | bytes 24580
  4.0 21.8 %all-to-all-start = ((bf16[8,64,512]{2,1,0:T(8,128)(2,1)}), bf16[8,64,512]{2,1,0:T(8,128)(2,1)}, u32[]{:S(2)}, u32[]{:S(2)}) async-start(bf16[8,64,512]{2,1,0:T(8,128)(2,1)} %bitcast.2), calls=%async_computation | async-start | bytes 1048576 | tf_op jit(solution)/shard_map/all_to_all | solution.py:310
  12.1 19.6 %copy-start.17 = (bf16[512,512]{1,0:T(8,128)(2,1)S(1)}, bf16[512,512]{1,0:T(8,128)(2,1)}, u32[]{:S(2)}) copy-start(bf16[512,512]{1,0:T(8,128)(2,1)} %param.17) | copy-start | bytes 1572868
  12.1 34.3 %copy-start.5 = (bf16[512,512]{1,0:T(8,128)(2,1)S(1)}, bf16[512,512]{1,0:T(8,128)(2,1)}, u32[]{:S(2)}) copy-start(bf16[512,512]{1,0:T(8,128)(2,1)} %param.9) | copy-start | bytes 1572868
  12.7 33.8 %copy-start.14 = (bf16[512,512]{1,0:T(8,128)(2,1)}, bf16[512,512]{1,0:T(8,128)(2,1)S(1)}, u32[]{:S(2)}) copy-start(bf16[512,512]{1,0:T(8,128)(2,1)S(1)} %mul.56) | copy-start | bytes 1572868
  28.1 18.3 %all-to-all-start.1 = ((bf16[8,64,512]{2,1,0:T(8,128)(2,1)}), bf16[8,64,512]{2,1,0:T(8,128)(2,1)S(1)}, u32[]{:S(2)}, u32[]{:S(2)}) async-start(bf16[8,64,512]{2,1,0:T(8,128)(2,1)} %bitcast.4), calls=%async_computation.1 | async-start | bytes 1048576 | tf_op jit(solution)/shard_map/all_to_all | solution.py:312
  31.7 16.4 %collective-permute-start.4 = (bf16[512,512]{1,0:T(8,128)(2,1)S(1)}, bf16[512,512]{1,0:T(8,128)(2,1)}, u32[]{:S(2)}, u32[]{:S(2)}) collective-permute-start(bf16[512,512]{1,0:T(8,128)(2,1)S(1)} %copy-done.17), channel_id=1, source_target_pairs={{0,2},{1,3},{2,0},{3,1},{4,6},{5,7},{6,4},{7,5},{8,10},{9,11},{10,... | collective-permute-start | bytes 1572872 | tf_op jit(solution)/shard_map/ppermute | solution.py:36
  46.6 14.9 %copy-start.6 = (bf16[512,512]{1,0:T(8,128)(2,1)}, bf16[512,512]{1,0:T(8,128)(2,1)S(1)}, u32[]{:S(2)}) copy-start(bf16[512,512]{1,0:T(8,128)(2,1)S(1)} %fusion.10) | copy-start | bytes 1572868
  46.6 12.6 %collective-permute-start = (bf16[512,512]{1,0:T(8,128)(2,1)S(1)}, bf16[512,512]{1,0:T(8,128)(2,1)}, u32[]{:S(2)}, u32[]{:S(2)}) collective-permute-start(bf16[512,512]{1,0:T(8,128)(2,1)S(1)} %fusion.10), channel_id=1, source_target_pairs={{0,2},{1,3},{2,0},{3,1},{4,6},{5,7},{6,4},{7,5},{8,10},{9,11},{10,... | collective-permute-start | bytes 1572872 | tf_op jit(solution)/shard_map/ppermute | solution.py:36
  61.4 1.1 copy-start.29
  62.5 3.0 collective-permute-start.1
  82.5 12.8 %copy-start.8 = (bf16[1,512,512]{2,1,0:T(8,128)(2,1)S(1)}, bf16[1,512,512]{2,1,0:T(8,128)(2,1)}, u32[]{:S(2)}) copy-start(bf16[1,512,512]{2,1,0:T(8,128)(2,1)} %get-tuple-element.58) | copy-start | bytes 1572868
  82.5 12.8 %copy-start.9 = (bf16[1,512,512]{2,1,0:T(8,128)(2,1)S(1)}, bf16[1,512,512]{2,1,0:T(8,128)(2,1)}, u32[]{:S(2)}) copy-start(bf16[1,512,512]{2,1,0:T(8,128)(2,1)} %get-tuple-element.59) | copy-start | bytes 1572868
  82.5 4.4 %collective-permute-start.2 = (bf16[512,2048]{1,0:T(8,128)(2,1)}, bf16[512,2048]{1,0:T(8,128)(2,1)S(1)}, u32[]{:S(2)}, u32[]{:S(2)}) collective-permute-start(bf16[512,2048]{1,0:T(8,128)(2,1)} %get-tuple-element.21.state), channel_id=1, source_target_pairs={{0,1},{1,0},{2,3},{3,2},{4,5},{5,4},{6,7},{7,6},{8,9},{9,8},{10,11... | collective-permute-start | bytes 6291464 | tf_op jit(solution)/shard_map/ppermute | solution.py:36
  86.9 1.4 copy-start.3
  93.8 47.9 %collective-permute-start.3 = (bf16[512,2048]{1,0:T(8,128)(2,1)}, bf16[512,2048]{1,0:T(8,128)(2,1)S(1)}, u32[]{:S(2)}, u32[]{:S(2)}) collective-permute-start(bf16[512,2048]{1,0:T(8,128)(2,1)} %shard_map.137.state), channel_id=1, source_target_pairs={{0,2},{1,3},{2,0},{3,1},{4,6},{5,7},{6,4},{7,5},{8,10},{9,11},{10,... | collective-permute-start | bytes 6291464 | tf_op jit(solution)/shard_map/ppermute | solution.py:36
  95.4 2.7 collective-permute-start.5
  141.6 1.3 copy-start.4
  157.3 47.0 %collective-permute-start.8 = (bf16[512,2048]{1,0:T(8,128)(2,1)}, bf16[512,2048]{1,0:T(8,128)(2,1)S(1)}, u32[]{:S(2)}, u32[]{:S(2)}) collective-permute-start(bf16[512,2048]{1,0:T(8,128)(2,1)} %get-tuple-element.24), channel_id=1, source_target_pairs={{0,2},{1,3},{2,0},{3,1},{4,6},{5,7},{6,4},{7,5},{8,10},{9,11},{10,... | collective-permute-start | bytes 6291464 | tf_op jit(solution)/shard_map/ppermute | solution.py:36
  167.5 48.5 %collective-permute-start.25 = (bf16[1,2,16,4,16,128]{5,4,3,2,1,0:T(8,128)(2,1)}, bf16[1,2,16,4,16,128]{5,4,3,2,1,0:T(8,128)(2,1)}, u32[]{:S(2)}, u32[]{:S(2)}) collective-permute-start(bf16[1,2,16,4,16,128]{5,4,3,2,1,0:T(8,128)(2,1)} %dynamic-slice_bitcast_fusion.3), channel_id=1, source_target_pairs={{0,4},{4,0},{8,12},{12,8},{16,20},{20,16},{24,28},{28,24},{1,5},{5... | collective-permute-start | bytes 1572872 | tf_op jit(solution)/shard_map/ppermute | solution.py:36
  204.3 1.3 copy-start.13
  212.1 2.8 copy-start.18
  212.1 3.9 copy-start.10
  212.1 28.3 %collective-permute-start.9 = (bf16[512,2048]{1,0:T(8,128)(2,1)}, bf16[512,2048]{1,0:T(8,128)(2,1)}, u32[]{:S(2)}, u32[]{:S(2)}) collective-permute-start(bf16[512,2048]{1,0:T(8,128)(2,1)} %get-tuple-element.26), channel_id=1, source_target_pairs={{0,1},{1,0},{2,3},{3,2},{4,5},{5,4},{6,7},{7,6},{8,9},{9,8},{10,11... | collective-permute-start | bytes 6291464 | tf_op jit(solution)/shard_map/ppermute | solution.py:36
  214.6 17.2 %collective-permute-start.6 = (bf16[2,512,512]{2,1,0:T(8,128)(2,1)}, bf16[2,512,512]{2,1,0:T(8,128)(2,1)}, u32[]{:S(2)}, u32[]{:S(2)}) collective-permute-start(bf16[2,512,512]{2,1,0:T(8,128)(2,1)} %dynamic-slice_bitcast_fusion.2), channel_id=1, source_target_pairs={{0,1},{1,0},{2,3},{3,2},{4,5},{5,4},{6,7},{7,6},{8,9},{9,8},{10,11... | collective-permute-start | bytes 3145736 | tf_op jit(solution)/shard_map/ppermute | solution.py:36
  217.3 10.8 %collective-permute-start.26 = (bf16[1,2,16,2,16,128]{5,4,2,1,3,0:T(8,128)(2,1)S(1)}, bf16[1,2,16,2,16,128]{5,4,2,1,3,0:T(8,128)(2,1)S(1)}, u32[]{:S(2)}, u32[]{:S(2)}) collective-permute-start(bf16[1,2,16,2,16,128]{5,4,2,1,3,0:T(8,128)(2,1)S(1)} %bitcast.197), channel_id=1, source_target_pairs={{0,8},{4,12},{8,0},{12,4},{16,24},{20,28},{24,16},{28,20},{1,9},{5... | collective-permute-start | bytes 786440 | tf_op jit(solution)/shard_map/ppermute | solution.py:36
  224.7 7.1 %copy-start.23 = (bf16[4,512,512]{2,1,0:T(8,128)(2,1)S(1)}, bf16[4,512,512]{2,1,0:T(8,128)(2,1)}, u32[]{:S(2)}) copy-start(bf16[4,512,512]{2,1,0:T(8,128)(2,1)} %get-tuple-element.22) | copy-start | bytes 6291460
  225.9 14.3 %collective-permute-start.22 = (bf16[1,2,16,4,16,128]{5,4,3,2,1,0:T(8,128)(2,1)S(1)}, bf16[1,2,16,4,16,128]{5,4,3,2,1,0:T(8,128)(2,1)S(1)}, u32[]{:S(2)}, u32[]{:S(2)}) collective-permute-start(bf16[1,2,16,4,16,128]{5,4,3,2,1,0:T(8,128)(2,1)S(1)} %dynamic-slice_bitcast_fusion.4), channel_id=1, source_target_pairs={{0,4},{4,0},{8,12},{12,8},{16,20},{20,16},{24,28},{28,24},{1,5},{5... | collective-permute-start | bytes 1572872 | tf_op jit(solution)/shard_map/ppermute | solution.py:36
  228.1 3.7 copy-start.25
  228.8 11.4 %copy-start.12 = (bf16[1,2,16,128,128]{4,3,2,1,0:T(8,128)(2,1)S(1)}, bf16[1,2,16,128,128]{4,3,2,1,0:T(8,128)(2,1)}, u32[]{:S(2)}) copy-start(bf16[1,2,16,128,128]{4,3,2,1,0:T(8,128)(2,1)} %shard_map.143) | copy-start | bytes 3145732
  228.8 139.9 %collective-permute-start.27 = (bf16[1,2,16,1,16,128]{5,4,2,1,3,0:T(8,128)(2,1)}, bf16[1,2,16,1,16,128]{5,4,2,1,3,0:T(8,128)(2,1)S(1)}, u32[]{:S(2)}, u32[]{:S(2)}) collective-permute-start(bf16[1,2,16,1,16,128]{5,4,2,1,3,0:T(8,128)(2,1)} %constant_dynamic-slice_fusion), channel_id=1, source_target_pairs={{0,16},{4,20},{8,24},{12,28},{16,0},{20,4},{24,8},{28,12},{1,17},{... | collective-permute-start | bytes 393224 | tf_op jit(solution)/shard_map/ppermute | solution.py:36
  233.3 51.1 %collective-permute-start.7 = (bf16[1,512,512]{2,1,0:T(8,128)(2,1)S(1)}, bf16[1,512,512]{2,1,0:T(8,128)(2,1)S(1)}, u32[]{:S(2)}, u32[]{:S(2)}) collective-permute-start(bf16[1,512,512]{2,1,0:T(8,128)(2,1)S(1)} %constant_dynamic-slice_fusion.13), channel_id=1, source_target_pairs={{0,2},{1,3},{2,0},{3,1},{4,6},{5,7},{6,4},{7,5},{8,10},{9,11},{10,... | collective-permute-start | bytes 1572872 | tf_op jit(solution)/shard_map/ppermute | solution.py:36
  269.5 26.4 %collective-permute-start.19 = (bf16[2,2,16,4,16,128]{5,4,3,2,1,0:T(8,128)(2,1)}, bf16[2,2,16,4,16,128]{5,4,3,2,1,0:T(8,128)(2,1)}, u32[]{:S(2)}, u32[]{:S(2)}) collective-permute-start(bf16[2,2,16,4,16,128]{5,4,3,2,1,0:T(8,128)(2,1)} %dynamic-slice_bitcast_fusion), channel_id=1, source_target_pairs={{0,4},{4,0},{8,12},{12,8},{16,20},{20,16},{24,28},{28,24},{1,5},{5... | collective-permute-start | bytes 3145736 | tf_op jit(solution)/shard_map/ppermute | solution.py:36
  271.9 16.0 %collective-permute-start.23 = (bf16[1,2,16,2,16,128]{5,4,2,1,3,0:T(8,128)(2,1)}, bf16[1,2,16,2,16,128]{5,4,2,1,3,0:T(8,128)(2,1)}, u32[]{:S(2)}, u32[]{:S(2)}) collective-permute-start(bf16[1,2,16,2,16,128]{5,4,2,1,3,0:T(8,128)(2,1)} %bitcast.172), channel_id=1, source_target_pairs={{0,8},{4,12},{8,0},{12,4},{16,24},{20,28},{24,16},{28,20},{1,9},{5... | collective-permute-start | bytes 786440 | tf_op jit(solution)/shard_map/ppermute | solution.py:36
  281.6 2.8 copy-start.7
  281.6 3.8 copy-start.16
  284.1 32.8 %collective-permute-start.16 = (bf16[2,2,16,4,16,128]{5,4,3,2,1,0:T(8,128)(2,1)}, bf16[2,2,16,4,16,128]{5,4,3,2,1,0:T(8,128)(2,1)}, u32[]{:S(2)}, u32[]{:S(2)}) collective-permute-start(bf16[2,2,16,4,16,128]{5,4,3,2,1,0:T(8,128)(2,1)} %dynamic-slice_bitcast_fusion.1), channel_id=1, source_target_pairs={{0,4},{4,0},{8,12},{12,8},{16,20},{20,16},{24,28},{28,24},{1,5},{5... | collective-permute-start | bytes 3145736 | tf_op jit(solution)/shard_map/ppermute | solution.py:36
  287.9 7.9 %copy-start.1 = (bf16[2,2,16,128,128]{4,3,2,1,0:T(8,128)(2,1)S(1)}, bf16[2,2,16,128,128]{4,3,2,1,0:T(8,128)(2,1)}, u32[]{:S(2)}) copy-start(bf16[2,2,16,128,128]{4,3,2,1,0:T(8,128)(2,1)} %shard_map.142) | copy-start | bytes 6291460
  287.9 32.1 %collective-permute-start.10 = (bf16[2,512,512]{1,2,0:T(8,128)(2,1)}, bf16[2,512,512]{1,2,0:T(8,128)(2,1)}, u32[]{:S(2)}, u32[]{:S(2)}) collective-permute-start(bf16[2,512,512]{1,2,0:T(8,128)(2,1)} %bitcast.194), channel_id=1, source_target_pairs={{0,1},{1,0},{2,3},{3,2},{4,5},{5,4},{6,7},{7,6},{8,9},{9,8},{10,11... | collective-permute-start | bytes 3145736 | tf_op jit(solution)/shard_map/ppermute | solution.py:36
  289.1 0.7 copy-start.27
  290.5 77.2 %collective-permute-start.24 = (bf16[1,2,16,1,16,128]{5,4,2,1,3,0:T(8,128)(2,1)}, bf16[1,2,16,1,16,128]{5,4,2,1,3,0:T(8,128)(2,1)}, u32[]{:S(2)}, u32[]{:S(2)}) collective-permute-start(bf16[1,2,16,1,16,128]{5,4,2,1,3,0:T(8,128)(2,1)} %constant_dynamic-slice_fusion.3), channel_id=1, source_target_pairs={{0,16},{4,20},{8,24},{12,28},{16,0},{20,4},{24,8},{28,12},{1,17},{... | collective-permute-start | bytes 393224 | tf_op jit(solution)/shard_map/ppermute | solution.py:36
  297.5 19.5 %copy-start.2 = (bf16[2,2,16,128,128]{4,3,2,1,0:T(8,128)(2,1)S(1)}, bf16[2,2,16,128,128]{4,3,2,1,0:T(8,128)(2,1)}, u32[]{:S(2)}) copy-start(bf16[2,2,16,128,128]{4,3,2,1,0:T(8,128)(2,1)} %shard_map.141) | copy-start | bytes 6291460
  297.8 22.3 %copy-start.11 = (bf16[2,1,512,512]{2,3,0,1:T(8,128)(2,1)S(1)}, bf16[2,1,512,512]{2,3,0,1:T(8,128)(2,1)}, u32[]{:S(2)}) copy-start(bf16[2,1,512,512]{2,3,0,1:T(8,128)(2,1)} %copy.56) | copy-start | bytes 3145732
  297.8 25.4 %collective-permute-start.20 = (bf16[2,2,16,2,16,128]{5,4,2,1,3,0:T(8,128)(2,1)S(1)}, bf16[2,2,16,2,16,128]{5,4,2,1,3,0:T(8,128)(2,1)S(1)}, u32[]{:S(2)}, u32[]{:S(2)}) collective-permute-start(bf16[2,2,16,2,16,128]{5,4,2,1,3,0:T(8,128)(2,1)S(1)} %bitcast.196), channel_id=1, source_target_pairs={{0,8},{4,12},{8,0},{12,4},{16,24},{20,28},{24,16},{28,20},{1,9},{5... | collective-permute-start | bytes 1572872 | tf_op jit(solution)/shard_map/ppermute | solution.py:36
  318.6 18.3 %collective-permute-start.17 = (bf16[2,2,16,2,16,128]{5,4,3,2,1,0:T(8,128)(2,1)S(1)}, bf16[2,2,16,2,16,128]{5,4,3,2,1,0:T(8,128)(2,1)S(1)}, u32[]{:S(2)}, u32[]{:S(2)}) collective-permute-start(bf16[2,2,16,2,16,128]{5,4,3,2,1,0:T(8,128)(2,1)S(1)} %dynamic-slice_bitcast_fusion.5), channel_id=1, source_target_pairs={{0,8},{4,12},{8,0},{12,4},{16,24},{20,28},{24,16},{28,20},{1,9},{5... | collective-permute-start | bytes 1572872 | tf_op jit(solution)/shard_map/ppermute | solution.py:36
  321.7 15.6 %collective-permute-start.11 = (bf16[1,512,512]{1,2,0:T(8,128)(2,1)S(1)}, bf16[1,512,512]{1,2,0:T(8,128)(2,1)S(1)}, u32[]{:S(2)}, u32[]{:S(2)}) collective-permute-start(bf16[1,512,512]{1,2,0:T(8,128)(2,1)S(1)} %constant_dynamic-slice_fusion.10), channel_id=1, source_target_pairs={{0,2},{1,3},{2,0},{3,1},{4,6},{5,7},{6,4},{7,5},{8,10},{9,11},{10,... | collective-permute-start | bytes 1572872 | tf_op jit(solution)/shard_map/ppermute | solution.py:36
  323.1 14.1 %copy-start.19 = (bf16[512,512]{0,1:T(8,128)(2,1)S(1)}, bf16[512,512]{0,1:T(8,128)(2,1)}, u32[]{:S(2)}) copy-start(bf16[512,512]{0,1:T(8,128)(2,1)} %copy.37) | copy-start | bytes 1572868
  323.3 13.9 %copy-start.22 = (bf16[2,2,16,2,16,128]{5,4,2,1,3,0:T(8,128)(2,1)}, bf16[2,2,16,2,16,128]{5,4,2,1,3,0:T(8,128)(2,1)S(1)}, u32[]{:S(2)}) copy-start(bf16[2,2,16,2,16,128]{5,4,2,1,3,0:T(8,128)(2,1)S(1)} %fusion.8) | copy-start | bytes 1572868
  323.3 32.1 %collective-permute-start.21 = (bf16[2,2,16,1,16,128]{5,4,2,1,3,0:T(8,128)(2,1)S(1)}, bf16[2,2,16,1,16,128]{5,4,2,1,3,0:T(8,128)(2,1)}, u32[]{:S(2)}, u32[]{:S(2)}) collective-permute-start(bf16[2,2,16,1,16,128]{5,4,2,1,3,0:T(8,128)(2,1)S(1)} %constant_dynamic-slice_fusion.6), channel_id=1, source_target_pairs={{0,16},{4,20},{8,24},{12,28},{16,0},{20,4},{24,8},{28,12},{1,17},{... | collective-permute-start | bytes 786440 | tf_op jit(solution)/shard_map/ppermute | solution.py:36
  337.1 18.2 %collective-permute-start.18 = (bf16[2,2,16,1,16,128]{5,4,3,2,1,0:T(8,128)(2,1)S(1)}, bf16[2,2,16,1,16,128]{5,4,3,2,1,0:T(8,128)(2,1)S(1)}, u32[]{:S(2)}, u32[]{:S(2)}) collective-permute-start(bf16[2,2,16,1,16,128]{5,4,3,2,1,0:T(8,128)(2,1)S(1)} %constant_dynamic-slice_fusion.9), channel_id=1, source_target_pairs={{0,16},{4,20},{8,24},{12,28},{16,0},{20,4},{24,8},{28,12},{1,17},{... | collective-permute-start | bytes 786440 | tf_op jit(solution)/shard_map/ppermute | solution.py:36
  337.4 17.9 %copy-start.20 = (bf16[512,512]{0,1:T(8,128)(2,1)}, bf16[512,512]{0,1:T(8,128)(2,1)S(1)}, u32[]{:S(2)}) copy-start(bf16[512,512]{0,1:T(8,128)(2,1)S(1)} %fusion.11) | copy-start | bytes 1572868
  338.5 22.5 %all-to-all-start.2 = ((bf16[8,64,512]{2,1,0:T(8,128)(2,1)}), bf16[8,64,512]{2,1,0:T(8,128)(2,1)}, u32[]{:S(2)}, u32[]{:S(2)}) async-start(bf16[8,64,512]{2,1,0:T(8,128)(2,1)} %bitcast.24), calls=%async_computation.2 | async-start | bytes 1048576 | tf_op jit(solution)/shard_map/all_to_all | solution.py:428
  343.2 17.8 %copy-start.15 = (bf16[512,512]{1,0:T(8,128)(2,1)S(1)}, bf16[512,512]{1,0:T(8,128)(2,1)}, u32[]{:S(2)}) copy-start(bf16[512,512]{1,0:T(8,128)(2,1)} %copy-done.14) | copy-start | bytes 1572868
  356.5 0.8 copy-start.24
  357.3 11.4 %copy-start.26 = (bf16[1,2,16,2,16,128]{5,4,2,1,3,0:T(8,128)(2,1)S(1)}, bf16[1,2,16,2,16,128]{5,4,2,1,3,0:T(8,128)(2,1)}, u32[]{:S(2)}) copy-start(bf16[1,2,16,2,16,128]{5,4,2,1,3,0:T(8,128)(2,1)} %copy-done.25) | copy-start | bytes 786436
  363.2 18.4 %all-to-all-start.3 = ((bf16[8,64,512]{2,1,0:T(8,128)(2,1)}), bf16[8,64,512]{2,1,0:T(8,128)(2,1)S(1)}, u32[]{:S(2)}, u32[]{:S(2)}) async-start(bf16[8,64,512]{2,1,0:T(8,128)(2,1)} %bitcast.195), calls=%async_computation.3 | async-start | bytes 1048576 | tf_op jit(solution)/shard_map/all_to_all | solution.py:430
  370.7 11.6 %collective-permute-start.14 = (f32[64,8,8]{0,2,1:T(8,128)S(1)}, f32[64,8,8]{0,2,1:T(8,128)S(1)}, u32[]{:S(2)}, u32[]{:S(2)}) collective-permute-start(f32[64,8,8]{0,2,1:T(8,128)S(1)} %bitcast.198), channel_id=1, source_target_pairs={{0,1},{1,0},{2,3},{3,2},{4,5},{5,4},{6,7},{7,6},{8,9},{9,8},{10,11... | collective-permute-start | bytes 49160 | tf_op jit(solution)/shard_map/ppermute | solution.py:36
  382.1 2.0 collective-permute-start.12
  382.3 5.3 %copy-start.21 = (bf16[512,512]{0,1:T(8,128)(2,1)S(1)}, bf16[512,512]{0,1:T(8,128)(2,1)}, u32[]{:S(2)}) copy-start(bf16[512,512]{0,1:T(8,128)(2,1)} %copy-done.20) | copy-start | bytes 1572868
  382.3 4.7 %collective-permute-start.15 = (f32[64,8,8]{0,2,1:T(8,128)S(1)}, f32[64,8,8]{0,2,1:T(8,128)S(1)}, u32[]{:S(2)}, u32[]{:S(2)}) collective-permute-start(f32[64,8,8]{0,2,1:T(8,128)S(1)} %bitcast_add_fusion.2), channel_id=1, source_target_pairs={{0,2},{1,3},{2,0},{3,1},{4,6},{5,7},{6,4},{7,5},{8,10},{9,11},{10,... | collective-permute-start | bytes 49160 | tf_op jit(solution)/shard_map/ppermute | solution.py:36
  384.2 14.0 %collective-permute-start.13 = (bf16[512,512]{1,0:T(8,128)(2,1)S(1)}, bf16[512,512]{1,0:T(8,128)(2,1)S(1)}, u32[]{:S(2)}, u32[]{:S(2)}) collective-permute-start(bf16[512,512]{1,0:T(8,128)(2,1)S(1)} %add_convert_fusion), channel_id=1, source_target_pairs={{0,2},{1,3},{2,0},{3,1},{4,6},{5,7},{6,4},{7,5},{8,10},{9,11},{10,... | collective-permute-start | bytes 1572872 | tf_op jit(solution)/shard_map/ppermute | solution.py:36

commit v3 on v2

--- a/solution.py
+++ b/solution.py
@@ -44,16 +44,25 @@
     return lax.axis_size(axis).bit_length() - 1
 
 
-def halved_sum(value, axis, dim):
-    for bit in range(bits_of(axis)):
-        shape = value.shape
-        folded = value.reshape(shape[:dim] + (shape[dim] // 2, 2) + shape[dim + 1 :])
-        mine = bit_of(axis, bit)
-        keep = lax.dynamic_index_in_dim(folded, mine, dim + 1, keepdims=False)
-        give = lax.dynamic_index_in_dim(folded, 1 - mine, dim + 1, keepdims=False)
-        total = keep.astype(F32) + partner_2(give, axis, bit).astype(F32)
+def halve(value, axis, dim, left, bit):
+    at = dim + left.index(bit)
+    mine = bit_of(axis, bit)
+    keep = lax.dynamic_index_in_dim(value, mine, at, keepdims=False)
+    give = lax.dynamic_index_in_dim(value, 1 - mine, at, keepdims=False)
+    total = keep.astype(F32) + partner_2(give, axis, bit).astype(F32)
+    return total, [other for other in left if other != bit]
+
+
+def halved_sum(value, axis, dim, order):
+    left = list(reversed(range(bits_of(axis))))
+    shape = value.shape
+    value = value.reshape(shape[:dim] + (2,) * len(left) + shape[dim + 1 :])
+    steps = []
+    for bit in order:
+        total, left = halve(value, axis, dim, left, bit)
         value = total.astype(BF)
-    return lax.squeeze(total, (dim,))
+        steps.append(value)
+    return total, steps[0]
 
 
 def doubled_gather(value, axis):
@@ -168,7 +177,7 @@
     put_chunks(down, total)
 
 
-def across_grad_kernel(slots, width, state, partner, grad, terms):
+def across_grad_kernel(slots, width, state, partner, grad, after, terms):
     @pl.loop(0, slots, unroll=UNROLL)
     def _(j):
         both = jnp.concatenate([state[:, lanes(j, width)], partner[:, lanes(j, width)]], axis=1)
@@ -221,7 +230,7 @@
 
 def pair_grad_kernel(group, slots, width, *refs):
     count = len(group)
-    states, grads, terms = refs[:count], refs[count : 2 * count], refs[2 * count]
+    states, grads, terms = refs[:count], refs[count : 2 * count], refs[2 * count + 1]
     for at, level in enumerate(group):
 
         @pl.loop(0, slots // 2, unroll=UNROLL)
@@ -290,9 +299,13 @@
     def terms_of(count):
         return jax.ShapeDtypeStruct((count, 2, slots, width, width), BF)
 
-    def summed(result):
+    seq_bits = list(range(bits_of("seq")))
+    orders = [seq_bits, seq_bits[1:2] + seq_bits[:1] + seq_bits[2:]]
+    tp_bits = list(range(bits_of("tp")))
+
+    def summed(result, order):
         chunked = result.reshape(result.shape[:3] + (seq_size, width // seq_size, width))
-        return halved_sum(chunked, "seq", 3)
+        return halved_sum(chunked, "seq", 3, order)[0]
 
     row_state = rows_of(state_shape.shape, tile)
     row_model = chunk_rows_of(model_shape.shape, tile)
@@ -361,21 +374,23 @@
     )
     terms = [None] * levels
 
-    def across_terms(level, gradient):
+    anywhere = pl.BlockSpec(memory_space=pl.ANY)
+
+    def across_terms(level, gradient, after):
         (result,) = call(
             functools.partial(across_grad_kernel, slots, width),
             1,
-            [states[level], partners[level], gradient],
-            [whole(states[level]), whole(states[level]), whole(gradient)],
+            [states[level], partners[level], gradient, after],
+            [whole(states[level]), whole(states[level]), whole(gradient), anywhere],
             [terms_of(1)],
             [whole(terms_of(1))],
             2 * unit,
         )
-        return summed(result)[0]
+        return summed(result, orders[level % 2])[0]
 
     for level in range(last, local, -1):
         incoming = partner_2(send, "tp", level - local)
-        terms[level] = across_terms(level, grad)
+        terms[level] = across_terms(level, grad, send)
         grad, send = call(
             functools.partial(middle_kernel, slots, width),
             steps,
@@ -386,7 +401,7 @@
             2 * unit,
         )
     incoming = partner_2(send, "tp", 0)
-    terms[local] = across_terms(local, grad)
+    grad_above = grad
     *grads, spread = call(
         functools.partial(down_kernel, local, slots, width),
         steps,
@@ -405,24 +420,27 @@
         (2 * local + 3) * unit,
         [pltpu.VMEM((tile, model_width), F32)],
     )
-    spread_part = halved_sum(spread, "tp", 0)
+    spread_part, spread_first = halved_sum(spread, "tp", 0, tp_bits)
+    terms[local] = across_terms(local, grad_above, spread)
     grad_hidden = (cotangent.astype(F32) + spread_part).astype(BF)
     for top in range(local, 0, -2):
         group = list(range(max(top - 2, 0), top))
         (result,) = call(
             functools.partial(pair_grad_kernel, group, slots, width),
             1,
-            [states[level] for level in group] + [grads[level + 1] for level in group],
-            [whole(states[0])] * (2 * len(group)),
+            [states[level] for level in group]
+            + [grads[level + 1] for level in group]
+            + [spread_first],
+            [whole(states[0])] * (2 * len(group)) + [anywhere],
             [terms_of(len(group))],
             [whole(terms_of(len(group)))],
             2 * len(group) * unit,
         )
-        sums = summed(result)
+        sums = summed(result, orders[(local - top) // 2 % 2])
         for at, level in enumerate(group):
             terms[level] = sums[at]
 
-    down_sum = halved_sum(down_part, "tp", 0)
+    down_sum, _ = halved_sum(down_part, "tp", 0, tp_bits)
     layer_out = (hidden_in.astype(F32) + down_sum).astype(BF)
 
     grad_rows = lax.all_to_all(grad_hidden, "seq", split_axis=0, concat_axis=0, tiled=True)

time: 401 us -> 431 us (1.075)
  waiting for transfers between devices: 196 us -> 226 us
  local copies, waits for them, and re-layouts: 34.6 us -> 30.1 us
    ppermute x28, waiting for transfers between devices: 155 us -> 200 us  [partner_2(): return lax.ppermute(value, axis, pairs)]
    all_to_all x1, waiting for transfers between devices: 10.8 us -> 0.01 us  [per_device(): lax.all_to_all(moved_back, 'seq', split_axis=0, concat_axis=0, tiled=True)]
    dynamic_slice x8, local copies, waits for them, and re-layouts: 3.56 us -> 9.52 us  [the longest x4 6.85 us: halve(): keep = lax.dynamic_index_in_dim(value, mine, at, keepdims=False)]
    unnamed x68 -> x55, local copies, waits for them, and re-layouts: 12.8 us -> 7.28 us
  transfers between devices with their start and end apart: 32 -> 32, of which waited for: 17 -> 16; matrix products, arithmetic and copies ran while one was open for 12% -> 11% of each run, Pallas kernels for 14% -> 11%
where the time goes in v3:
time: 431 us; the launch traced here: 430 us
  waiting for transfers between devices  226 us (52%)
  Pallas kernels  88.6 us (21%)
  starting transfers between devices  45.5 us (11%)
  local copies, waits for them, and re-layouts  30.1 us (7%)
  other arithmetic  25.6 us (6%)
  matrix products  12.1 us (3%)
    ppermute x28, waiting for transfers between devices, partner_2(): return lax.ppermute(value, axis, pairs)  200 us
    pallas_call x9, Pallas kernels, call(): pl.pallas_call(kernel, grid=(steps,), in_specs=in_specs, out_specs=out_sp...  88.6 us
    ppermute x28, starting transfers between devices, partner_2(): return lax.ppermute(value, axis, pairs)  26.9 us
    all_to_all x1, waiting for transfers between devices, per_device(): lax.all_to_all(mixed_part, 'seq', split_axis=0, concat_axis=0, tiled=True)  13.1 us
    all_to_all x1, waiting for transfers between devices, per_device(): lax.all_to_all(first_out, 'seq', split_axis=0, concat_axis=0, tiled=True)  13.1 us
    dot_general x6, matrix products, dot(): lax.dot_general(left, right, (contract, ((), ())), preferred_element_type...  12.1 us
    convert_element_type x10, other arithmetic, halved_sum(): value = total.astype(BF)  11.4 us
  transfers between devices with their start and end apart: 32, of which 16 were waited for; matrix products, arithmetic and copies ran while one was open for 11% of the time, Pallas kernels for 11%

profile of v3, /device:TPU:0, one launch (start us, length us, event | category | flops | bytes accessed | tf_op | source)
XLA Modules:
  0.0 429.6 jit_solution(1638173745775649155)
XLA Ops:
  1.7 2.3 convolution_convert_fusion.3
  4.0 7.3 %all-to-all-start = ((bf16[8,64,512]{2,1,0:T(8,128)(2,1)}), bf16[8,64,512]{2,1,0:T(8,128)(2,1)}, u32[]{:S(2)}, u32[]{:S(2)}) async-start(bf16[8,64,512]{2,1,0:T(8,128)(2,1)} %bitcast.2), calls=%async_computation | async-start | bytes 1048576 | tf_op jit(solution)/shard_map/all_to_all | solution.py:323
  12.7 13.1 %all-to-all-done = bf16[8,64,512]{2,1,0:T(8,128)(2,1)} async-done(((bf16[8,64,512]{2,1,0:T(8,128)(2,1)}), bf16[8,64,512]{2,1,0:T(8,128)(2,1)}, u32[]{:S(2)}, u32[]{:S(2)}) %all-to-all-start) | async-done | bytes 524320 | tf_op jit(solution)/shard_map/all_to_all | solution.py:323
  25.8 2.3 convolution_convert_fusion.2
  28.1 3.6 all-to-all-start.1
  31.7 1.6 collective-permute-start.4
  33.3 13.1 %all-to-all-done.1 = bf16[8,64,512]{2,1,0:T(8,128)(2,1)S(1)} async-done(((bf16[8,64,512]{2,1,0:T(8,128)(2,1)}), bf16[8,64,512]{2,1,0:T(8,128)(2,1)S(1)}, u32[]{:S(2)}, u32[]{:S(2)}) %all-to-all-start.1) | async-done | bytes 524320 | tf_op jit(solution)/shard_map/all_to_all | solution.py:325
  46.6 1.6 collective-permute-start
  48.2 11.0 %collective-permute-done = bf16[512,512]{1,0:T(8,128)(2,1)} collective-permute-done((bf16[512,512]{1,0:T(8,128)(2,1)S(1)}, bf16[512,512]{1,0:T(8,128)(2,1)}, u32[]{:S(2)}, u32[]{:S(2)}) %collective-permute-start) | collective-permute-done | bytes 524320 | tf_op jit(solution)/shard_map/ppermute | solution.py:36
  59.1 2.3 select_bitcast_fusion.5
  63.2 2.3 collective-permute-done.1
  65.5 1.4 select_bitcast_fusion.3
  67.1 1.6 copy.36
  68.6 13.8 %shard_map.136 = (bf16[512,2048]{1,0:T(8,128)(2,1)}, bf16[512,2048]{1,0:T(8,128)(2,1)}, bf16[512,2048]{1,0:T(8,128)(2,1)}, bf16[512,2048]{1,0:T(8,128)(2,1)}, bf16[512,2048]{1,0:T(8,128)(2,1)}) custom-call(s32[16,2]{1,0:T(8,128)} %copy.39.pairs, bf16[4,512,512]{2,1,0:T(8,128)(2,1)} %bitcast.201, bf16[16,2,128,128]{3,2,1,0:T(8,128)(2,1)} %w_up.3, ...), custom_call_target="tpu_custom_call" | custom-call | flops 2684354560 | bytes 16777344 | tf_op jit(solution)/shard_map/pallas_call | solution.py:268
  82.7 4.2 collective-permute-done.2.partner
  86.9 1.4 copy-done.4
  88.3 5.4 %shard_map.137.state = bf16[512,2048]{1,0:T(8,128)(2,1)} custom-call(bf16[512,2048]{1,0:T(8,128)(2,1)} %get-tuple-element.21.state, bf16[512,2048]{1,0:T(8,128)(2,1)} %copy-done.4, bf16[6,16,128,128]{3,2,1,0:T(8,128)(2,1)} %refs_3_.3, bf16[6,16,128,128]{3,2,1,0:T(8,128)(2,1)} %refs_7_.3), custom_call_target="tpu_custom_call" | custom-call | flops 536870912 | bytes 12582912 | tf_op jit(solution)/shard_map/pallas_call | solution.py:268
  93.7 1.5 collective-permute-start.3
  95.5 2.6 collective-permute-done.5
  98.5 1.4 copy.38
  99.9 41.7 %collective-permute-done.3.partner = bf16[512,2048]{1,0:T(8,128)(2,1)S(1)} collective-permute-done((bf16[512,2048]{1,0:T(8,128)(2,1)}, bf16[512,2048]{1,0:T(8,128)(2,1)S(1)}, u32[]{:S(2)}, u32[]{:S(2)}) %collective-permute-start.3) | collective-permute-done | bytes 2097184 | tf_op jit(solution)/shard_map/ppermute | solution.py:36
  141.6 1.4 copy-done.5
  143.0 14.4 %shard_map.138 = (bf16[4,512,512]{2,1,0:T(8,128)(2,1)}, bf16[512,2048]{1,0:T(8,128)(2,1)}, bf16[512,2048]{1,0:T(8,128)(2,1)}) custom-call(s32[16,2]{1,0:T(8,128)} %copy.39.pairs, bf16[512,2048]{1,0:T(8,128)(2,1)} %shard_map.137.state, bf16[512,2048]{1,0:T(8,128)(2,1)} %copy-done.5, bf16[6,16,128,128]{3,2,1,0:T(8,128)(2,1)} %refs_3_.3, ...), custom_call_target="tpu_custom_call" | custom-call | flops 1879048192 | bytes 13631616 | tf_op jit(solution)/shard_map/pallas_call | solution.py:268
  157.4 1.6 collective-permute-start.8
  158.9 45.5 %collective-permute-done.8.incoming = bf16[512,2048]{1,0:T(8,128)(2,1)S(1)} collective-permute-done((bf16[512,2048]{1,0:T(8,128)(2,1)}, bf16[512,2048]{1,0:T(8,128)(2,1)S(1)}, u32[]{:S(2)}, u32[]{:S(2)}) %collective-permute-start.8) | collective-permute-done | bytes 2097184 | tf_op jit(solution)/shard_map/ppermute | solution.py:36
  204.5 1.4 copy-done.14
  205.9 6.6 %shard_map.139 = (bf16[512,2048]{1,0:T(8,128)(2,1)}, bf16[512,2048]{1,0:T(8,128)(2,1)}) custom-call(bf16[512,2048]{1,0:T(8,128)(2,1)} %get-tuple-element.23.grad, bf16[512,2048]{1,0:T(8,128)(2,1)} %copy-done.14, bf16[6,16,128,128]{3,2,1,0:T(8,128)(2,1)} %refs_3_.3, bf16[6,16,128,128]{3,2,1,0:T(8,128)(2,1)} %refs_7_.3), custom_call_target="tpu_custom_call" | custom-call | flops 536870912 | bytes 14680064 | tf_op jit(solution)/shard_map/pallas_call | solution.py:268
  214.0 6.7 %shard_map.144 = bf16[1,2,16,128,128]{4,3,2,1,0:T(8,128)(2,1)} custom-call(bf16[512,2048]{1,0:T(8,128)(2,1)} %shard_map.137.state, bf16[512,2048]{1,0:T(8,128)(2,1)} %copy-done.5, bf16[512,2048]{1,0:T(8,128)(2,1)} %get-tuple-element.23.grad, bf16[512,2048]{1,0:T(8,128)(2,1)} %get-tuple-element.24.after), custom_call_target="tpu_custom_call" | custom-call | flops 536870912 | bytes 9437184 | tf_op jit(solution)/shard_map/pallas_call | solution.py:268
  220.7 1.3 constant_dynamic-slice_fusion.1
  222.2 13.8 %collective-permute-done.25 = bf16[1,2,16,2,2,16,128]{6,5,2,1,3,4,0:T(8,128)(2,1)S(1)} collective-permute-done((bf16[1,2,16,2,2,16,128]{6,5,2,1,3,4,0:T(8,128)(2,1)S(1)}, bf16[1,2,16,2,2,16,128]{6,5,2,1,3,4,0:T(8,128)(2,1)S(1)}, u32[]{:S(2)}, u32[]{:S(2)}) %collective-permute-start.25) | collective-permute-done | bytes 524320 | tf_op jit(solution)/shard_map/ppermute | solution.py:36
  236.2 2.1 collective-permute-start.26
  238.3 1.8 fusion.3
  240.2 18.8 %shard_map.140 = (bf16[512,2048]{1,0:T(8,128)(2,1)}, bf16[512,2048]{1,0:T(8,128)(2,1)}, bf16[512,2048]{1,0:T(8,128)(2,1)}, bf16[512,2048]{1,0:T(8,128)(2,1)}, bf...) custom-call(s32[16,2]{1,0:T(8,128)} %copy.39.pairs, bf16[512,2048]{1,0:T(8,128)(2,1)} %get-tuple-element.25.grad, ...), custom_call_target="tpu_custom_call" | custom-call | flops 2952790016 | bytes 19923072 | tf_op jit(solution)/shard_map/pallas_call | solution.py:268
  259.0 2.3 dynamic-slice_bitcast_fusion
  262.1 1.5 collective-permute-start.7
  267.2 9.6 %collective-permute-done.7 = bf16[512,512]{1,0:T(8,128)(2,1)} collective-permute-done((bf16[512,512]{1,0:T(8,128)(2,1)}, bf16[512,512]{1,0:T(8,128)(2,1)}, u32[]{:S(2)}, u32[]{:S(2)}) %collective-permute-start.7) | collective-permute-done | bytes 524320 | tf_op jit(solution)/shard_map/ppermute | solution.py:36
  276.8 2.0 fusion.11
  278.8 7.0 %shard_map.143 = bf16[1,2,16,128,128]{4,3,2,1,0:T(8,128)(2,1)} custom-call(bf16[512,2048]{1,0:T(8,128)(2,1)} %get-tuple-element.21.state, bf16[512,2048]{1,0:T(8,128)(2,1)} %copy-done.4, bf16[512,2048]{1,0:T(8,128)(2,1)} %get-tuple-element.25.grad, bf16[4,512,512]{2,1,0:T(8,128)(2,1)} %get-tuple-element.27.after), custom_call_target="tpu_custom_call" | custom-call | flops 536870912 | bytes 9437184 | tf_op jit(solution)/shard_map/pallas_call | solution.py:268
  285.8 1.5 constant_dynamic-slice_fusion.3
  287.7 1.5 fusion.2.refs_4_
  289.3 1.6 collective-permute-start.11
  290.9 7.7 %shard_map.142 = bf16[2,2,16,128,128]{4,3,2,1,0:T(8,128)(2,1)} custom-call(bf16[512,2048]{1,0:T(8,128)(2,1)} %get-tuple-element.32.refs_0_, bf16[512,2048]{1,0:T(8,128)(2,1)} %get-tuple-element.33.refs_1_, bf16[512,2048]{1,0:T(8,128)(2,1)} %get-tuple-element.34.refs_2_, bf16[512,2048]{1,0:T(8,128)(2,1)} %get-tuple-element.35.refs_3_, ...), custom_call_target="tpu_custom_call" | custom-call | flops 1073741824 | bytes 10485760 | tf_op jit(solution)/shard_map/pallas_call | solution.py:268
  298.6 2.0 constant_dynamic-slice_fusion.5
  301.9 1.8 collective-permute-start.19
  303.8 8.1 %shard_map.141 = bf16[2,2,16,128,128]{4,3,2,1,0:T(8,128)(2,1)} custom-call(bf16[512,2048]{1,0:T(8,128)(2,1)} %get-tuple-element.28.refs_0_, bf16[512,2048]{1,0:T(8,128)(2,1)} %get-tuple-element.29.refs_1_, bf16[512,2048]{1,0:T(8,128)(2,1)} %get-tuple-element.30.refs_2_, bf16[512,2048]{1,0:T(8,128)(2,1)} %get-tuple-element.31.refs_3_, ...), custom_call_target="tpu_custom_call" | custom-call | flops 1073741824 | bytes 10485760 | tf_op jit(solution)/shard_map/pallas_call | solution.py:268
  312.0 2.0 constant_dynamic-slice_fusion.7
  316.3 1.8 collective-permute-start.23
  319.1 4.2 all-to-all-start.2
  323.2 28.3 %collective-permute-done.23 = bf16[1,2,16,2,16,128]{5,4,2,1,3,0:T(8,128)(2,1)} collective-permute-done((bf16[1,2,16,2,16,128]{5,4,2,1,3,0:T(8,128)(2,1)}, bf16[1,2,16,2,16,128]{5,4,2,1,3,0:T(8,128)(2,1)}, u32[]{:S(2)}, u32[]{:S(2)}) %collective-permute-start.23) | collective-permute-done | bytes 262176 | tf_op jit(solution)/shard_map/ppermute | solution.py:36
  354.6 1.5 fusion
  357.9 2.5 collective-permute-start.20
  360.4 1.5 fusion.1
  362.0 2.3 multiply_reduce_fusion
  367.6 2.4 convolution_convert_fusion.1
  369.9 3.5 all-to-all-start.3
  373.5 1.4 add_multiply_fusion
  374.9 8.2 %collective-permute-done.17 = bf16[2,2,16,2,16,128]{5,4,2,1,0,3:T(8,128)(2,1)} collective-permute-done((bf16[2,2,16,2,16,128]{5,4,2,1,0,3:T(8,128)(2,1)}, bf16[2,2,16,2,16,128]{5,4,2,1,0,3:T(8,128)(2,1)}, u32[]{:S(2)}, u32[]{:S(2)}) %collective-permute-start.17) | collective-permute-done | bytes 524320 | tf_op jit(solution)/shard_map/ppermute | solution.py:36
  383.1 1.3 fusion.7
  385.8 3.0 collective-permute-start.21
  388.8 17.3 %collective-permute-done.18 = bf16[2,2,16,16,128]{4,3,2,1,0:T(8,128)(2,1)S(1)} collective-permute-done((bf16[2,2,16,16,128]{4,3,2,1,0:T(8,128)(2,1)S(1)}, bf16[2,2,16,16,128]{4,3,2,1,0:T(8,128)(2,1)S(1)}, u32[]{:S(2)}, u32[]{:S(2)}) %collective-permute-start.18) | collective-permute-done | bytes 262176 | tf_op jit(solution)/shard_map/ppermute | solution.py:36
  406.2 4.5 %collective-permute-done.21 = bf16[2,2,16,16,128]{4,3,2,1,0:T(8,128)(2,1)S(1)} collective-permute-done((bf16[2,2,16,16,128]{4,3,2,1,0:T(8,128)(2,1)S(1)}, bf16[2,2,16,16,128]{4,3,2,1,0:T(8,128)(2,1)S(1)}, u32[]{:S(2)}, u32[]{:S(2)}) %collective-permute-start.21) | collective-permute-done | bytes 262176 | tf_op jit(solution)/shard_map/ppermute | solution.py:36
  412.5 1.7 collective-permute-done.12
  416.7 2.3 add_convert_fusion.1
  419.0 9.4 %collective-permute-done.13 = bf16[512,512]{1,0:T(8,128)(2,1)S(1)} collective-permute-done((bf16[512,512]{1,0:T(8,128)(2,1)S(1)}, bf16[512,512]{1,0:T(8,128)(2,1)S(1)}, u32[]{:S(2)}, u32[]{:S(2)}) %collective-permute-start.13) | collective-permute-done | bytes 524320 | tf_op jit(solution)/shard_map/ppermute | solution.py:36
  (128 shorter events, 31.5 us)
Async XLA Ops:
  0.6 1.0 copy-start
  0.6 10.7 %copy-start.23 = (bf16[64,8,8]{0,2,1:T(8,128)(2,1)S(1)}, bf16[64,8,8]{0,2,1:T(8,128)(2,1)}, u32[]{:S(2)}) copy-start(bf16[64,8,8]{0,2,1:T(8,128)(2,1)} %param.11) | copy-start | bytes 24580
  4.0 21.8 %all-to-all-start = ((bf16[8,64,512]{2,1,0:T(8,128)(2,1)}), bf16[8,64,512]{2,1,0:T(8,128)(2,1)}, u32[]{:S(2)}, u32[]{:S(2)}) async-start(bf16[8,64,512]{2,1,0:T(8,128)(2,1)} %bitcast.2), calls=%async_computation | async-start | bytes 1048576 | tf_op jit(solution)/shard_map/all_to_all | solution.py:323
  12.1 19.6 %copy-start.15 = (bf16[512,512]{1,0:T(8,128)(2,1)S(1)}, bf16[512,512]{1,0:T(8,128)(2,1)}, u32[]{:S(2)}) copy-start(bf16[512,512]{1,0:T(8,128)(2,1)} %param.17) | copy-start | bytes 1572868
  12.1 34.3 %copy-start.6 = (bf16[512,512]{1,0:T(8,128)(2,1)S(1)}, bf16[512,512]{1,0:T(8,128)(2,1)}, u32[]{:S(2)}) copy-start(bf16[512,512]{1,0:T(8,128)(2,1)} %param.9) | copy-start | bytes 1572868
  12.7 33.8 %copy-start.17 = (bf16[512,512]{1,0:T(8,128)(2,1)}, bf16[512,512]{1,0:T(8,128)(2,1)S(1)}, u32[]{:S(2)}) copy-start(bf16[512,512]{1,0:T(8,128)(2,1)S(1)} %mul.56) | copy-start | bytes 1572868
  28.1 18.3 %all-to-all-start.1 = ((bf16[8,64,512]{2,1,0:T(8,128)(2,1)}), bf16[8,64,512]{2,1,0:T(8,128)(2,1)S(1)}, u32[]{:S(2)}, u32[]{:S(2)}) async-start(bf16[8,64,512]{2,1,0:T(8,128)(2,1)} %bitcast.4), calls=%async_computation.1 | async-start | bytes 1048576 | tf_op jit(solution)/shard_map/all_to_all | solution.py:325
  31.7 16.4 %collective-permute-start.4 = (bf16[512,512]{1,0:T(8,128)(2,1)S(1)}, bf16[512,512]{1,0:T(8,128)(2,1)}, u32[]{:S(2)}, u32[]{:S(2)}) collective-permute-start(bf16[512,512]{1,0:T(8,128)(2,1)S(1)} %copy-done.15), channel_id=1, source_target_pairs={{0,2},{1,3},{2,0},{3,1},{4,6},{5,7},{6,4},{7,5},{8,10},{9,11},{10,... | collective-permute-start | bytes 1572872 | tf_op jit(solution)/shard_map/ppermute | solution.py:36
  46.6 14.9 %copy-start.7 = (bf16[512,512]{1,0:T(8,128)(2,1)}, bf16[512,512]{1,0:T(8,128)(2,1)S(1)}, u32[]{:S(2)}) copy-start(bf16[512,512]{1,0:T(8,128)(2,1)S(1)} %fusion.12) | copy-start | bytes 1572868
  46.6 12.6 %collective-permute-start = (bf16[512,512]{1,0:T(8,128)(2,1)S(1)}, bf16[512,512]{1,0:T(8,128)(2,1)}, u32[]{:S(2)}, u32[]{:S(2)}) collective-permute-start(bf16[512,512]{1,0:T(8,128)(2,1)S(1)} %fusion.12), channel_id=1, source_target_pairs={{0,2},{1,3},{2,0},{3,1},{4,6},{5,7},{6,4},{7,5},{8,10},{9,11},{10,... | collective-permute-start | bytes 1572872 | tf_op jit(solution)/shard_map/ppermute | solution.py:36
  61.4 1.1 copy-start.24
  62.5 3.0 collective-permute-start.1
  82.4 12.8 %copy-start.9 = (bf16[1,512,512]{2,1,0:T(8,128)(2,1)S(1)}, bf16[1,512,512]{2,1,0:T(8,128)(2,1)}, u32[]{:S(2)}) copy-start(bf16[1,512,512]{2,1,0:T(8,128)(2,1)} %get-tuple-element.50) | copy-start | bytes 1572868
  82.4 12.8 %copy-start.10 = (bf16[1,512,512]{2,1,0:T(8,128)(2,1)S(1)}, bf16[1,512,512]{2,1,0:T(8,128)(2,1)}, u32[]{:S(2)}) copy-start(bf16[1,512,512]{2,1,0:T(8,128)(2,1)} %get-tuple-element.51) | copy-start | bytes 1572868
  82.5 4.4 %collective-permute-start.2 = (bf16[512,2048]{1,0:T(8,128)(2,1)}, bf16[512,2048]{1,0:T(8,128)(2,1)S(1)}, u32[]{:S(2)}, u32[]{:S(2)}) collective-permute-start(bf16[512,2048]{1,0:T(8,128)(2,1)} %get-tuple-element.21.state), channel_id=1, source_target_pairs={{0,1},{1,0},{2,3},{3,2},{4,5},{5,4},{6,7},{7,6},{8,9},{9,8},{10,11... | collective-permute-start | bytes 6291464 | tf_op jit(solution)/shard_map/ppermute | solution.py:36
  86.9 1.4 copy-start.4
  93.7 47.9 %collective-permute-start.3 = (bf16[512,2048]{1,0:T(8,128)(2,1)}, bf16[512,2048]{1,0:T(8,128)(2,1)S(1)}, u32[]{:S(2)}, u32[]{:S(2)}) collective-permute-start(bf16[512,2048]{1,0:T(8,128)(2,1)} %shard_map.137.state), channel_id=1, source_target_pairs={{0,2},{1,3},{2,0},{3,1},{4,6},{5,7},{6,4},{7,5},{8,10},{9,11},{10,... | collective-permute-start | bytes 6291464 | tf_op jit(solution)/shard_map/ppermute | solution.py:36
  95.4 2.7 collective-permute-start.5
  141.6 1.4 copy-start.5
  157.4 47.1 %collective-permute-start.8 = (bf16[512,2048]{1,0:T(8,128)(2,1)}, bf16[512,2048]{1,0:T(8,128)(2,1)S(1)}, u32[]{:S(2)}, u32[]{:S(2)}) collective-permute-start(bf16[512,2048]{1,0:T(8,128)(2,1)} %get-tuple-element.24.after), channel_id=1, source_target_pairs={{0,2},{1,3},{2,0},{3,1},{4,6},{5,7},{6,4},{7,5},{8,10},{9,11},{10,... | collective-permute-start | bytes 6291464 | tf_op jit(solution)/shard_map/ppermute | solution.py:36
  204.5 1.4 copy-start.14
  205.9 6.6 %copy-start.20 = (bf16[4,512,512]{2,1,0:T(8,128)(2,1)S(1)}, bf16[4,512,512]{2,1,0:T(8,128)(2,1)}, u32[]{:S(2)}) copy-start(bf16[4,512,512]{2,1,0:T(8,128)(2,1)} %get-tuple-element.22) | copy-start | bytes 6291460
  212.4 27.7 %collective-permute-start.9 = (bf16[512,2048]{1,0:T(8,128)(2,1)}, bf16[512,2048]{1,0:T(8,128)(2,1)}, u32[]{:S(2)}, u32[]{:S(2)}) collective-permute-start(bf16[512,2048]{1,0:T(8,128)(2,1)} %get-tuple-element.26), channel_id=1, source_target_pairs={{0,1},{1,0},{2,3},{3,2},{4,5},{5,4},{6,7},{7,6},{8,9},{9,8},{10,11... | collective-permute-start | bytes 6291464 | tf_op jit(solution)/shard_map/ppermute | solution.py:36
  213.5 24.8 %collective-permute-start.6 = (bf16[2,512,512]{2,1,0:T(8,128)(2,1)}, bf16[2,512,512]{2,1,0:T(8,128)(2,1)}, u32[]{:S(2)}, u32[]{:S(2)}) collective-permute-start(bf16[2,512,512]{2,1,0:T(8,128)(2,1)} %dynamic-slice_bitcast_fusion.1), channel_id=1, source_target_pairs={{0,1},{1,0},{2,3},{3,2},{4,5},{5,4},{6,7},{7,6},{8,9},{9,8},{10,11... | collective-permute-start | bytes 3145736 | tf_op jit(solution)/shard_map/ppermute | solution.py:36
  222.1 13.9 %collective-permute-start.25 = (bf16[1,2,16,2,2,16,128]{6,5,2,1,3,4,0:T(8,128)(2,1)S(1)}, bf16[1,2,16,2,2,16,128]{6,5,2,1,3,4,0:T(8,128)(2,1)S(1)}, u32[]{:S(2)}, u32[]{:S(2)}) collective-permute-start(bf16[1,2,16,2,2,16,128]{6,5,2,1,3,4,0:T(8,128)(2,1)S(1)} %bitcast.209), channel_id=1, source_target_pairs={{0,8},{4,12},{8,0},{12,4},{16,24},{20,28},{24,16},{28,20},{1,9},{5... | collective-permute-start | bytes 1572872 | tf_op jit(solution)/shard_map/ppermute | solution.py:36
  236.2 28.1 %collective-permute-start.26 = (bf16[1,2,16,2,16,128]{5,4,2,1,3,0:T(8,128)(2,1)S(1)}, bf16[1,2,16,2,16,128]{5,4,2,1,3,0:T(8,128)(2,1)}, u32[]{:S(2)}, u32[]{:S(2)}) collective-permute-start(bf16[1,2,16,2,16,128]{5,4,2,1,3,0:T(8,128)(2,1)S(1)} %dynamic-slice_bitcast_fusion.6), channel_id=1, source_target_pairs={{0,4},{4,0},{8,12},{12,8},{16,20},{20,16},{24,28},{28,24},{1,5},{5... | collective-permute-start | bytes 786440 | tf_op jit(solution)/shard_map/ppermute | solution.py:36
  259.0 17.8 %copy-start.8 = (bf16[512,512]{1,0:T(8,128)(2,1)S(1)}, bf16[512,512]{1,0:T(8,128)(2,1)}, u32[]{:S(2)}) copy-start(bf16[512,512]{1,0:T(8,128)(2,1)} %copy-done.7) | copy-start | bytes 1572868
  261.3 26.2 %collective-permute-start.10 = (bf16[2,512,512]{2,1,0:T(8,128)(2,1)}, bf16[2,512,512]{2,1,0:T(8,128)(2,1)}, u32[]{:S(2)}, u32[]{:S(2)}) collective-permute-start(bf16[2,512,512]{2,1,0:T(8,128)(2,1)} %dynamic-slice_bitcast_fusion), channel_id=1, source_target_pairs={{0,1},{1,0},{2,3},{3,2},{4,5},{5,4},{6,7},{7,6},{8,9},{9,8},{10,11... | collective-permute-start | bytes 3145736 | tf_op jit(solution)/shard_map/ppermute | solution.py:36
  262.1 14.7 %collective-permute-start.7 = (bf16[512,512]{1,0:T(8,128)(2,1)}, bf16[512,512]{1,0:T(8,128)(2,1)}, u32[]{:S(2)}, u32[]{:S(2)}) collective-permute-start(bf16[512,512]{1,0:T(8,128)(2,1)} %dynamic-slice_bitcast_fusion.5), channel_id=1, source_target_pairs={{0,2},{1,3},{2,0},{3,1},{4,6},{5,7},{6,4},{7,5},{8,10},{9,11},{10,... | collective-permute-start | bytes 1572872 | tf_op jit(solution)/shard_map/ppermute | solution.py:36
  266.0 146.4 %collective-permute-start.27 = (bf16[1,2,16,16,128]{4,3,2,1,0:T(8,128)(2,1)}, bf16[1,2,16,16,128]{4,3,2,1,0:T(8,128)(2,1)S(1)}, u32[]{:S(2)}, u32[]{:S(2)}) collective-permute-start(bf16[1,2,16,16,128]{4,3,2,1,0:T(8,128)(2,1)} %dynamic-slice_bitcast_fusion.10), channel_id=1, source_target_pairs={{0,16},{4,20},{8,24},{12,28},{16,0},{20,4},{24,8},{28,12},{1,17},{... | collective-permute-start | bytes 393224 | tf_op jit(solution)/shard_map/ppermute | solution.py:36
  285.8 1.9 copy-start.3
  287.4 16.3 %collective-permute-start.22 = (bf16[1,2,16,2,2,16,128]{6,5,2,1,3,4,0:T(8,128)(2,1)S(1)}, bf16[1,2,16,2,2,16,128]{6,5,2,1,3,4,0:T(8,128)(2,1)S(1)}, u32[]{:S(2)}, u32[]{:S(2)}) collective-permute-start(bf16[1,2,16,2,2,16,128]{6,5,2,1,3,4,0:T(8,128)(2,1)S(1)} %bitcast.210), channel_id=1, source_target_pairs={{0,4},{4,0},{8,12},{12,8},{16,20},{20,16},{24,28},{28,24},{1,5},{5... | collective-permute-start | bytes 1572872 | tf_op jit(solution)/shard_map/ppermute | solution.py:36
  289.2 1.7 copy-start.1
  289.3 28.8 %collective-permute-start.11 = (bf16[512,512]{1,0:T(8,128)(2,1)S(1)}, bf16[512,512]{1,0:T(8,128)(2,1)S(1)}, u32[]{:S(2)}, u32[]{:S(2)}) collective-permute-start(bf16[512,512]{1,0:T(8,128)(2,1)S(1)} %dynamic-slice_bitcast_fusion.4), channel_id=1, source_target_pairs={{0,2},{1,3},{2,0},{3,1},{4,6},{5,7},{6,4},{7,5},{8,10},{9,11},{10,... | collective-permute-start | bytes 1572872 | tf_op jit(solution)/shard_map/ppermute | solution.py:36
  301.9 52.7 %collective-permute-start.19 = (bf16[2,2,16,2,2,16,128]{6,5,2,1,0,3,4:T(8,128)(2,1)}, bf16[2,2,16,2,2,16,128]{6,5,2,1,0,3,4:T(8,128)(2,1)}, u32[]{:S(2)}, u32[]{:S(2)}) collective-permute-start(bf16[2,2,16,2,2,16,128]{6,5,2,1,0,3,4:T(8,128)(2,1)} %bitcast.192), channel_id=1, source_target_pairs={{0,4},{4,0},{8,12},{12,8},{16,20},{20,16},{24,28},{28,24},{1,5},{5... | collective-permute-start | bytes 3145736 | tf_op jit(solution)/shard_map/ppermute | solution.py:36
  303.8 11.8 %copy-start.19 = (bf16[1,2,16,2,2,16,128]{6,5,2,1,3,4,0:T(8,128)(2,1)}, bf16[1,2,16,2,2,16,128]{6,5,2,1,3,4,0:T(8,128)(2,1)S(1)}, u32[]{:S(2)}) copy-start(bf16[1,2,16,2,2,16,128]{6,5,2,1,3,4,0:T(8,128)(2,1)S(1)} %fusion.5) | copy-start | bytes 1572868
  314.0 4.1 copy-start.2
  314.0 4.1 copy-start.16
  315.3 45.1 %collective-permute-start.16 = (bf16[2,2,16,2,2,16,128]{6,5,2,1,0,3,4:T(8,128)(2,1)}, bf16[2,2,16,2,2,16,128]{6,5,2,1,0,3,4:T(8,128)(2,1)}, u32[]{:S(2)}, u32[]{:S(2)}) collective-permute-start(bf16[2,2,16,2,2,16,128]{6,5,2,1,0,3,4:T(8,128)(2,1)} %bitcast.193), channel_id=1, source_target_pairs={{0,8},{4,12},{8,0},{12,4},{16,24},{20,28},{24,16},{28,20},{1,9},{5... | collective-permute-start | bytes 3145736 | tf_op jit(solution)/shard_map/ppermute | solution.py:36
  316.3 35.2 %collective-permute-start.23 = (bf16[1,2,16,2,16,128]{5,4,2,1,3,0:T(8,128)(2,1)}, bf16[1,2,16,2,16,128]{5,4,2,1,3,0:T(8,128)(2,1)}, u32[]{:S(2)}, u32[]{:S(2)}) collective-permute-start(bf16[1,2,16,2,16,128]{5,4,2,1,3,0:T(8,128)(2,1)} %dynamic-slice_bitcast_fusion.7), channel_id=1, source_target_pairs={{0,8},{4,12},{8,0},{12,4},{16,24},{20,28},{24,16},{28,20},{1,9},{5... | collective-permute-start | bytes 786440 | tf_op jit(solution)/shard_map/ppermute | solution.py:36
  319.1 42.9 %all-to-all-start.2 = ((bf16[8,64,512]{2,1,0:T(8,128)(2,1)}), bf16[8,64,512]{2,1,0:T(8,128)(2,1)}, u32[]{:S(2)}, u32[]{:S(2)}) async-start(bf16[8,64,512]{2,1,0:T(8,128)(2,1)} %bitcast.26), calls=%async_computation.2 | async-start | bytes 1048576 | tf_op jit(solution)/shard_map/all_to_all | solution.py:446
  352.6 1.9 copy-start.21
  353.4 57.5 %collective-permute-start.24 = (bf16[1,2,16,16,128]{4,3,2,1,0:T(8,128)(2,1)}, bf16[1,2,16,16,128]{4,3,2,1,0:T(8,128)(2,1)}, u32[]{:S(2)}, u32[]{:S(2)}) collective-permute-start(bf16[1,2,16,16,128]{4,3,2,1,0:T(8,128)(2,1)} %dynamic-slice_bitcast_fusion.11), channel_id=1, source_target_pairs={{0,16},{4,20},{8,24},{12,28},{16,0},{20,4},{24,8},{28,12},{1,17},{... | collective-permute-start | bytes 393224 | tf_op jit(solution)/shard_map/ppermute | solution.py:36
  356.1 1.0 copy-start.11
  357.9 26.6 %collective-permute-start.20 = (bf16[2,2,16,2,16,128]{5,4,2,1,0,3:T(8,128)(2,1)}, bf16[2,2,16,2,16,128]{5,4,2,1,0,3:T(8,128)(2,1)}, u32[]{:S(2)}, u32[]{:S(2)}) collective-permute-start(bf16[2,2,16,2,16,128]{5,4,2,1,0,3:T(8,128)(2,1)} %dynamic-slice_bitcast_fusion.2), channel_id=1, source_target_pairs={{0,8},{4,12},{8,0},{12,4},{16,24},{20,28},{24,16},{28,20},{1,9},{5... | collective-permute-start | bytes 1572872 | tf_op jit(solution)/shard_map/ppermute | solution.py:36
  362.0 4.5 %copy-start.13 = (bf16[2,2,16,2,2,16,128]{6,5,2,1,0,3,4:T(8,128)(2,1)}, bf16[2,2,16,2,2,16,128]{6,5,2,1,0,3,4:T(8,128)(2,1)S(1)}, u32[]{:S(2)}) copy-start(bf16[2,2,16,2,2,16,128]{6,5,2,1,0,3,4:T(8,128)(2,1)S(1)} %fusion.1) | copy-start | bytes 3145732
  362.0 5.6 %copy-start.18 = (bf16[512,512]{1,0:T(8,128)(2,1)S(1)}, bf16[512,512]{1,0:T(8,128)(2,1)}, u32[]{:S(2)}) copy-start(bf16[512,512]{1,0:T(8,128)(2,1)} %copy-done.17) | copy-start | bytes 1572868
  364.3 1.5 collective-permute-start.14
  365.3 17.8 %collective-permute-start.17 = (bf16[2,2,16,2,16,128]{5,4,2,1,0,3:T(8,128)(2,1)}, bf16[2,2,16,2,16,128]{5,4,2,1,0,3:T(8,128)(2,1)}, u32[]{:S(2)}, u32[]{:S(2)}) collective-permute-start(bf16[2,2,16,2,16,128]{5,4,2,1,0,3:T(8,128)(2,1)} %dynamic-slice_bitcast_fusion.3), channel_id=1, source_target_pairs={{0,4},{4,0},{8,12},{12,8},{16,20},{20,16},{24,28},{28,24},{1,5},{5... | collective-permute-start | bytes 1572872 | tf_op jit(solution)/shard_map/ppermute | solution.py:36
  366.4 7.0 %collective-permute-start.15 = (f32[64,8,8]{0,2,1:T(8,128)}, f32[64,8,8]{0,2,1:T(8,128)}, u32[]{:S(2)}, u32[]{:S(2)}) collective-permute-start(f32[64,8,8]{0,2,1:T(8,128)} %bitcast_add_fusion), channel_id=1, source_target_pairs={{0,2},{1,3},{2,0},{3,1},{4,6},{5,7},{6,4},{7,5},{8,10},{9,11},{10,... | collective-permute-start | bytes 49160 | tf_op jit(solution)/shard_map/ppermute | solution.py:36
  367.5 17.0 %copy-start.12 = (bf16[2,2,16,2,2,16,128]{6,5,2,1,0,3,4:T(8,128)(2,1)S(1)}, bf16[2,2,16,2,2,16,128]{6,5,2,1,0,3,4:T(8,128)(2,1)}, u32[]{:S(2)}) copy-start(bf16[2,2,16,2,2,16,128]{6,5,2,1,0,3,4:T(8,128)(2,1)} %copy-done.11) | copy-start | bytes 3145732
  369.9 41.9 %all-to-all-start.3 = ((bf16[8,64,512]{2,1,0:T(8,128)(2,1)}), bf16[8,64,512]{2,1,0:T(8,128)(2,1)S(1)}, u32[]{:S(2)}, u32[]{:S(2)}) async-start(bf16[8,64,512]{2,1,0:T(8,128)(2,1)} %bitcast.208), calls=%async_computation.3 | async-start | bytes 1048576 | tf_op jit(solution)/shard_map/all_to_all | solution.py:448
  384.5 21.6 %collective-permute-start.18 = (bf16[2,2,16,16,128]{4,3,2,1,0:T(8,128)(2,1)S(1)}, bf16[2,2,16,16,128]{4,3,2,1,0:T(8,128)(2,1)S(1)}, u32[]{:S(2)}, u32[]{:S(2)}) collective-permute-start(bf16[2,2,16,16,128]{4,3,2,1,0:T(8,128)(2,1)S(1)} %dynamic-slice_bitcast_fusion.9), channel_id=1, source_target_pairs={{0,16},{4,20},{8,24},{12,28},{16,0},{20,4},{24,8},{28,12},{1,17},{... | collective-permute-start | bytes 786440 | tf_op jit(solution)/shard_map/ppermute | solution.py:36
  385.8 25.1 %copy-start.22 = (bf16[1,2,16,2,16,128]{5,4,2,1,3,0:T(8,128)(2,1)S(1)}, bf16[1,2,16,2,16,128]{5,4,2,1,3,0:T(8,128)(2,1)}, u32[]{:S(2)}) copy-start(bf16[1,2,16,2,16,128]{5,4,2,1,3,0:T(8,128)(2,1)} %copy-done.21) | copy-start | bytes 786436
  385.8 24.9 %collective-permute-start.21 = (bf16[2,2,16,16,128]{4,3,2,1,0:T(8,128)(2,1)S(1)}, bf16[2,2,16,16,128]{4,3,2,1,0:T(8,128)(2,1)S(1)}, u32[]{:S(2)}, u32[]{:S(2)}) collective-permute-start(bf16[2,2,16,16,128]{4,3,2,1,0:T(8,128)(2,1)S(1)} %dynamic-slice_bitcast_fusion.8), channel_id=1, source_target_pairs={{0,16},{4,20},{8,24},{12,28},{16,0},{20,4},{24,8},{28,12},{1,17},{... | collective-permute-start | bytes 786440 | tf_op jit(solution)/shard_map/ppermute | solution.py:36
  412.3 2.0 collective-permute-start.12
  414.4 14.0 %collective-permute-start.13 = (bf16[512,512]{1,0:T(8,128)(2,1)S(1)}, bf16[512,512]{1,0:T(8,128)(2,1)S(1)}, u32[]{:S(2)}, u32[]{:S(2)}) collective-permute-start(bf16[512,512]{1,0:T(8,128)(2,1)S(1)} %add_convert_fusion), channel_id=1, source_target_pairs={{0,2},{1,3},{2,0},{3,1},{4,6},{5,7},{6,4},{7,5},{8,10},{9,11},{10,... | collective-permute-start | bytes 1572872 | tf_op jit(solution)/shard_map/ppermute | solution.py:36

commit v4 on v3

--- a/solution.py
+++ b/solution.py
@@ -44,25 +44,44 @@
     return lax.axis_size(axis).bit_length() - 1
 
 
+def nothing(value, tie, out):
+    pass
+
+
+def hold(value, tie):
+    anywhere = pl.BlockSpec(memory_space=pl.ANY)
+    return pl.pallas_call(
+        nothing,
+        out_shape=jax.ShapeDtypeStruct(value.shape, value.dtype),
+        in_specs=[anywhere, anywhere],
+        out_specs=anywhere,
+        input_output_aliases={0: 0},
+    )(value, tie)
+
+
 def halve(value, axis, dim, left, bit):
     at = dim + left.index(bit)
     mine = bit_of(axis, bit)
     keep = lax.dynamic_index_in_dim(value, mine, at, keepdims=False)
     give = lax.dynamic_index_in_dim(value, 1 - mine, at, keepdims=False)
     total = keep.astype(F32) + partner_2(give, axis, bit).astype(F32)
-    return total, [other for other in left if other != bit]
-
-
-def halved_sum(value, axis, dim, order):
+    return total, [other for other in left if other != bit], give
+
+
+def halved_sum(value, axis, dim, order, ties=()):
     left = list(reversed(range(bits_of(axis))))
     shape = value.shape
     value = value.reshape(shape[:dim] + (2,) * len(left) + shape[dim + 1 :])
-    steps = []
-    for bit in order:
-        total, left = halve(value, axis, dim, left, bit)
+    sent = []
+    firsts = None
+    for step, bit in enumerate(order):
+        if step < len(ties) and ties[step] is not None:
+            value = hold(value, ties[step])
+        total, left, give = halve(value, axis, dim, left, bit)
         value = total.astype(BF)
-        steps.append(value)
-    return total, steps[0]
+        firsts = value if step == 0 else firsts
+        sent.append(give)
+    return total, (sent[0], firsts)
 
 
 def doubled_gather(value, axis):
@@ -186,7 +205,7 @@
         terms[0, 1, j] = result[width:]
 
 
-def middle_kernel(slots, width, grad, incoming, w_self, w_cross_below, out, send):
+def middle_kernel(slots, width, grad, incoming, w_self, w_cross_below, after, out, send):
     @pl.loop(0, slots, unroll=UNROLL)
     def _(j):
         own = dot_nt(grad[:, lanes(j, width)], w_self[0, j])
@@ -303,9 +322,9 @@
     orders = [seq_bits, seq_bits[1:2] + seq_bits[:1] + seq_bits[2:]]
     tp_bits = list(range(bits_of("tp")))
 
-    def summed(result, order):
+    def summed(result, order, ties=()):
         chunked = result.reshape(result.shape[:3] + (seq_size, width // seq_size, width))
-        return halved_sum(chunked, "seq", 3, order)[0]
+        return halved_sum(chunked, "seq", 3, order, ties)[0]
 
     row_state = rows_of(state_shape.shape, tile)
     row_model = chunk_rows_of(model_shape.shape, tile)
@@ -386,16 +405,23 @@
             [whole(terms_of(1))],
             2 * unit,
         )
-        return summed(result, orders[level % 2])[0]
+        return result
 
     for level in range(last, local, -1):
         incoming = partner_2(send, "tp", level - local)
-        terms[level] = across_terms(level, grad, send)
+        result = across_terms(level, grad, send)
+        terms[level] = summed(result, orders[level % 2])[0]
         grad, send = call(
             functools.partial(middle_kernel, slots, width),
             steps,
-            [grad, incoming, w_self, w_cross],
-            [row_state, row_state, level_of(w_self, level), level_of(w_cross, level - 1)],
+            [grad, incoming, w_self, w_cross, result],
+            [
+                row_state,
+                row_state,
+                level_of(w_self, level),
+                level_of(w_cross, level - 1),
+                anywhere,
+            ],
             [state_shape, state_shape],
             [row_state, row_state],
             2 * unit,
@@ -420,9 +446,17 @@
         (2 * local + 3) * unit,
         [pltpu.VMEM((tile, model_width), F32)],
     )
-    spread_part, spread_first = halved_sum(spread, "tp", 0, tp_bits)
-    terms[local] = across_terms(local, grad_above, spread)
+    spread_part, (spread_sent, spread_first) = halved_sum(spread, "tp", 0, tp_bits)
     grad_hidden = (cotangent.astype(F32) + spread_part).astype(BF)
+    down_sum, _ = halved_sum(down_part, "tp", 0, tp_bits)
+    layer_out = (hidden_in.astype(F32) + down_sum).astype(BF)
+
+    grad_rows = lax.all_to_all(grad_hidden, "seq", split_axis=0, concat_axis=0, tiled=True)
+    moved_back = dot_tn(mixer, grad_rows).astype(BF)
+    returned = lax.all_to_all(moved_back, "seq", split_axis=0, concat_axis=0, tiled=True)
+    ties = [None, grad_rows, returned]
+    result = across_terms(local, grad_above, spread_sent)
+    terms[local] = summed(result, orders[local % 2], ties)[0]
     for top in range(local, 0, -2):
         group = list(range(max(top - 2, 0), top))
         (result,) = call(
@@ -436,16 +470,10 @@
             [whole(terms_of(len(group)))],
             2 * len(group) * unit,
         )
-        sums = summed(result, orders[(local - top) // 2 % 2])
+        sums = summed(result, orders[(local - top) // 2 % 2], ties)
         for at, level in enumerate(group):
             terms[level] = sums[at]
 
-    down_sum, _ = halved_sum(down_part, "tp", 0, tp_bits)
-    layer_out = (hidden_in.astype(F32) + down_sum).astype(BF)
-
-    grad_rows = lax.all_to_all(grad_hidden, "seq", split_axis=0, concat_axis=0, tiled=True)
-    moved_back = dot_tn(mixer, grad_rows).astype(BF)
-    returned = lax.all_to_all(moved_back, "seq", split_axis=0, concat_axis=0, tiled=True)
     cross_rows = dot_nt(grad_rows, first_rows).reshape(groups, positions, groups, positions)
     second_part = jnp.sum(cross_rows * same.astype(F32)[None, :, None, :], axis=3).transpose(1, 0, 2)
     first_part = dot_nt(returned, tokens).astype(BF)

time: 431 us -> 407 us (0.944)
  waiting for transfers between devices: 226 us -> 199 us
  other arithmetic: 25.6 us -> 30 us
    ppermute x28, waiting for transfers between devices: 200 us -> 173 us  [partner_2(): return lax.ppermute(value, axis, pairs)]
    squeeze x12 -> x15, local copies, waits for them, and re-layouts: 8.12 us -> 19.1 us  [halve(): give = lax.dynamic_index_in_dim(value, 1 - mine, at, keepdims=False)]
    dynamic_slice x4 -> x1, local copies, waits for them, and re-layouts: 6.85 us -> 0.17 us  [halve(): keep = lax.dynamic_index_in_dim(value, mine, at, keepdims=False)]
    convert_element_type x10, other arithmetic: 11.4 us -> 15.8 us  [halved_sum(): value = total.astype(BF)]
  transfers between devices with their start and end apart: 32 -> 32, of which waited for: 16 -> 18; matrix products, arithmetic and copies ran while one was open for 11% -> 14% of each run, Pallas kernels for 11% -> 12%
where the time goes in v4:
time: 407 us; the launch traced here: 406 us
  waiting for transfers between devices  199 us (49%)
  Pallas kernels  88 us (22%)
  starting transfers between devices  44.7 us (11%)
  local copies, waits for them, and re-layouts  31.9 us (8%)
  other arithmetic  30 us (7%)
  matrix products  11.1 us (3%)
    ppermute x28, waiting for transfers between devices, partner_2(): return lax.ppermute(value, axis, pairs)  173 us
    pallas_call x9, Pallas kernels, call(): pl.pallas_call(kernel, grid=(steps,), in_specs=in_specs, out_specs=out_sp...  88 us
    ppermute x28, starting transfers between devices, partner_2(): return lax.ppermute(value, axis, pairs)  26.7 us
    squeeze x15, local copies, waits for them, and re-layouts, halve(): give = lax.dynamic_index_in_dim(value, 1 - mine, at, keepdims=False)  19.1 us
    convert_element_type x10, other arithmetic, halved_sum(): value = total.astype(BF)  15.8 us
    all_to_all x1, waiting for transfers between devices, per_device(): lax.all_to_all(mixed_part, 'seq', split_axis=0, concat_axis=0, tiled=True)  13.1 us
    all_to_all x1, waiting for transfers between devices, per_device(): lax.all_to_all(first_out, 'seq', split_axis=0, concat_axis=0, tiled=True)  13.1 us
    dot_general x6, matrix products, dot(): lax.dot_general(left, right, (contract, ((), ())), preferred_element_type...  11.1 us
  transfers between devices with their start and end apart: 32, of which 18 were waited for; matrix products, arithmetic and copies ran while one was open for 14% of the time, Pallas kernels for 12%

profile of v4, /device:TPU:0, one launch (start us, length us, event | category | flops | bytes accessed | tf_op | source)
XLA Modules:
  0.0 406.0 jit_solution(4882154057792091917)
XLA Ops:
  1.7 2.3 convolution_convert_fusion.3
  4.0 7.3 %all-to-all-start = ((bf16[8,64,512]{2,1,0:T(8,128)(2,1)}), bf16[8,64,512]{2,1,0:T(8,128)(2,1)}, u32[]{:S(2)}, u32[]{:S(2)}) async-start(bf16[8,64,512]{2,1,0:T(8,128)(2,1)} %bitcast.2), calls=%async_computation | async-start | bytes 1048576 | tf_op jit(solution)/shard_map/all_to_all | solution.py:342
  12.7 13.1 %all-to-all-done = bf16[8,64,512]{2,1,0:T(8,128)(2,1)} async-done(((bf16[8,64,512]{2,1,0:T(8,128)(2,1)}), bf16[8,64,512]{2,1,0:T(8,128)(2,1)}, u32[]{:S(2)}, u32[]{:S(2)}) %all-to-all-start) | async-done | bytes 524320 | tf_op jit(solution)/shard_map/all_to_all | solution.py:342
  25.8 2.3 convolution_convert_fusion.2
  28.1 3.6 all-to-all-start.1
  31.7 1.6 collective-permute-start.4
  33.3 13.1 %all-to-all-done.1 = bf16[8,64,512]{2,1,0:T(8,128)(2,1)S(1)} async-done(((bf16[8,64,512]{2,1,0:T(8,128)(2,1)}), bf16[8,64,512]{2,1,0:T(8,128)(2,1)S(1)}, u32[]{:S(2)}, u32[]{:S(2)}) %all-to-all-start.1) | async-done | bytes 524320 | tf_op jit(solution)/shard_map/all_to_all | solution.py:344
  46.6 1.6 collective-permute-start
  48.1 11.0 %collective-permute-done = bf16[512,512]{1,0:T(8,128)(2,1)} collective-permute-done((bf16[512,512]{1,0:T(8,128)(2,1)S(1)}, bf16[512,512]{1,0:T(8,128)(2,1)}, u32[]{:S(2)}, u32[]{:S(2)}) %collective-permute-start) | collective-permute-done | bytes 524320 | tf_op jit(solution)/shard_map/ppermute | solution.py:36
  59.1 1.5 select_bitcast_fusion.5
  63.2 2.3 collective-permute-done.1
  65.5 1.5 select_bitcast_fusion.3
  67.2 1.6 copy.37
  68.7 13.9 %shard_map.136 = (bf16[512,2048]{1,0:T(8,128)(2,1)}, bf16[512,2048]{1,0:T(8,128)(2,1)}, bf16[512,2048]{1,0:T(8,128)(2,1)}, bf16[512,2048]{1,0:T(8,128)(2,1)}, bf16[512,2048]{1,0:T(8,128)(2,1)}) custom-call(s32[16,2]{1,0:T(8,128)} %copy.40.pairs, bf16[4,512,512]{2,1,0:T(8,128)(2,1)} %bitcast.214, bf16[16,2,128,128]{3,2,1,0:T(8,128)(2,1)} %w_up.3, ...), custom_call_target="tpu_custom_call" | custom-call | flops 2684354560 | bytes 16777344 | tf_op jit(solution)/shard_map/pallas_call | solution.py:287
  82.7 4.2 %collective-permute-done.2.partner = bf16[512,2048]{1,0:T(8,128)(2,1)S(1)} collective-permute-done((bf16[512,2048]{1,0:T(8,128)(2,1)}, bf16[512,2048]{1,0:T(8,128)(2,1)S(1)}, u32[]{:S(2)}, u32[]{:S(2)}) %collective-permute-start.2) | collective-permute-done | bytes 2097184 | tf_op jit(solution)/shard_map/ppermute | solution.py:36
  88.4 5.4 %shard_map.137.state = bf16[512,2048]{1,0:T(8,128)(2,1)} custom-call(bf16[512,2048]{1,0:T(8,128)(2,1)} %get-tuple-element.21.state, bf16[512,2048]{1,0:T(8,128)(2,1)} %copy-done.11, bf16[6,16,128,128]{3,2,1,0:T(8,128)(2,1)} %refs_3_.3, bf16[6,16,128,128]{3,2,1,0:T(8,128)(2,1)} %refs_7_.3), custom_call_target="tpu_custom_call" | custom-call | flops 536870912 | bytes 12582912 | tf_op jit(solution)/shard_map/pallas_call | solution.py:287
  93.8 1.5 collective-permute-start.3
  95.5 2.6 collective-permute-done.5
  98.5 1.5 copy.39
  100.0 41.6 %collective-permute-done.3.partner = bf16[512,2048]{1,0:T(8,128)(2,1)S(1)} collective-permute-done((bf16[512,2048]{1,0:T(8,128)(2,1)}, bf16[512,2048]{1,0:T(8,128)(2,1)S(1)}, u32[]{:S(2)}, u32[]{:S(2)}) %collective-permute-start.3) | collective-permute-done | bytes 2097184 | tf_op jit(solution)/shard_map/ppermute | solution.py:36
  143.0 14.3 %shard_map.138 = (bf16[4,512,512]{2,1,0:T(8,128)(2,1)}, bf16[512,2048]{1,0:T(8,128)(2,1)}, bf16[512,2048]{1,0:T(8,128)(2,1)}) custom-call(s32[16,2]{1,0:T(8,128)} %copy.40.pairs, bf16[512,2048]{1,0:T(8,128)(2,1)} %shard_map.137.state, bf16[512,2048]{1,0:T(8,128)(2,1)} %copy-done.12, bf16[6,16,128,128]{3,2,1,0:T(8,128)(2,1)} %refs_3_.3, ...), custom_call_target="tpu_custom_call" | custom-call | flops 1879048192 | bytes 13631616 | tf_op jit(solution)/shard_map/pallas_call | solution.py:287
  157.3 1.5 collective-permute-start.8
  158.8 6.7 %shard_map.139.after = bf16[1,2,16,128,128]{4,3,2,1,0:T(8,128)(2,1)} custom-call(bf16[512,2048]{1,0:T(8,128)(2,1)} %shard_map.137.state, bf16[512,2048]{1,0:T(8,128)(2,1)} %copy-done.12, bf16[512,2048]{1,0:T(8,128)(2,1)} %get-tuple-element.23.grad, bf16[512,2048]{1,0:T(8,128)(2,1)} %get-tuple-element.24.after), custom_call_target="tpu_custom_call" | custom-call | flops 536870912 | bytes 9437184 | tf_op jit(solution)/shard_map/pallas_call | solution.py:287
  165.6 38.8 %collective-permute-done.8.incoming = bf16[512,2048]{1,0:T(8,128)(2,1)S(1)} collective-permute-done((bf16[512,2048]{1,0:T(8,128)(2,1)}, bf16[512,2048]{1,0:T(8,128)(2,1)S(1)}, u32[]{:S(2)}, u32[]{:S(2)}) %collective-permute-start.8) | collective-permute-done | bytes 2097184 | tf_op jit(solution)/shard_map/ppermute | solution.py:36
  205.7 6.4 %shard_map.140 = (bf16[512,2048]{1,0:T(8,128)(2,1)}, bf16[512,2048]{1,0:T(8,128)(2,1)}) custom-call(bf16[512,2048]{1,0:T(8,128)(2,1)} %get-tuple-element.23.grad, bf16[512,2048]{1,0:T(8,128)(2,1)} %copy-done.25, bf16[6,16,128,128]{3,2,1,0:T(8,128)(2,1)} %refs_3_.3, bf16[6,16,128,128]{3,2,1,0:T(8,128)(2,1)} %refs_7_.3, ...), custom_call_target="tpu_custom_call" | custom-call | flops 536870912 | bytes 14680064 | tf_op jit(solution)/shard_map/pallas_call | solution.py:287
  212.5 2.3 dynamic-slice_bitcast_fusion.3
  215.2 11.5 %collective-permute-done.25 = bf16[1,2,16,2,2,16,128]{6,5,2,1,3,4,0:T(8,128)(2,1)S(1)} collective-permute-done((bf16[1,2,16,2,2,16,128]{6,5,2,1,3,4,0:T(8,128)(2,1)S(1)}, bf16[1,2,16,2,2,16,128]{6,5,2,1,3,4,0:T(8,128)(2,1)S(1)}, u32[]{:S(2)}, u32[]{:S(2)}) %collective-permute-start.25) | collective-permute-done | bytes 524320 | tf_op jit(solution)/shard_map/ppermute | solution.py:36
  226.9 2.1 collective-permute-start.26
  229.0 18.8 %shard_map.141 = (bf16[512,2048]{1,0:T(8,128)(2,1)}, bf16[512,2048]{1,0:T(8,128)(2,1)}, bf16[512,2048]{1,0:T(8,128)(2,1)}, bf16[512,2048]{1,0:T(8,128)(2,1)}, bf...) custom-call(s32[16,2]{1,0:T(8,128)} %copy.40.pairs, bf16[512,2048]{1,0:T(8,128)(2,1)} %get-tuple-element.25.grad, ...), custom_call_target="tpu_custom_call" | custom-call | flops 2952790016 | bytes 19923072 | tf_op jit(solution)/shard_map/pallas_call | solution.py:287
  247.8 2.3 dynamic-slice_bitcast_fusion.2.after
  252.7 1.8 fusion.3
  255.4 1.6 collective-permute-start.7
  256.9 6.8 %shard_map.148 = bf16[1,2,16,128,128]{4,3,2,1,0:T(8,128)(2,1)} custom-call(bf16[512,2048]{1,0:T(8,128)(2,1)} %get-tuple-element.21.state, bf16[512,2048]{1,0:T(8,128)(2,1)} %copy-done.11, bf16[512,2048]{1,0:T(8,128)(2,1)} %get-tuple-element.25.grad, bf16[2,512,512]{2,1,0:T(8,128)(2,1)} %dynamic-slice_bitcast_fusion.2.after), custom_call_target="tpu_custom_call" | custom-call | flops 536870912 | bytes 8388608 | tf_op jit(solution)/shard_map/pallas_call | solution.py:287
  263.7 1.5 fusion.2.refs_4_
  266.2 7.9 %shard_map.142 = bf16[2,2,16,128,128]{4,3,2,1,0:T(8,128)(2,1)} custom-call(bf16[512,2048]{1,0:T(8,128)(2,1)} %get-tuple-element.28.refs_0_, bf16[512,2048]{1,0:T(8,128)(2,1)} %get-tuple-element.29.refs_1_, bf16[512,2048]{1,0:T(8,128)(2,1)} %get-tuple-element.30.refs_2_, bf16[512,2048]{1,0:T(8,128)(2,1)} %get-tuple-element.31.refs_3_, ...), custom_call_target="tpu_custom_call" | custom-call | flops 1073741824 | bytes 10485760 | tf_op jit(solution)/shard_map/pallas_call | solution.py:287
  274.1 2.5 dynamic-slice_bitcast_fusion.1
  276.6 1.7 collective-permute-start.16
  279.2 7.8 %shard_map.145 = bf16[2,2,16,128,128]{4,3,2,1,0:T(8,128)(2,1)} custom-call(bf16[512,2048]{1,0:T(8,128)(2,1)} %get-tuple-element.32.refs_0_, bf16[512,2048]{1,0:T(8,128)(2,1)} %get-tuple-element.33.refs_1_, bf16[512,2048]{1,0:T(8,128)(2,1)} %get-tuple-element.34.refs_2_, bf16[512,2048]{1,0:T(8,128)(2,1)} %get-tuple-element.35.refs_3_, ...), custom_call_target="tpu_custom_call" | custom-call | flops 1073741824 | bytes 10485760 | tf_op jit(solution)/shard_map/pallas_call | solution.py:287
  287.0 2.5 dynamic-slice_bitcast_fusion
  289.5 2.0 collective-permute-start.19
  292.5 3.5 all-to-all-start.2
  296.0 2.2 fusion.11
  298.2 2.3 fusion.5.value
  300.6 7.3 %collective-permute-done.16 = bf16[2,2,16,2,2,16,128]{6,5,4,3,2,1,0:T(8,128)(2,1)} collective-permute-done((bf16[2,2,16,2,2,16,128]{6,5,4,3,2,1,0:T(8,128)(2,1)}, bf16[2,2,16,2,2,16,128]{6,5,4,3,2,1,0:T(8,128)(2,1)}, u32[]{:S(2)}, u32[]{:S(2)}) %collective-permute-start.16) | collective-permute-done | bytes 1048608 | tf_op jit(solution)/shard_map/ppermute | solution.py:36
  307.8 2.6 fusion.1.value
  310.4 9.9 %collective-permute-done.19 = bf16[2,2,16,2,2,16,128]{6,5,4,3,2,1,0:T(8,128)(2,1)} collective-permute-done((bf16[2,2,16,2,2,16,128]{6,5,4,3,2,1,0:T(8,128)(2,1)}, bf16[2,2,16,2,2,16,128]{6,5,4,3,2,1,0:T(8,128)(2,1)}, u32[]{:S(2)}, u32[]{:S(2)}) %collective-permute-start.19) | collective-permute-done | bytes 1048608 | tf_op jit(solution)/shard_map/ppermute | solution.py:36
  320.3 2.7 fusion.value
  324.3 3.6 all-to-all-start.3
  327.9 2.6 multiply_reduce_fusion
  331.2 1.9 collective-permute-start.23
  333.2 1.9 dynamic-slice_bitcast_fusion.6
  341.9 2.9 collective-permute-done.23
  344.8 1.7 fusion.14.value
  346.5 3.6 collective-permute-done.17
  350.1 2.0 fusion.7.value
  352.1 3.3 collective-permute-done.20
  357.2 1.6 dynamic-slice_bitcast_fusion.14
  358.7 1.5 collective-permute-start.24
  361.2 1.5 collective-permute-start.18
  363.7 1.5 collective-permute-start.21
  365.2 2.3 add_convert_fusion.1
  367.5 16.8 %collective-permute-done.18 = bf16[2,2,16,16,128]{4,3,2,1,0:T(8,128)(2,1)} collective-permute-done((bf16[2,2,16,16,128]{4,3,2,1,0:T(8,128)(2,1)S(1)}, bf16[2,2,16,16,128]{4,3,2,1,0:T(8,128)(2,1)}, u32[]{:S(2)}, u32[]{:S(2)}) %collective-permute-start.18) | collective-permute-done | bytes 262176 | tf_op jit(solution)/shard_map/ppermute | solution.py:36
  385.4 4.4 %collective-permute-done.21 = bf16[2,2,16,16,128]{4,3,2,1,0:T(8,128)(2,1)S(1)} collective-permute-done((bf16[2,2,16,16,128]{4,3,2,1,0:T(8,128)(2,1)S(1)}, bf16[2,2,16,16,128]{4,3,2,1,0:T(8,128)(2,1)S(1)}, u32[]{:S(2)}, u32[]{:S(2)}) %collective-permute-start.21) | collective-permute-done | bytes 262176 | tf_op jit(solution)/shard_map/ppermute | solution.py:36
  393.4 11.5 %collective-permute-done.13 = bf16[512,512]{1,0:T(8,128)(2,1)S(1)} collective-permute-done((bf16[512,512]{1,0:T(8,128)(2,1)S(1)}, bf16[512,512]{1,0:T(8,128)(2,1)S(1)}, u32[]{:S(2)}, u32[]{:S(2)}) %collective-permute-start.13) | collective-permute-done | bytes 524320 | tf_op jit(solution)/shard_map/ppermute | solution.py:36
  (139 shorter events, 35.7 us)
Async XLA Ops:
  0.6 1.0 copy-start
  0.6 10.7 %copy-start.27 = (bf16[64,8,8]{0,2,1:T(8,128)(2,1)S(1)}, bf16[64,8,8]{0,2,1:T(8,128)(2,1)}, u32[]{:S(2)}) copy-start(bf16[64,8,8]{0,2,1:T(8,128)(2,1)} %param.11) | copy-start | bytes 24580
  4.0 21.8 %all-to-all-start = ((bf16[8,64,512]{2,1,0:T(8,128)(2,1)}), bf16[8,64,512]{2,1,0:T(8,128)(2,1)}, u32[]{:S(2)}, u32[]{:S(2)}) async-start(bf16[8,64,512]{2,1,0:T(8,128)(2,1)} %bitcast.2), calls=%async_computation | async-start | bytes 1048576 | tf_op jit(solution)/shard_map/all_to_all | solution.py:342
  12.1 19.6 %copy-start.20 = (bf16[512,512]{1,0:T(8,128)(2,1)S(1)}, bf16[512,512]{1,0:T(8,128)(2,1)}, u32[]{:S(2)}) copy-start(bf16[512,512]{1,0:T(8,128)(2,1)} %param.17) | copy-start | bytes 1572868
  12.1 34.3 %copy-start.13 = (bf16[512,512]{1,0:T(8,128)(2,1)S(1)}, bf16[512,512]{1,0:T(8,128)(2,1)}, u32[]{:S(2)}) copy-start(bf16[512,512]{1,0:T(8,128)(2,1)} %param.9) | copy-start | bytes 1572868
  12.7 33.8 %copy-start.22 = (bf16[512,512]{1,0:T(8,128)(2,1)}, bf16[512,512]{1,0:T(8,128)(2,1)S(1)}, u32[]{:S(2)}) copy-start(bf16[512,512]{1,0:T(8,128)(2,1)S(1)} %mul.56) | copy-start | bytes 1572868
  28.1 18.3 %all-to-all-start.1 = ((bf16[8,64,512]{2,1,0:T(8,128)(2,1)}), bf16[8,64,512]{2,1,0:T(8,128)(2,1)S(1)}, u32[]{:S(2)}, u32[]{:S(2)}) async-start(bf16[8,64,512]{2,1,0:T(8,128)(2,1)} %bitcast.4), calls=%async_computation.1 | async-start | bytes 1048576 | tf_op jit(solution)/shard_map/all_to_all | solution.py:344
  31.7 16.4 %collective-permute-start.4 = (bf16[512,512]{1,0:T(8,128)(2,1)S(1)}, bf16[512,512]{1,0:T(8,128)(2,1)}, u32[]{:S(2)}, u32[]{:S(2)}) collective-permute-start(bf16[512,512]{1,0:T(8,128)(2,1)S(1)} %copy-done.20), channel_id=1, source_target_pairs={{0,2},{1,3},{2,0},{3,1},{4,6},{5,7},{6,4},{7,5},{8,10},{9,11},{10,... | collective-permute-start | bytes 1572872 | tf_op jit(solution)/shard_map/ppermute | solution.py:36
  46.6 12.6 %collective-permute-start = (bf16[512,512]{1,0:T(8,128)(2,1)S(1)}, bf16[512,512]{1,0:T(8,128)(2,1)}, u32[]{:S(2)}, u32[]{:S(2)}) collective-permute-start(bf16[512,512]{1,0:T(8,128)(2,1)S(1)} %fusion.12), channel_id=1, source_target_pairs={{0,2},{1,3},{2,0},{3,1},{4,6},{5,7},{6,4},{7,5},{8,10},{9,11},{10,... | collective-permute-start | bytes 1572872 | tf_op jit(solution)/shard_map/ppermute | solution.py:36
  60.6 0.8 copy-start.14
  60.6 1.9 copy-start.28
  62.5 3.0 collective-permute-start.1
  82.6 4.4 %collective-permute-start.2 = (bf16[512,2048]{1,0:T(8,128)(2,1)}, bf16[512,2048]{1,0:T(8,128)(2,1)S(1)}, u32[]{:S(2)}, u32[]{:S(2)}) collective-permute-start(bf16[512,2048]{1,0:T(8,128)(2,1)} %get-tuple-element.21.state), channel_id=1, source_target_pairs={{0,1},{1,0},{2,3},{3,2},{4,5},{5,4},{6,7},{7,6},{8,9},{9,8},{10,11... | collective-permute-start | bytes 6291464 | tf_op jit(solution)/shard_map/ppermute | solution.py:36
  87.0 1.4 copy-start.11
  93.8 47.9 %collective-permute-start.3 = (bf16[512,2048]{1,0:T(8,128)(2,1)}, bf16[512,2048]{1,0:T(8,128)(2,1)S(1)}, u32[]{:S(2)}, u32[]{:S(2)}) collective-permute-start(bf16[512,2048]{1,0:T(8,128)(2,1)} %shard_map.137.state), channel_id=1, source_target_pairs={{0,2},{1,3},{2,0},{3,1},{4,6},{5,7},{6,4},{7,5},{8,10},{9,11},{10,... | collective-permute-start | bytes 6291464 | tf_op jit(solution)/shard_map/ppermute | solution.py:36
  95.4 2.7 collective-permute-start.5
  141.6 1.4 copy-start.12
  157.3 47.1 %collective-permute-start.8 = (bf16[512,2048]{1,0:T(8,128)(2,1)}, bf16[512,2048]{1,0:T(8,128)(2,1)S(1)}, u32[]{:S(2)}, u32[]{:S(2)}) collective-permute-start(bf16[512,2048]{1,0:T(8,128)(2,1)} %get-tuple-element.24.after), channel_id=1, source_target_pairs={{0,2},{1,3},{2,0},{3,1},{4,6},{5,7},{6,4},{7,5},{8,10},{9,11},{10,... | collective-permute-start | bytes 6291464 | tf_op jit(solution)/shard_map/ppermute | solution.py:36
  165.6 46.6 %copy-start.7 = (bf16[1,2,16,128,128]{4,3,2,1,0:T(8,128)(2,1)S(1)}, bf16[1,2,16,128,128]{4,3,2,1,0:T(8,128)(2,1)}, u32[]{:S(2)}) copy-start(bf16[1,2,16,128,128]{4,3,2,1,0:T(8,128)(2,1)} %shard_map.139.after) | copy-start | bytes 3145732
  204.4 1.4 copy-start.25
  212.1 16.9 %collective-permute-start.9 = (bf16[512,2048]{1,0:T(8,128)(2,1)}, bf16[512,2048]{1,0:T(8,128)(2,1)}, u32[]{:S(2)}, u32[]{:S(2)}) collective-permute-start(bf16[512,2048]{1,0:T(8,128)(2,1)} %get-tuple-element.26), channel_id=1, source_target_pairs={{0,1},{1,0},{2,3},{3,2},{4,5},{5,4},{6,7},{7,6},{8,9},{9,8},{10,11... | collective-permute-start | bytes 6291464 | tf_op jit(solution)/shard_map/ppermute | solution.py:36
  212.4 14.4 %collective-permute-start.25 = (bf16[1,2,16,2,2,16,128]{6,5,2,1,3,4,0:T(8,128)(2,1)S(1)}, bf16[1,2,16,2,2,16,128]{6,5,2,1,3,4,0:T(8,128)(2,1)S(1)}, u32[]{:S(2)}, u32[]{:S(2)}) collective-permute-start(bf16[1,2,16,2,2,16,128]{6,5,2,1,3,4,0:T(8,128)(2,1)S(1)} %bitcast.221), channel_id=1, source_target_pairs={{0,8},{4,12},{8,0},{12,4},{16,24},{20,28},{24,16},{28,20},{1,9},{5... | collective-permute-start | bytes 1572872 | tf_op jit(solution)/shard_map/ppermute | solution.py:36
  214.7 38.0 %collective-permute-start.6 = (bf16[2,512,512]{2,1,0:T(8,128)(2,1)}, bf16[2,512,512]{2,1,0:T(8,128)(2,1)}, u32[]{:S(2)}, u32[]{:S(2)}) collective-permute-start(bf16[2,512,512]{2,1,0:T(8,128)(2,1)} %dynamic-slice_bitcast_fusion.3), channel_id=1, source_target_pairs={{0,1},{1,0},{2,3},{3,2},{4,5},{5,4},{6,7},{7,6},{8,9},{9,8},{10,11... | collective-permute-start | bytes 3145736 | tf_op jit(solution)/shard_map/ppermute | solution.py:36
  226.9 23.8 %collective-permute-start.26 = (bf16[1,2,16,2,16,128]{5,4,2,1,3,0:T(8,128)(2,1)S(1)}, bf16[1,2,16,2,16,128]{5,4,2,1,3,0:T(8,128)(2,1)S(1)}, u32[]{:S(2)}, u32[]{:S(2)}) collective-permute-start(bf16[1,2,16,2,16,128]{5,4,2,1,3,0:T(8,128)(2,1)S(1)} %dynamic-slice_bitcast_fusion.9), channel_id=1, source_target_pairs={{0,4},{4,0},{8,12},{12,8},{16,20},{20,16},{24,28},{28,24},{1,5},{5... | collective-permute-start | bytes 786440 | tf_op jit(solution)/shard_map/ppermute | solution.py:36
  250.1 13.6 %collective-permute-start.10 = (bf16[2,512,512]{2,1,0:T(8,128)(2,1)}, bf16[2,512,512]{2,1,0:T(8,128)(2,1)}, u32[]{:S(2)}, u32[]{:S(2)}) collective-permute-start(bf16[2,512,512]{2,1,0:T(8,128)(2,1)} %dynamic-slice_bitcast_fusion.2.after), channel_id=1, source_target_pairs={{0,1},{1,0},{2,3},{3,2},{4,5},{5,4},{6,7},{7,6},{8,9},{9,8},{10,11... | collective-permute-start | bytes 3145736 | tf_op jit(solution)/shard_map/ppermute | solution.py:36
  251.5 139.3 %collective-permute-start.27 = (bf16[1,2,16,16,128]{4,3,2,1,0:T(8,128)(2,1)}, bf16[1,2,16,16,128]{4,3,2,1,0:T(8,128)(2,1)S(1)}, u32[]{:S(2)}, u32[]{:S(2)}) collective-permute-start(bf16[1,2,16,16,128]{4,3,2,1,0:T(8,128)(2,1)} %dynamic-slice_bitcast_fusion.13), channel_id=1, source_target_pairs={{0,16},{4,20},{8,24},{12,28},{16,0},{20,4},{24,8},{28,12},{1,17},{... | collective-permute-start | bytes 393224 | tf_op jit(solution)/shard_map/ppermute | solution.py:36
  255.4 8.3 %copy-start.24 = (bf16[4,512,512]{2,1,0:T(8,128)(2,1)S(1)}, bf16[4,512,512]{2,1,0:T(8,128)(2,1)}, u32[]{:S(2)}) copy-start(bf16[4,512,512]{2,1,0:T(8,128)(2,1)} %get-tuple-element.27) | copy-start | bytes 6291460
  255.4 40.7 %collective-permute-start.7 = (bf16[512,512]{1,0:T(8,128)(2,1)}, bf16[512,512]{1,0:T(8,128)(2,1)}, u32[]{:S(2)}, u32[]{:S(2)}) collective-permute-start(bf16[512,512]{1,0:T(8,128)(2,1)} %dynamic-slice_bitcast_fusion.8), channel_id=1, source_target_pairs={{0,2},{1,3},{2,0},{3,1},{4,6},{5,7},{6,4},{7,5},{8,10},{9,11},{10,... | collective-permute-start | bytes 1572872 | tf_op jit(solution)/shard_map/ppermute | solution.py:36
  265.2 1.0 copy-start.3
  265.3 24.2 %collective-permute-start.11 = (bf16[512,512]{1,0:T(8,128)(2,1)S(1)}, bf16[512,512]{1,0:T(8,128)(2,1)S(1)}, u32[]{:S(2)}, u32[]{:S(2)}) collective-permute-start(bf16[512,512]{1,0:T(8,128)(2,1)S(1)} %dynamic-slice_bitcast_fusion.7), channel_id=1, source_target_pairs={{0,2},{1,3},{2,0},{3,1},{4,6},{5,7},{6,4},{7,5},{8,10},{9,11},{10,... | collective-permute-start | bytes 1572872 | tf_op jit(solution)/shard_map/ppermute | solution.py:36
  274.1 4.2 %copy-start.18 = (bf16[1,2,16,128,128]{4,3,2,1,0:T(8,128)(2,1)S(1)}, bf16[1,2,16,128,128]{4,3,2,1,0:T(8,128)(2,1)}, u32[]{:S(2)}) copy-start(bf16[1,2,16,128,128]{4,3,2,1,0:T(8,128)(2,1)} %shard_map.148) | copy-start | bytes 3145732
  276.6 31.3 %collective-permute-start.16 = (bf16[2,2,16,2,2,16,128]{6,5,4,3,2,1,0:T(8,128)(2,1)}, bf16[2,2,16,2,2,16,128]{6,5,4,3,2,1,0:T(8,128)(2,1)}, u32[]{:S(2)}, u32[]{:S(2)}) collective-permute-start(bf16[2,2,16,2,2,16,128]{6,5,4,3,2,1,0:T(8,128)(2,1)} %dynamic-slice_bitcast_fusion.1), channel_id=1, source_target_pairs={{0,8},{4,12},{8,0},{12,4},{16,24},{20,28},{24,16},{28,20},{1,9},{5... | collective-permute-start | bytes 3145736 | tf_op jit(solution)/shard_map/ppermute | solution.py:36
  279.1 19.1 %collective-permute-start.22 = (bf16[1,2,16,2,2,16,128]{6,5,4,3,2,1,0:T(8,128)(2,1)}, bf16[1,2,16,2,2,16,128]{6,5,4,3,2,1,0:T(8,128)(2,1)}, u32[]{:S(2)}, u32[]{:S(2)}) collective-permute-start(bf16[1,2,16,2,2,16,128]{6,5,4,3,2,1,0:T(8,128)(2,1)} %dynamic-slice_bitcast_fusion.4), channel_id=1, source_target_pairs={{0,4},{4,0},{8,12},{12,8},{16,20},{20,16},{24,28},{28,24},{1,5},{5... | collective-permute-start | bytes 1572872 | tf_op jit(solution)/shard_map/ppermute | solution.py:36
  287.0 4.5 %copy-start.4 = (bf16[2,512,512]{2,1,0:T(8,128)(2,1)S(1)}, bf16[2,512,512]{2,1,0:T(8,128)(2,1)}, u32[]{:S(2)}) copy-start(bf16[2,512,512]{2,1,0:T(8,128)(2,1)} %copy-done.3) | copy-start | bytes 3145732
  287.0 4.5 %copy-start.21 = (bf16[512,512]{1,0:T(8,128)(2,1)S(1)}, bf16[512,512]{1,0:T(8,128)(2,1)}, u32[]{:S(2)}) copy-start(bf16[512,512]{1,0:T(8,128)(2,1)} %param.17) | copy-start | bytes 1572868
  289.5 30.8 %collective-permute-start.19 = (bf16[2,2,16,2,2,16,128]{6,5,4,3,2,1,0:T(8,128)(2,1)}, bf16[2,2,16,2,2,16,128]{6,5,4,3,2,1,0:T(8,128)(2,1)}, u32[]{:S(2)}, u32[]{:S(2)}) collective-permute-start(bf16[2,2,16,2,2,16,128]{6,5,4,3,2,1,0:T(8,128)(2,1)} %dynamic-slice_bitcast_fusion), channel_id=1, source_target_pairs={{0,4},{4,0},{8,12},{12,8},{16,20},{20,16},{24,28},{28,24},{1,5},{5... | collective-permute-start | bytes 3145736 | tf_op jit(solution)/shard_map/ppermute | solution.py:36
  292.5 30.5 %all-to-all-start.2 = ((bf16[8,64,512]{2,1,0:T(8,128)(2,1)}), bf16[8,64,512]{2,1,0:T(8,128)(2,1)S(1)}, u32[]{:S(2)}, u32[]{:S(2)}) async-start(bf16[8,64,512]{2,1,0:T(8,128)(2,1)} %bitcast.26), calls=%async_computation.2 | async-start | bytes 1048576 | tf_op jit(solution)/shard_map/all_to_all | solution.py:454
  296.0 11.8 %copy-start.9 = (bf16[2,2,16,128,128]{4,3,2,1,0:T(8,128)(2,1)S(1)}, bf16[2,2,16,128,128]{4,3,2,1,0:T(8,128)(2,1)}, u32[]{:S(2)}) copy-start(bf16[2,2,16,128,128]{4,3,2,1,0:T(8,128)(2,1)} %shard_map.142) | copy-start | bytes 6291460
  298.2 22.1 %copy-start.10 = (bf16[2,2,16,128,128]{4,3,2,1,0:T(8,128)(2,1)S(1)}, bf16[2,2,16,128,128]{4,3,2,1,0:T(8,128)(2,1)}, u32[]{:S(2)}) copy-start(bf16[2,2,16,128,128]{4,3,2,1,0:T(8,128)(2,1)} %shard_map.145) | copy-start | bytes 6291460
  310.4 12.6 %copy-start.23 = (bf16[512,512]{1,0:T(8,128)(2,1)S(1)}, bf16[512,512]{1,0:T(8,128)(2,1)}, u32[]{:S(2)}) copy-start(bf16[512,512]{1,0:T(8,128)(2,1)} %copy-done.22) | copy-start | bytes 1572868
  323.0 1.3 copy-start.8
  323.0 4.9 %copy-start.26 = (f32[64,64]{0,1:T(8,128)S(1)}, f32[64,64]{0,1:T(8,128)}, u32[]{:S(2)}) copy-start(f32[64,64]{0,1:T(8,128)} %fusion.30) | copy-start | bytes 49156
  324.3 6.2 %copy-start.17 = (bf16[1,2,16,2,2,16,128]{6,5,4,3,2,1,0:T(8,128)(2,1)S(1)}, bf16[1,2,16,2,2,16,128]{6,5,4,3,2,1,0:T(8,128)(2,1)}, u32[]{:S(2)}) copy-start(bf16[1,2,16,2,2,16,128]{6,5,4,3,2,1,0:T(8,128)(2,1)} %shard_map.149) | copy-start | bytes 1572868
  324.3 32.1 %all-to-all-start.3 = ((bf16[8,64,512]{2,1,0:T(8,128)(2,1)}), bf16[8,64,512]{2,1,0:T(8,128)(2,1)S(1)}, u32[]{:S(2)}, u32[]{:S(2)}) async-start(bf16[8,64,512]{2,1,0:T(8,128)(2,1)} %bitcast.28), calls=%async_computation.3 | async-start | bytes 1048576 | tf_op jit(solution)/shard_map/all_to_all | solution.py:456
  330.5 6.0 %collective-permute-start.14 = (f32[64,8,8]{0,2,1:T(8,128)}, f32[64,8,8]{0,2,1:T(8,128)}, u32[]{:S(2)}, u32[]{:S(2)}) collective-permute-start(f32[64,8,8]{0,2,1:T(8,128)} %bitcast.35), channel_id=1, source_target_pairs={{0,1},{1,0},{2,3},{3,2},{4,5},{5,4},{6,7},{7,6},{8,9},{9,8},{10,11... | collective-permute-start | bytes 49160 | tf_op jit(solution)/shard_map/ppermute | solution.py:36
  331.2 13.5 %collective-permute-start.23 = (bf16[1,2,16,2,16,128]{5,4,3,2,1,0:T(8,128)(2,1)}, bf16[1,2,16,2,16,128]{5,4,3,2,1,0:T(8,128)(2,1)}, u32[]{:S(2)}, u32[]{:S(2)}) collective-permute-start(bf16[1,2,16,2,16,128]{5,4,3,2,1,0:T(8,128)(2,1)} %dynamic-slice_bitcast_fusion.10), channel_id=1, source_target_pairs={{0,8},{4,12},{8,0},{12,4},{16,24},{20,28},{24,16},{28,20},{1,9},{5... | collective-permute-start | bytes 786440 | tf_op jit(solution)/shard_map/ppermute | solution.py:36
  335.0 15.1 %copy-start.6 = (bf16[2,2,16,2,2,16,128]{6,5,4,3,2,1,0:T(8,128)(2,1)S(1)}, bf16[2,2,16,2,2,16,128]{6,5,4,3,2,1,0:T(8,128)(2,1)}, u32[]{:S(2)}) copy-start(bf16[2,2,16,2,2,16,128]{6,5,4,3,2,1,0:T(8,128)(2,1)} %shard_map.143) | copy-start | bytes 3145732
  335.0 15.1 %collective-permute-start.17 = (bf16[2,2,16,2,16,128]{5,4,3,2,1,0:T(8,128)(2,1)}, bf16[2,2,16,2,16,128]{5,4,3,2,1,0:T(8,128)(2,1)}, u32[]{:S(2)}, u32[]{:S(2)}) collective-permute-start(bf16[2,2,16,2,16,128]{5,4,3,2,1,0:T(8,128)(2,1)} %dynamic-slice_bitcast_fusion.6), channel_id=1, source_target_pairs={{0,4},{4,0},{8,12},{12,8},{16,20},{20,16},{24,28},{28,24},{1,5},{5... | collective-permute-start | bytes 1572872 | tf_op jit(solution)/shard_map/ppermute | solution.py:36
  336.5 18.9 %copy-start.5 = (bf16[2,2,16,2,2,16,128]{6,5,4,3,2,1,0:T(8,128)(2,1)S(1)}, bf16[2,2,16,2,2,16,128]{6,5,4,3,2,1,0:T(8,128)(2,1)}, u32[]{:S(2)}) copy-start(bf16[2,2,16,2,2,16,128]{6,5,4,3,2,1,0:T(8,128)(2,1)} %shard_map.146) | copy-start | bytes 3145732
  337.4 3.9 collective-permute-start.15
  339.4 16.0 %collective-permute-start.20 = (bf16[2,2,16,2,16,128]{5,4,3,2,1,0:T(8,128)(2,1)S(1)}, bf16[2,2,16,2,16,128]{5,4,3,2,1,0:T(8,128)(2,1)S(1)}, u32[]{:S(2)}, u32[]{:S(2)}) collective-permute-start(bf16[2,2,16,2,16,128]{5,4,3,2,1,0:T(8,128)(2,1)S(1)} %dynamic-slice_bitcast_fusion.5), channel_id=1, source_target_pairs={{0,8},{4,12},{8,0},{12,4},{16,24},{20,28},{24,16},{28,20},{1,9},{5... | collective-permute-start | bytes 1572872 | tf_op jit(solution)/shard_map/ppermute | solution.py:36
  356.4 0.8 copy-start.1
  358.7 6.5 %copy-start.2 = (bf16[8,64,512]{2,1,0:T(8,128)(2,1)S(1)}, bf16[8,64,512]{2,1,0:T(8,128)(2,1)}, u32[]{:S(2)}) copy-start(bf16[8,64,512]{2,1,0:T(8,128)(2,1)} %copy-done.1) | copy-start | bytes 1572868
  358.7 31.1 %collective-permute-start.24 = (bf16[1,2,16,16,128]{4,3,2,1,0:T(8,128)(2,1)}, bf16[1,2,16,16,128]{4,3,2,1,0:T(8,128)(2,1)}, u32[]{:S(2)}, u32[]{:S(2)}) collective-permute-start(bf16[1,2,16,16,128]{4,3,2,1,0:T(8,128)(2,1)} %dynamic-slice_bitcast_fusion.14), channel_id=1, source_target_pairs={{0,16},{4,20},{8,24},{12,28},{16,0},{20,4},{24,8},{28,12},{1,17},{... | collective-permute-start | bytes 393224 | tf_op jit(solution)/shard_map/ppermute | solution.py:36
  360.2 30.7 %collective-permute-start.12 = (bf16[512,512]{1,0:T(8,128)(2,1)S(1)}, bf16[512,512]{1,0:T(8,128)(2,1)S(1)}, u32[]{:S(2)}, u32[]{:S(2)}) collective-permute-start(bf16[512,512]{1,0:T(8,128)(2,1)S(1)} %convolution_convert_fusion), channel_id=1, source_target_pairs={{0,1},{1,0},{2,3},{3,2},{4,5},{5,4},{6,7},{7,6},{8,9},{9,8},{10,11... | collective-permute-start | bytes 1572872 | tf_op jit(solution)/shard_map/ppermute | solution.py:36
  361.2 23.1 %copy-start.15 = (bf16[2,2,16,2,16,128]{5,4,3,2,1,0:T(8,128)(2,1)S(1)}, bf16[2,2,16,2,16,128]{5,4,3,2,1,0:T(8,128)(2,1)}, u32[]{:S(2)}) copy-start(bf16[2,2,16,2,16,128]{5,4,3,2,1,0:T(8,128)(2,1)} %shard_map.144) | copy-start | bytes 1572868
  361.2 23.1 %collective-permute-start.18 = (bf16[2,2,16,16,128]{4,3,2,1,0:T(8,128)(2,1)S(1)}, bf16[2,2,16,16,128]{4,3,2,1,0:T(8,128)(2,1)}, u32[]{:S(2)}, u32[]{:S(2)}) collective-permute-start(bf16[2,2,16,16,128]{4,3,2,1,0:T(8,128)(2,1)S(1)} %dynamic-slice_bitcast_fusion.12), channel_id=1, source_target_pairs={{0,16},{4,20},{8,24},{12,28},{16,0},{20,4},{24,8},{28,12},{1,17},{... | collective-permute-start | bytes 786440 | tf_op jit(solution)/shard_map/ppermute | solution.py:36
  363.7 26.1 %copy-start.16 = (bf16[2,2,16,2,16,128]{5,4,3,2,1,0:T(8,128)(2,1)S(1)}, bf16[2,2,16,2,16,128]{5,4,3,2,1,0:T(8,128)(2,1)}, u32[]{:S(2)}) copy-start(bf16[2,2,16,2,16,128]{5,4,3,2,1,0:T(8,128)(2,1)} %shard_map.147) | copy-start | bytes 1572868
  363.7 26.0 %collective-permute-start.21 = (bf16[2,2,16,16,128]{4,3,2,1,0:T(8,128)(2,1)S(1)}, bf16[2,2,16,16,128]{4,3,2,1,0:T(8,128)(2,1)S(1)}, u32[]{:S(2)}, u32[]{:S(2)}) collective-permute-start(bf16[2,2,16,16,128]{4,3,2,1,0:T(8,128)(2,1)S(1)} %dynamic-slice_bitcast_fusion.11), channel_id=1, source_target_pairs={{0,16},{4,20},{8,24},{12,28},{16,0},{20,4},{24,8},{28,12},{1,17},{... | collective-permute-start | bytes 786440 | tf_op jit(solution)/shard_map/ppermute | solution.py:36
  367.5 22.3 %copy-start.19 = (bf16[1,2,16,2,16,128]{5,4,3,2,1,0:T(8,128)(2,1)S(1)}, bf16[1,2,16,2,16,128]{5,4,3,2,1,0:T(8,128)(2,1)}, u32[]{:S(2)}) copy-start(bf16[1,2,16,2,16,128]{5,4,3,2,1,0:T(8,128)(2,1)} %shard_map.150) | copy-start | bytes 786436
  391.0 13.9 %collective-permute-start.13 = (bf16[512,512]{1,0:T(8,128)(2,1)S(1)}, bf16[512,512]{1,0:T(8,128)(2,1)S(1)}, u32[]{:S(2)}, u32[]{:S(2)}) collective-permute-start(bf16[512,512]{1,0:T(8,128)(2,1)S(1)} %add_convert_fusion), channel_id=1, source_target_pairs={{0,2},{1,3},{2,0},{3,1},{4,6},{5,7},{6,4},{7,5},{8,10},{9,11},{10,... | collective-permute-start | bytes 1572872 | tf_op jit(solution)/shard_map/ppermute | solution.py:36

commit v5 on v4

--- a/solution.py
+++ b/solution.py
@@ -102,7 +102,9 @@
     for bit in range(bits_of(axis)):
         total = value.astype(F32) + partner_2(value, axis, bit).astype(F32)
         value = total.astype(kind)
-    return total
+        if bit == 0:
+            first = value
+    return total, first
 
 
 def lanes(index, width):
@@ -322,8 +324,17 @@
     orders = [seq_bits, seq_bits[1:2] + seq_bits[:1] + seq_bits[2:]]
     tp_bits = list(range(bits_of("tp")))
 
+    def chunks_of(result):
+        return result.reshape(result.shape[:3] + (seq_size, width // seq_size, width))
+
+    def first_given(result, order):
+        left = list(reversed(range(bits_of("seq"))))
+        chunked = chunks_of(result)
+        chunked = chunked.reshape(chunked.shape[:3] + (2,) * len(left) + chunked.shape[4:])
+        return halve(chunked, "seq", 3, left, order[0])[2]
+
     def summed(result, order, ties=()):
-        chunked = result.reshape(result.shape[:3] + (seq_size, width // seq_size, width))
+        chunked = chunks_of(result)
         return halved_sum(chunked, "seq", 3, order, ties)[0]
 
     row_state = rows_of(state_shape.shape, tile)
@@ -407,14 +418,16 @@
         )
         return result
 
+    early = []
     for level in range(last, local, -1):
         incoming = partner_2(send, "tp", level - local)
         result = across_terms(level, grad, send)
-        terms[level] = summed(result, orders[level % 2])[0]
+        early.append((level, result))
+        given = first_given(result, orders[level % 2])
         grad, send = call(
             functools.partial(middle_kernel, slots, width),
             steps,
-            [grad, incoming, w_self, w_cross, result],
+            [grad, incoming, w_self, w_cross, given],
             [
                 row_state,
                 row_state,
@@ -454,7 +467,11 @@
     grad_rows = lax.all_to_all(grad_hidden, "seq", split_axis=0, concat_axis=0, tiled=True)
     moved_back = dot_tn(mixer, grad_rows).astype(BF)
     returned = lax.all_to_all(moved_back, "seq", split_axis=0, concat_axis=0, tiled=True)
-    ties = [None, grad_rows, returned]
+    first_part = dot_nt(returned, tokens).astype(BF)
+    first_sum, first_hop = exchanged_sum(first_part, "tp")
+    ties = [None, grad_rows, first_hop]
+    for level, result in early:
+        terms[level] = summed(result, orders[level % 2], [None, spread, grad_rows])[0]
     result = across_terms(local, grad_above, spread_sent)
     terms[local] = summed(result, orders[local % 2], ties)[0]
     for top in range(local, 0, -2):
@@ -476,9 +493,7 @@
 
     cross_rows = dot_nt(grad_rows, first_rows).reshape(groups, positions, groups, positions)
     second_part = jnp.sum(cross_rows * same.astype(F32)[None, :, None, :], axis=3).transpose(1, 0, 2)
-    first_part = dot_nt(returned, tokens).astype(BF)
-    second_sum = exchanged_sum(second_part, "tp")
-    first_sum = exchanged_sum(first_part, "tp")
+    second_sum, _ = exchanged_sum(second_part, "tp")
     grad_mix = dot_tn(first_factor, returned)
     grad_tokens = (grad_hidden.astype(F32) + grad_mix).astype(BF)
     level_terms = jnp.stack(terms, axis=1) * token_scale

time: 407 us -> 410 us (level)
    convert_element_type x10, other arithmetic: 15.8 us -> 20.3 us  [halved_sum(): value = total.astype(BF)]
    squeeze x15 -> x16, local copies, waits for them, and re-layouts: 19.1 us -> 21.8 us  [halve(): give = lax.dynamic_index_in_dim(value, 1 - mine, at, keepdims=False)]
where the time goes in v5:
time: 410 us; the launch traced here: 408 us
  waiting for transfers between devices  198 us (48%)
  Pallas kernels  88.1 us (21%)
  starting transfers between devices  46.3 us (11%)
  other arithmetic  32 us (8%)
  local copies, waits for them, and re-layouts  31.7 us (8%)
  matrix products  11.4 us (3%)
    ppermute x28, waiting for transfers between devices, partner_2(): return lax.ppermute(value, axis, pairs)  171 us
    pallas_call x9, Pallas kernels, call(): pl.pallas_call(kernel, grid=(steps,), in_specs=in_specs, out_specs=out_sp...  88.1 us
    ppermute x28, starting transfers between devices, partner_2(): return lax.ppermute(value, axis, pairs)  26.8 us
    squeeze x16, local copies, waits for them, and re-layouts, halve(): give = lax.dynamic_index_in_dim(value, 1 - mine, at, keepdims=False)  21.8 us
    convert_element_type x10, other arithmetic, halved_sum(): value = total.astype(BF)  20.3 us
    all_to_all x1, waiting for transfers between devices, per_device(): lax.all_to_all(first_out, 'seq', split_axis=0, concat_axis=0, tiled=True)  13.1 us
    all_to_all x1, waiting for transfers between devices, per_device(): lax.all_to_all(mixed_part, 'seq', split_axis=0, concat_axis=0, tiled=True)  13.1 us
    dot_general x6, matrix products, dot(): lax.dot_general(left, right, (contract, ((), ())), preferred_element_type...  11.4 us
  transfers between devices with their start and end apart: 32, of which 18 were waited for; matrix products, arithmetic and copies ran while one was open for 14% of the time, Pallas kernels for 12%

profile of v5, /device:TPU:0, one launch (start us, length us, event | category | flops | bytes accessed | tf_op | source)
XLA Modules:
  0.0 408.5 jit_solution(9749221441316165276)
XLA Ops:
  1.7 2.3 convolution_convert_fusion.3
  4.0 7.3 %all-to-all-start = ((bf16[8,64,512]{2,1,0:T(8,128)(2,1)}), bf16[8,64,512]{2,1,0:T(8,128)(2,1)}, u32[]{:S(2)}, u32[]{:S(2)}) async-start(bf16[8,64,512]{2,1,0:T(8,128)(2,1)} %bitcast.2), calls=%async_computation | async-start | bytes 1048576 | tf_op jit(solution)/shard_map/all_to_all | solution.py:353
  12.7 13.1 %all-to-all-done = bf16[8,64,512]{2,1,0:T(8,128)(2,1)} async-done(((bf16[8,64,512]{2,1,0:T(8,128)(2,1)}), bf16[8,64,512]{2,1,0:T(8,128)(2,1)}, u32[]{:S(2)}, u32[]{:S(2)}) %all-to-all-start) | async-done | bytes 524320 | tf_op jit(solution)/shard_map/all_to_all | solution.py:353
  25.8 2.3 convolution_convert_fusion.2
  28.1 3.6 all-to-all-start.1
  31.7 1.6 collective-permute-start.4
  33.3 13.1 %all-to-all-done.1 = bf16[8,64,512]{2,1,0:T(8,128)(2,1)S(1)} async-done(((bf16[8,64,512]{2,1,0:T(8,128)(2,1)}), bf16[8,64,512]{2,1,0:T(8,128)(2,1)S(1)}, u32[]{:S(2)}, u32[]{:S(2)}) %all-to-all-start.1) | async-done | bytes 524320 | tf_op jit(solution)/shard_map/all_to_all | solution.py:355
  46.5 1.6 collective-permute-start
  48.1 11.0 %collective-permute-done = bf16[512,512]{1,0:T(8,128)(2,1)} collective-permute-done((bf16[512,512]{1,0:T(8,128)(2,1)S(1)}, bf16[512,512]{1,0:T(8,128)(2,1)}, u32[]{:S(2)}, u32[]{:S(2)}) %collective-permute-start) | collective-permute-done | bytes 524320 | tf_op jit(solution)/shard_map/ppermute | solution.py:36
  59.1 2.1 select_bitcast_fusion.5
  63.0 2.2 collective-permute-done.1
  65.5 1.6 copy.41
  67.1 13.8 %shard_map.136 = (bf16[512,2048]{1,0:T(8,128)(2,1)}, bf16[512,2048]{1,0:T(8,128)(2,1)}, bf16[512,2048]{1,0:T(8,128)(2,1)}, bf16[512,2048]{1,0:T(8,128)(2,1)}, bf16[512,2048]{1,0:T(8,128)(2,1)}) custom-call(s32[16,2]{1,0:T(8,128)} %copy.44.pairs, bf16[4,512,512]{2,1,0:T(8,128)(2,1)} %bitcast.214, bf16[16,2,128,128]{3,2,1,0:T(8,128)(2,1)} %w_up.3, ...), custom_call_target="tpu_custom_call" | custom-call | flops 2684354560 | bytes 16777344 | tf_op jit(solution)/shard_map/pallas_call | solution.py:289
  81.1 4.2 %collective-permute-done.2.partner = bf16[512,2048]{1,0:T(8,128)(2,1)S(1)} collective-permute-done((bf16[512,2048]{1,0:T(8,128)(2,1)}, bf16[512,2048]{1,0:T(8,128)(2,1)S(1)}, u32[]{:S(2)}, u32[]{:S(2)}) %collective-permute-start.2) | collective-permute-done | bytes 2097184 | tf_op jit(solution)/shard_map/ppermute | solution.py:36
  86.8 5.4 %shard_map.137.state = bf16[512,2048]{1,0:T(8,128)(2,1)} custom-call(bf16[512,2048]{1,0:T(8,128)(2,1)} %get-tuple-element.21.state, bf16[512,2048]{1,0:T(8,128)(2,1)} %copy-done.12, bf16[6,16,128,128]{3,2,1,0:T(8,128)(2,1)} %refs_3_.3, bf16[6,16,128,128]{3,2,1,0:T(8,128)(2,1)} %refs_7_.3), custom_call_target="tpu_custom_call" | custom-call | flops 536870912 | bytes 12582912 | tf_op jit(solution)/shard_map/pallas_call | solution.py:289
  92.2 1.5 collective-permute-start.3
  93.9 2.6 collective-permute-done.5
  96.9 1.5 copy.43
  98.5 41.7 %collective-permute-done.3.partner = bf16[512,2048]{1,0:T(8,128)(2,1)S(1)} collective-permute-done((bf16[512,2048]{1,0:T(8,128)(2,1)}, bf16[512,2048]{1,0:T(8,128)(2,1)S(1)}, u32[]{:S(2)}, u32[]{:S(2)}) %collective-permute-start.3) | collective-permute-done | bytes 2097184 | tf_op jit(solution)/shard_map/ppermute | solution.py:36
  141.4 14.4 %shard_map.138 = (bf16[4,512,512]{2,1,0:T(8,128)(2,1)}, bf16[512,2048]{1,0:T(8,128)(2,1)}, bf16[512,2048]{1,0:T(8,128)(2,1)}) custom-call(s32[16,2]{1,0:T(8,128)} %copy.44.pairs, bf16[512,2048]{1,0:T(8,128)(2,1)} %shard_map.137.state, bf16[512,2048]{1,0:T(8,128)(2,1)} %copy-done.13, bf16[6,16,128,128]{3,2,1,0:T(8,128)(2,1)} %refs_3_.3, ...), custom_call_target="tpu_custom_call" | custom-call | flops 1879048192 | bytes 13631616 | tf_op jit(solution)/shard_map/pallas_call | solution.py:289
  155.8 1.5 collective-permute-start.8
  157.4 6.7 %shard_map.139 = bf16[1,2,16,128,128]{4,3,2,1,0:T(8,128)(2,1)} custom-call(bf16[512,2048]{1,0:T(8,128)(2,1)} %shard_map.137.state, bf16[512,2048]{1,0:T(8,128)(2,1)} %copy-done.13, bf16[512,2048]{1,0:T(8,128)(2,1)} %get-tuple-element.23.grad, bf16[512,2048]{1,0:T(8,128)(2,1)} %get-tuple-element.24.after), custom_call_target="tpu_custom_call" | custom-call | flops 536870912 | bytes 9437184 | tf_op jit(solution)/shard_map/pallas_call | solution.py:289
  164.1 1.9 dynamic-slice_bitcast_fusion.8.after
  165.9 37.1 %collective-permute-done.8.incoming = bf16[512,2048]{1,0:T(8,128)(2,1)} collective-permute-done((bf16[512,2048]{1,0:T(8,128)(2,1)}, bf16[512,2048]{1,0:T(8,128)(2,1)}, u32[]{:S(2)}, u32[]{:S(2)}) %collective-permute-start.8) | collective-permute-done | bytes 2097184 | tf_op jit(solution)/shard_map/ppermute | solution.py:36
  203.0 6.4 %shard_map.140 = (bf16[512,2048]{1,0:T(8,128)(2,1)}, bf16[512,2048]{1,0:T(8,128)(2,1)}) custom-call(bf16[512,2048]{1,0:T(8,128)(2,1)} %get-tuple-element.23.grad, bf16[512,2048]{1,0:T(8,128)(2,1)} %collective-permute-done.8.incoming, bf16[6,16,128,128]{3,2,1,0:T(8,128)(2,1)} %refs_3_.3, bf16[6,16,128,128]{3,2,1,0:T(8,128)(2,1)} %refs_7_.3, ...), custom_call_target="tpu_custom_call" | custom-call | flops 536870912 | bytes 14680064 | tf_op jit(solution)/shard_map/pallas_call | solution.py:289
  211.0 4.3 %collective-permute-done.6 = bf16[2,512,512]{2,1,0:T(8,128)(2,1)S(1)} collective-permute-done((bf16[2,512,512]{2,1,0:T(8,128)(2,1)}, bf16[2,512,512]{2,1,0:T(8,128)(2,1)S(1)}, u32[]{:S(2)}, u32[]{:S(2)}) %collective-permute-start.6) | collective-permute-done | bytes 1048608 | tf_op jit(solution)/shard_map/ppermute | solution.py:36
  215.3 1.5 fusion.3
  216.8 18.9 %shard_map.141 = (bf16[512,2048]{1,0:T(8,128)(2,1)}, bf16[512,2048]{1,0:T(8,128)(2,1)}, bf16[512,2048]{1,0:T(8,128)(2,1)}, bf16[512,2048]{1,0:T(8,128)(2,1)}, bf...) custom-call(s32[16,2]{1,0:T(8,128)} %copy.44.pairs, bf16[512,2048]{1,0:T(8,128)(2,1)} %get-tuple-element.25.grad, ...), custom_call_target="tpu_custom_call" | custom-call | flops 2952790016 | bytes 19923072 | tf_op jit(solution)/shard_map/pallas_call | solution.py:289
  235.7 2.4 dynamic-slice_bitcast_fusion.2.after
  239.0 1.6 collective-permute-start.7
  240.6 2.0 fusion.4.value
  242.6 10.9 %collective-permute-done.7 = bf16[512,512]{1,0:T(8,128)(2,1)} collective-permute-done((bf16[512,512]{1,0:T(8,128)(2,1)}, bf16[512,512]{1,0:T(8,128)(2,1)}, u32[]{:S(2)}, u32[]{:S(2)}) %collective-permute-start.7) | collective-permute-done | bytes 524320 | tf_op jit(solution)/shard_map/ppermute | solution.py:36
  253.5 2.0 fusion.11
  255.6 6.9 %shard_map.148 = bf16[1,2,16,128,128]{4,3,2,1,0:T(8,128)(2,1)} custom-call(bf16[512,2048]{1,0:T(8,128)(2,1)} %get-tuple-element.21.state, bf16[512,2048]{1,0:T(8,128)(2,1)} %copy-done.12, bf16[512,2048]{1,0:T(8,128)(2,1)} %get-tuple-element.25.grad, bf16[2,512,512]{2,1,0:T(8,128)(2,1)} %dynamic-slice_bitcast_fusion.2.after), custom_call_target="tpu_custom_call" | custom-call | flops 536870912 | bytes 8388608 | tf_op jit(solution)/shard_map/pallas_call | solution.py:289
  262.4 1.9 dynamic-slice_bitcast_fusion.4
  264.3 2.0 collective-permute-start.22
  266.3 1.5 fusion.2.refs_4_
  267.9 1.6 collective-permute-start.11
  269.4 7.9 %shard_map.142 = bf16[2,2,16,128,128]{4,3,2,1,0:T(8,128)(2,1)} custom-call(bf16[512,2048]{1,0:T(8,128)(2,1)} %get-tuple-element.28.refs_0_, bf16[512,2048]{1,0:T(8,128)(2,1)} %get-tuple-element.29.refs_1_, bf16[512,2048]{1,0:T(8,128)(2,1)} %get-tuple-element.30.refs_2_, bf16[512,2048]{1,0:T(8,128)(2,1)} %get-tuple-element.31.refs_3_, ...), custom_call_target="tpu_custom_call" | custom-call | flops 1073741824 | bytes 10485760 | tf_op jit(solution)/shard_map/pallas_call | solution.py:289
  277.3 2.4 dynamic-slice_bitcast_fusion.1
  279.8 7.7 %shard_map.145 = bf16[2,2,16,128,128]{4,3,2,1,0:T(8,128)(2,1)} custom-call(bf16[512,2048]{1,0:T(8,128)(2,1)} %get-tuple-element.32.refs_0_, bf16[512,2048]{1,0:T(8,128)(2,1)} %get-tuple-element.33.refs_1_, bf16[512,2048]{1,0:T(8,128)(2,1)} %get-tuple-element.34.refs_2_, bf16[512,2048]{1,0:T(8,128)(2,1)} %get-tuple-element.35.refs_3_, ...), custom_call_target="tpu_custom_call" | custom-call | flops 1073741824 | bytes 10485760 | tf_op jit(solution)/shard_map/pallas_call | solution.py:289
  287.5 2.5 dynamic-slice_bitcast_fusion
  290.1 2.0 collective-permute-start.26
  293.1 4.4 %all-to-all-start.2 = ((bf16[8,64,512]{2,1,0:T(8,128)(2,1)}), bf16[8,64,512]{2,1,0:T(8,128)(2,1)S(1)}, u32[]{:S(2)}, u32[]{:S(2)}) async-start(bf16[8,64,512]{2,1,0:T(8,128)(2,1)} %bitcast.215), calls=%async_computation.2 | async-start | bytes 1048576 | tf_op jit(solution)/shard_map/all_to_all | solution.py:467
  297.5 27.4 %collective-permute-done.26 = bf16[1,2,16,2,16,128]{5,4,3,2,1,0:T(8,128)(2,1)} collective-permute-done((bf16[1,2,16,2,16,128]{5,4,3,2,1,0:T(8,128)(2,1)S(1)}, bf16[1,2,16,2,16,128]{5,4,3,2,1,0:T(8,128)(2,1)}, u32[]{:S(2)}, u32[]{:S(2)}) %collective-permute-start.26) | collective-permute-done | bytes 262176 | tf_op jit(solution)/shard_map/ppermute | solution.py:36
  324.9 1.8 fusion.13.value
  326.8 2.4 fusion.5.value
  329.1 2.6 fusion.1.value
  331.7 2.7 fusion.value
  335.7 4.3 %all-to-all-start.3 = ((bf16[8,64,512]{2,1,0:T(8,128)(2,1)}), bf16[8,64,512]{2,1,0:T(8,128)(2,1)}, u32[]{:S(2)}, u32[]{:S(2)}) async-start(bf16[8,64,512]{2,1,0:T(8,128)(2,1)} %bitcast.30), calls=%async_computation.3 | async-start | bytes 1048576 | tf_op jit(solution)/shard_map/all_to_all | solution.py:469
  340.1 1.8 multiply_reduce_fusion
  342.6 2.8 collective-permute-start.27
  347.6 1.9 dynamic-slice_bitcast_fusion.6
  352.2 1.9 dynamic-slice_bitcast_fusion.5
  359.5 1.8 fusion.14.value
  361.3 2.3 collective-permute-done.17
  363.6 2.0 fusion.7.value
  365.5 4.8 %collective-permute-done.20 = bf16[2,2,16,2,16,128]{5,4,3,2,1,0:T(8,128)(2,1)} collective-permute-done((bf16[2,2,16,2,16,128]{5,4,3,2,1,0:T(8,128)(2,1)}, bf16[2,2,16,2,16,128]{5,4,3,2,1,0:T(8,128)(2,1)}, u32[]{:S(2)}, u32[]{:S(2)}) %collective-permute-start.20) | collective-permute-done | bytes 524320 | tf_op jit(solution)/shard_map/ppermute | solution.py:36
  370.4 2.0 fusion.6.value
  374.8 2.3 add_convert_fusion.1
  378.5 1.6 dynamic-slice_bitcast_fusion.15
  380.1 2.5 collective-permute-start.24
  384.1 12.3 %collective-permute-done.18 = bf16[2,2,16,16,128]{4,3,2,1,0:T(8,128)(2,1)S(1)} collective-permute-done((bf16[2,2,16,16,128]{4,3,2,1,0:T(8,128)(2,1)S(1)}, bf16[2,2,16,16,128]{4,3,2,1,0:T(8,128)(2,1)S(1)}, u32[]{:S(2)}, u32[]{:S(2)}) %collective-permute-start.18) | collective-permute-done | bytes 262176 | tf_op jit(solution)/shard_map/ppermute | solution.py:36
  396.5 8.2 %collective-permute-done.21 = bf16[2,2,16,16,128]{4,3,2,1,0:T(8,128)(2,1)S(1)} collective-permute-done((bf16[2,2,16,16,128]{4,3,2,1,0:T(8,128)(2,1)S(1)}, bf16[2,2,16,16,128]{4,3,2,1,0:T(8,128)(2,1)S(1)}, u32[]{:S(2)}, u32[]{:S(2)}) %collective-permute-start.21) | collective-permute-done | bytes 262176 | tf_op jit(solution)/shard_map/ppermute | solution.py:36
  (148 shorter events, 33.3 us)
Async XLA Ops:
  0.6 10.7 %copy-start.31 = (bf16[64,8,8]{0,2,1:T(8,128)(2,1)S(1)}, bf16[64,8,8]{0,2,1:T(8,128)(2,1)}, u32[]{:S(2)}) copy-start(bf16[64,8,8]{0,2,1:T(8,128)(2,1)} %param.11) | copy-start | bytes 24580
  4.0 21.8 %all-to-all-start = ((bf16[8,64,512]{2,1,0:T(8,128)(2,1)}), bf16[8,64,512]{2,1,0:T(8,128)(2,1)}, u32[]{:S(2)}, u32[]{:S(2)}) async-start(bf16[8,64,512]{2,1,0:T(8,128)(2,1)} %bitcast.2), calls=%async_computation | async-start | bytes 1048576 | tf_op jit(solution)/shard_map/all_to_all | solution.py:353
  12.1 19.6 %copy-start.26 = (bf16[512,512]{1,0:T(8,128)(2,1)S(1)}, bf16[512,512]{1,0:T(8,128)(2,1)}, u32[]{:S(2)}) copy-start(bf16[512,512]{1,0:T(8,128)(2,1)} %param.17) | copy-start | bytes 1572868
  12.1 34.3 %copy-start.14 = (bf16[512,512]{1,0:T(8,128)(2,1)S(1)}, bf16[512,512]{1,0:T(8,128)(2,1)}, u32[]{:S(2)}) copy-start(bf16[512,512]{1,0:T(8,128)(2,1)} %param.9) | copy-start | bytes 1572868
  12.7 20.6 %copy-start.28 = (bf16[512,512]{1,0:T(8,128)(2,1)}, bf16[512,512]{1,0:T(8,128)(2,1)S(1)}, u32[]{:S(2)}) copy-start(bf16[512,512]{1,0:T(8,128)(2,1)S(1)} %mul.56) | copy-start | bytes 1572868
  28.1 18.3 %all-to-all-start.1 = ((bf16[8,64,512]{2,1,0:T(8,128)(2,1)}), bf16[8,64,512]{2,1,0:T(8,128)(2,1)S(1)}, u32[]{:S(2)}, u32[]{:S(2)}) async-start(bf16[8,64,512]{2,1,0:T(8,128)(2,1)} %bitcast.4), calls=%async_computation.1 | async-start | bytes 1048576 | tf_op jit(solution)/shard_map/all_to_all | solution.py:355
  31.7 16.4 %collective-permute-start.4 = (bf16[512,512]{1,0:T(8,128)(2,1)S(1)}, bf16[512,512]{1,0:T(8,128)(2,1)S(1)}, u32[]{:S(2)}, u32[]{:S(2)}) collective-permute-start(bf16[512,512]{1,0:T(8,128)(2,1)S(1)} %copy-done.26), channel_id=1, source_target_pairs={{0,2},{1,3},{2,0},{3,1},{4,6},{5,7},{6,4},{7,5},{8,10},{9,11},{10,... | collective-permute-start | bytes 1572872 | tf_op jit(solution)/shard_map/ppermute | solution.py:36
  46.5 12.6 %collective-permute-start = (bf16[512,512]{1,0:T(8,128)(2,1)S(1)}, bf16[512,512]{1,0:T(8,128)(2,1)}, u32[]{:S(2)}, u32[]{:S(2)}) collective-permute-start(bf16[512,512]{1,0:T(8,128)(2,1)S(1)} %fusion.12), channel_id=1, source_target_pairs={{0,2},{1,3},{2,0},{3,1},{4,6},{5,7},{6,4},{7,5},{8,10},{9,11},{10,... | collective-permute-start | bytes 1572872 | tf_op jit(solution)/shard_map/ppermute | solution.py:36
  61.2 1.1 copy-start.32
  62.3 2.9 collective-permute-start.1
  80.9 12.8 %copy-start.16 = (bf16[1,512,512]{2,1,0:T(8,128)(2,1)S(1)}, bf16[1,512,512]{2,1,0:T(8,128)(2,1)}, u32[]{:S(2)}) copy-start(bf16[1,512,512]{2,1,0:T(8,128)(2,1)} %get-tuple-element.42) | copy-start | bytes 1572868
  80.9 12.8 %copy-start.17 = (bf16[1,512,512]{2,1,0:T(8,128)(2,1)S(1)}, bf16[1,512,512]{2,1,0:T(8,128)(2,1)}, u32[]{:S(2)}) copy-start(bf16[1,512,512]{2,1,0:T(8,128)(2,1)} %get-tuple-element.43) | copy-start | bytes 1572868
  80.9 4.4 %collective-permute-start.2 = (bf16[512,2048]{1,0:T(8,128)(2,1)}, bf16[512,2048]{1,0:T(8,128)(2,1)S(1)}, u32[]{:S(2)}, u32[]{:S(2)}) collective-permute-start(bf16[512,2048]{1,0:T(8,128)(2,1)} %get-tuple-element.21.state), channel_id=1, source_target_pairs={{0,1},{1,0},{2,3},{3,2},{4,5},{5,4},{6,7},{7,6},{8,9},{9,8},{10,11... | collective-permute-start | bytes 6291464 | tf_op jit(solution)/shard_map/ppermute | solution.py:36
  85.4 1.4 copy-start.12
  92.2 47.9 %collective-permute-start.3 = (bf16[512,2048]{1,0:T(8,128)(2,1)}, bf16[512,2048]{1,0:T(8,128)(2,1)S(1)}, u32[]{:S(2)}, u32[]{:S(2)}) collective-permute-start(bf16[512,2048]{1,0:T(8,128)(2,1)} %shard_map.137.state), channel_id=1, source_target_pairs={{0,2},{1,3},{2,0},{3,1},{4,6},{5,7},{6,4},{7,5},{8,10},{9,11},{10,... | collective-permute-start | bytes 6291464 | tf_op jit(solution)/shard_map/ppermute | solution.py:36
  93.8 2.7 collective-permute-start.5
  140.1 1.3 copy-start.13
  155.8 47.2 %collective-permute-start.8 = (bf16[512,2048]{1,0:T(8,128)(2,1)}, bf16[512,2048]{1,0:T(8,128)(2,1)}, u32[]{:S(2)}, u32[]{:S(2)}) collective-permute-start(bf16[512,2048]{1,0:T(8,128)(2,1)} %get-tuple-element.24.after), channel_id=1, source_target_pairs={{0,2},{1,3},{2,0},{3,1},{4,6},{5,7},{6,4},{7,5},{8,10},{9,11},{10,... | collective-permute-start | bytes 6291464 | tf_op jit(solution)/shard_map/ppermute | solution.py:36
  165.9 43.5 %copy-start.30 = (bf16[4,512,512]{2,1,0:T(8,128)(2,1)S(1)}, bf16[4,512,512]{2,1,0:T(8,128)(2,1)}, u32[]{:S(2)}) copy-start(bf16[4,512,512]{2,1,0:T(8,128)(2,1)} %get-tuple-element.22) | copy-start | bytes 6291460
  209.4 7.4 %collective-permute-start.9 = (bf16[512,2048]{1,0:T(8,128)(2,1)}, bf16[512,2048]{1,0:T(8,128)(2,1)}, u32[]{:S(2)}, u32[]{:S(2)}) collective-permute-start(bf16[512,2048]{1,0:T(8,128)(2,1)} %get-tuple-element.26), channel_id=1, source_target_pairs={{0,1},{1,0},{2,3},{3,2},{4,5},{5,4},{6,7},{7,6},{8,9},{9,8},{10,11... | collective-permute-start | bytes 6291464 | tf_op jit(solution)/shard_map/ppermute | solution.py:36
  210.5 4.8 %collective-permute-start.6 = (bf16[2,512,512]{2,1,0:T(8,128)(2,1)}, bf16[2,512,512]{2,1,0:T(8,128)(2,1)S(1)}, u32[]{:S(2)}, u32[]{:S(2)}) collective-permute-start(bf16[2,512,512]{2,1,0:T(8,128)(2,1)} %dynamic-slice_bitcast_fusion.3), channel_id=1, source_target_pairs={{0,1},{1,0},{2,3},{3,2},{4,5},{5,4},{6,7},{7,6},{8,9},{9,8},{10,11... | collective-permute-start | bytes 3145736 | tf_op jit(solution)/shard_map/ppermute | solution.py:36
  211.0 29.6 %collective-permute-start.25 = (bf16[1,2,16,2,2,16,128]{6,5,4,3,2,1,0:T(8,128)(2,1)}, bf16[1,2,16,2,2,16,128]{6,5,4,3,2,1,0:T(8,128)(2,1)}, u32[]{:S(2)}, u32[]{:S(2)}) collective-permute-start(bf16[1,2,16,2,2,16,128]{6,5,4,3,2,1,0:T(8,128)(2,1)} %dynamic-slice_bitcast_fusion.8.after), channel_id=1, source_target_pairs={{0,8},{4,12},{8,0},{12,4},{16,24},{20,28},{24,16},{28,20},{1,9},{5... | collective-permute-start | bytes 1572872 | tf_op jit(solution)/shard_map/ppermute | solution.py:36
  235.7 4.9 %copy-start.23 = (bf16[1,2,16,128,128]{4,3,2,1,0:T(8,128)(2,1)S(1)}, bf16[1,2,16,128,128]{4,3,2,1,0:T(8,128)(2,1)}, u32[]{:S(2)}) copy-start(bf16[1,2,16,128,128]{4,3,2,1,0:T(8,128)(2,1)} %shard_map.139) | copy-start | bytes 3145732
  238.0 28.2 %collective-permute-start.10 = (bf16[2,512,512]{2,1,0:T(8,128)(2,1)}, bf16[2,512,512]{2,1,0:T(8,128)(2,1)}, u32[]{:S(2)}, u32[]{:S(2)}) collective-permute-start(bf16[2,512,512]{2,1,0:T(8,128)(2,1)} %dynamic-slice_bitcast_fusion.2.after), channel_id=1, source_target_pairs={{0,1},{1,0},{2,3},{3,2},{4,5},{5,4},{6,7},{7,6},{8,9},{9,8},{10,11... | collective-permute-start | bytes 3145736 | tf_op jit(solution)/shard_map/ppermute | solution.py:36
  239.0 14.6 %collective-permute-start.7 = (bf16[512,512]{1,0:T(8,128)(2,1)}, bf16[512,512]{1,0:T(8,128)(2,1)}, u32[]{:S(2)}, u32[]{:S(2)}) collective-permute-start(bf16[512,512]{1,0:T(8,128)(2,1)} %dynamic-slice_bitcast_fusion.9), channel_id=1, source_target_pairs={{0,2},{1,3},{2,0},{3,1},{4,6},{5,7},{6,4},{7,5},{8,10},{9,11},{10,... | collective-permute-start | bytes 1572872 | tf_op jit(solution)/shard_map/ppermute | solution.py:36
  255.6 10.7 %copy-start.9 = (bf16[4,512,512]{2,1,0:T(8,128)(2,1)S(1)}, bf16[4,512,512]{2,1,0:T(8,128)(2,1)}, u32[]{:S(2)}) copy-start(bf16[4,512,512]{2,1,0:T(8,128)(2,1)} %get-tuple-element.27.tie) | copy-start | bytes 6291460
  264.3 62.5 %collective-permute-start.22 = (bf16[1,2,16,2,2,16,128]{6,5,4,3,2,1,0:T(8,128)(2,1)}, bf16[1,2,16,2,2,16,128]{6,5,4,3,2,1,0:T(8,128)(2,1)}, u32[]{:S(2)}, u32[]{:S(2)}) collective-permute-start(bf16[1,2,16,2,2,16,128]{6,5,4,3,2,1,0:T(8,128)(2,1)} %dynamic-slice_bitcast_fusion.4), channel_id=1, source_target_pairs={{0,4},{4,0},{8,12},{12,8},{16,20},{20,16},{24,28},{28,24},{1,5},{5... | collective-permute-start | bytes 1572872 | tf_op jit(solution)/shard_map/ppermute | solution.py:36
  267.8 1.6 copy-start.1
  267.9 24.3 %collective-permute-start.11 = (bf16[512,512]{1,0:T(8,128)(2,1)S(1)}, bf16[512,512]{1,0:T(8,128)(2,1)S(1)}, u32[]{:S(2)}, u32[]{:S(2)}) collective-permute-start(bf16[512,512]{1,0:T(8,128)(2,1)S(1)} %dynamic-slice_bitcast_fusion.7), channel_id=1, source_target_pairs={{0,2},{1,3},{2,0},{3,1},{4,6},{5,7},{6,4},{7,5},{8,10},{9,11},{10,... | collective-permute-start | bytes 1572872 | tf_op jit(solution)/shard_map/ppermute | solution.py:36
  279.8 49.4 %collective-permute-start.16 = (bf16[2,2,16,2,2,16,128]{6,5,4,3,2,1,0:T(8,128)(2,1)}, bf16[2,2,16,2,2,16,128]{6,5,4,3,2,1,0:T(8,128)(2,1)}, u32[]{:S(2)}, u32[]{:S(2)}) collective-permute-start(bf16[2,2,16,2,2,16,128]{6,5,4,3,2,1,0:T(8,128)(2,1)} %dynamic-slice_bitcast_fusion.1), channel_id=1, source_target_pairs={{0,8},{4,12},{8,0},{12,4},{16,24},{20,28},{24,16},{28,20},{1,9},{5... | collective-permute-start | bytes 3145736 | tf_op jit(solution)/shard_map/ppermute | solution.py:36
  287.5 2.6 copy-start.22
  287.5 4.7 %copy-start.2 = (bf16[2,512,512]{2,1,0:T(8,128)(2,1)S(1)}, bf16[2,512,512]{2,1,0:T(8,128)(2,1)}, u32[]{:S(2)}) copy-start(bf16[2,512,512]{2,1,0:T(8,128)(2,1)} %copy-done.1) | copy-start | bytes 3145732
  287.5 4.7 %copy-start.27 = (bf16[512,512]{1,0:T(8,128)(2,1)S(1)}, bf16[512,512]{1,0:T(8,128)(2,1)}, u32[]{:S(2)}) copy-start(bf16[512,512]{1,0:T(8,128)(2,1)} %param.17) | copy-start | bytes 1572868
  290.0 41.7 %collective-permute-start.19 = (bf16[2,2,16,2,2,16,128]{6,5,4,3,2,1,0:T(8,128)(2,1)}, bf16[2,2,16,2,2,16,128]{6,5,4,3,2,1,0:T(8,128)(2,1)}, u32[]{:S(2)}, u32[]{:S(2)}) collective-permute-start(bf16[2,2,16,2,2,16,128]{6,5,4,3,2,1,0:T(8,128)(2,1)} %dynamic-slice_bitcast_fusion), channel_id=1, source_target_pairs={{0,4},{4,0},{8,12},{12,8},{16,20},{20,16},{24,28},{28,24},{1,5},{5... | collective-permute-start | bytes 3145736 | tf_op jit(solution)/shard_map/ppermute | solution.py:36
  290.1 34.8 %collective-permute-start.26 = (bf16[1,2,16,2,16,128]{5,4,3,2,1,0:T(8,128)(2,1)S(1)}, bf16[1,2,16,2,16,128]{5,4,3,2,1,0:T(8,128)(2,1)}, u32[]{:S(2)}, u32[]{:S(2)}) collective-permute-start(bf16[1,2,16,2,16,128]{5,4,3,2,1,0:T(8,128)(2,1)S(1)} %dynamic-slice_bitcast_fusion.10), channel_id=1, source_target_pairs={{0,4},{4,0},{8,12},{12,8},{16,20},{20,16},{24,28},{28,24},{1,5},{5... | collective-permute-start | bytes 786440 | tf_op jit(solution)/shard_map/ppermute | solution.py:36
  293.1 36.0 %copy-start.10 = (bf16[2,2,16,128,128]{4,3,2,1,0:T(8,128)(2,1)S(1)}, bf16[2,2,16,128,128]{4,3,2,1,0:T(8,128)(2,1)}, u32[]{:S(2)}) copy-start(bf16[2,2,16,128,128]{4,3,2,1,0:T(8,128)(2,1)} %shard_map.142) | copy-start | bytes 6291460
  293.1 41.3 %all-to-all-start.2 = ((bf16[8,64,512]{2,1,0:T(8,128)(2,1)}), bf16[8,64,512]{2,1,0:T(8,128)(2,1)S(1)}, u32[]{:S(2)}, u32[]{:S(2)}) async-start(bf16[8,64,512]{2,1,0:T(8,128)(2,1)} %bitcast.215), calls=%async_computation.2 | async-start | bytes 1048576 | tf_op jit(solution)/shard_map/all_to_all | solution.py:467
  326.8 5.0 %copy-start.11 = (bf16[2,2,16,128,128]{4,3,2,1,0:T(8,128)(2,1)S(1)}, bf16[2,2,16,128,128]{4,3,2,1,0:T(8,128)(2,1)}, u32[]{:S(2)}) copy-start(bf16[2,2,16,128,128]{4,3,2,1,0:T(8,128)(2,1)} %shard_map.145) | copy-start | bytes 6291460
  331.7 2.7 copy-start.29
  334.5 1.3 copy-start.3
  335.7 4.3 %copy-start.4 = (bf16[8,64,512]{2,1,0:T(8,128)(2,1)S(1)}, bf16[8,64,512]{2,1,0:T(8,128)(2,1)}, u32[]{:S(2)}) copy-start(bf16[8,64,512]{2,1,0:T(8,128)(2,1)} %copy-done.3) | copy-start | bytes 1572868
  335.7 6.2 %copy-start.25 = (bf16[1,2,16,2,16,128]{5,4,3,2,1,0:T(8,128)(2,1)S(1)}, bf16[1,2,16,2,16,128]{5,4,3,2,1,0:T(8,128)(2,1)}, u32[]{:S(2)}) copy-start(bf16[1,2,16,2,16,128]{5,4,3,2,1,0:T(8,128)(2,1)} %shard_map.152) | copy-start | bytes 786436
  335.7 9.7 %copy-start.19 = (bf16[1,2,16,2,2,16,128]{6,5,4,3,2,1,0:T(8,128)(2,1)S(1)}, bf16[1,2,16,2,2,16,128]{6,5,4,3,2,1,0:T(8,128)(2,1)}, u32[]{:S(2)}) copy-start(bf16[1,2,16,2,2,16,128]{6,5,4,3,2,1,0:T(8,128)(2,1)} %shard_map.149) | copy-start | bytes 1572868
  335.7 21.0 %all-to-all-start.3 = ((bf16[8,64,512]{2,1,0:T(8,128)(2,1)}), bf16[8,64,512]{2,1,0:T(8,128)(2,1)}, u32[]{:S(2)}, u32[]{:S(2)}) async-start(bf16[8,64,512]{2,1,0:T(8,128)(2,1)} %bitcast.30), calls=%async_computation.3 | async-start | bytes 1048576 | tf_op jit(solution)/shard_map/all_to_all | solution.py:469
  341.8 9.1 %collective-permute-start.14 = (f32[64,8,8]{0,2,1:T(8,128)S(1)}, f32[64,8,8]{0,2,1:T(8,128)S(1)}, u32[]{:S(2)}, u32[]{:S(2)}) collective-permute-start(f32[64,8,8]{0,2,1:T(8,128)S(1)} %bitcast.222), channel_id=1, source_target_pairs={{0,1},{1,0},{2,3},{3,2},{4,5},{5,4},{6,7},{7,6},{8,9},{9,8},{10,11... | collective-permute-start | bytes 49160 | tf_op jit(solution)/shard_map/ppermute | solution.py:36
  342.6 63.2 %collective-permute-start.27 = (bf16[1,2,16,16,128]{4,3,2,1,0:T(8,128)(2,1)}, bf16[1,2,16,16,128]{4,3,2,1,0:T(8,128)(2,1)S(1)}, u32[]{:S(2)}, u32[]{:S(2)}) collective-permute-start(bf16[1,2,16,16,128]{4,3,2,1,0:T(8,128)(2,1)} %dynamic-slice_bitcast_fusion.14), channel_id=1, source_target_pairs={{0,16},{4,20},{8,24},{12,28},{16,0},{20,4},{24,8},{28,12},{1,17},{... | collective-permute-start | bytes 393224 | tf_op jit(solution)/shard_map/ppermute | solution.py:36
  346.1 13.3 %collective-permute-start.23 = (bf16[1,2,16,2,16,128]{5,4,3,2,1,0:T(8,128)(2,1)}, bf16[1,2,16,2,16,128]{5,4,3,2,1,0:T(8,128)(2,1)}, u32[]{:S(2)}, u32[]{:S(2)}) collective-permute-start(bf16[1,2,16,2,16,128]{5,4,3,2,1,0:T(8,128)(2,1)} %dynamic-slice_bitcast_fusion.11), channel_id=1, source_target_pairs={{0,8},{4,12},{8,0},{12,4},{16,24},{20,28},{24,16},{28,20},{1,9},{5... | collective-permute-start | bytes 786440 | tf_op jit(solution)/shard_map/ppermute | solution.py:36
  349.5 7.2 %copy-start.15 = (bf16[512,512]{1,0:T(8,128)(2,1)S(1)}, bf16[512,512]{1,0:T(8,128)(2,1)}, u32[]{:S(2)}) copy-start(bf16[512,512]{1,0:T(8,128)(2,1)} %param.9) | copy-start | bytes 1572868
  349.5 14.1 %collective-permute-start.17 = (bf16[2,2,16,2,16,128]{5,4,3,2,1,0:T(8,128)(2,1)}, bf16[2,2,16,2,16,128]{5,4,3,2,1,0:T(8,128)(2,1)}, u32[]{:S(2)}, u32[]{:S(2)}) collective-permute-start(bf16[2,2,16,2,16,128]{5,4,3,2,1,0:T(8,128)(2,1)} %dynamic-slice_bitcast_fusion.6), channel_id=1, source_target_pairs={{0,4},{4,0},{8,12},{12,8},{16,20},{20,16},{24,28},{28,24},{1,5},{5... | collective-permute-start | bytes 1572872 | tf_op jit(solution)/shard_map/ppermute | solution.py:36
  351.0 12.6 %copy-start.8 = (bf16[2,2,16,2,2,16,128]{6,5,4,3,2,1,0:T(8,128)(2,1)S(1)}, bf16[2,2,16,2,2,16,128]{6,5,4,3,2,1,0:T(8,128)(2,1)}, u32[]{:S(2)}) copy-start(bf16[2,2,16,2,2,16,128]{6,5,4,3,2,1,0:T(8,128)(2,1)} %shard_map.143) | copy-start | bytes 3145732
  351.0 4.0 collective-permute-start.15
  354.0 16.3 %copy-start.7 = (bf16[2,2,16,2,2,16,128]{6,5,4,3,2,1,0:T(8,128)(2,1)S(1)}, bf16[2,2,16,2,2,16,128]{6,5,4,3,2,1,0:T(8,128)(2,1)}, u32[]{:S(2)}) copy-start(bf16[2,2,16,2,2,16,128]{6,5,4,3,2,1,0:T(8,128)(2,1)} %shard_map.146) | copy-start | bytes 3145732
  354.0 16.3 %collective-permute-start.20 = (bf16[2,2,16,2,16,128]{5,4,3,2,1,0:T(8,128)(2,1)}, bf16[2,2,16,2,16,128]{5,4,3,2,1,0:T(8,128)(2,1)}, u32[]{:S(2)}, u32[]{:S(2)}) collective-permute-start(bf16[2,2,16,2,16,128]{5,4,3,2,1,0:T(8,128)(2,1)} %dynamic-slice_bitcast_fusion.5), channel_id=1, source_target_pairs={{0,8},{4,12},{8,0},{12,4},{16,24},{20,28},{24,16},{28,20},{1,9},{5... | collective-permute-start | bytes 1572872 | tf_op jit(solution)/shard_map/ppermute | solution.py:36
  358.2 14.1 %collective-permute-start.12 = (bf16[512,512]{1,0:T(8,128)(2,1)S(1)}, bf16[512,512]{1,0:T(8,128)(2,1)S(1)}, u32[]{:S(2)}, u32[]{:S(2)}) collective-permute-start(bf16[512,512]{1,0:T(8,128)(2,1)S(1)} %convolution_convert_fusion), channel_id=1, source_target_pairs={{0,1},{1,0},{2,3},{3,2},{4,5},{5,4},{6,7},{7,6},{8,9},{9,8},{10,11... | collective-permute-start | bytes 1572872 | tf_op jit(solution)/shard_map/ppermute | solution.py:36
  372.3 2.5 copy-start.21
  373.3 3.9 copy-start.5
  374.3 22.1 %collective-permute-start.18 = (bf16[2,2,16,16,128]{4,3,2,1,0:T(8,128)(2,1)S(1)}, bf16[2,2,16,16,128]{4,3,2,1,0:T(8,128)(2,1)S(1)}, u32[]{:S(2)}, u32[]{:S(2)}) collective-permute-start(bf16[2,2,16,16,128]{4,3,2,1,0:T(8,128)(2,1)S(1)} %dynamic-slice_bitcast_fusion.13), channel_id=1, source_target_pairs={{0,16},{4,20},{8,24},{12,28},{16,0},{20,4},{24,8},{28,12},{1,17},{... | collective-permute-start | bytes 786440 | tf_op jit(solution)/shard_map/ppermute | solution.py:36
  377.1 19.2 %copy-start.20 = (bf16[2,2,16,2,16,128]{5,4,3,2,1,0:T(8,128)(2,1)S(1)}, bf16[2,2,16,2,16,128]{5,4,3,2,1,0:T(8,128)(2,1)}, u32[]{:S(2)}) copy-start(bf16[2,2,16,2,16,128]{5,4,3,2,1,0:T(8,128)(2,1)} %shard_map.144) | copy-start | bytes 1572868
  377.1 30.2 %collective-permute-start.13 = (bf16[512,512]{1,0:T(8,128)(2,1)S(1)}, bf16[512,512]{1,0:T(8,128)(2,1)S(1)}, u32[]{:S(2)}, u32[]{:S(2)}) collective-permute-start(bf16[512,512]{1,0:T(8,128)(2,1)S(1)} %copy-done.5), channel_id=1, source_target_pairs={{0,2},{1,3},{2,0},{3,1},{4,6},{5,7},{6,4},{7,5},{8,10},{9,11},{10,... | collective-permute-start | bytes 1572872 | tf_op jit(solution)/shard_map/ppermute | solution.py:36
  380.1 24.8 %collective-permute-start.24 = (bf16[1,2,16,16,128]{4,3,2,1,0:T(8,128)(2,1)}, bf16[1,2,16,16,128]{4,3,2,1,0:T(8,128)(2,1)}, u32[]{:S(2)}, u32[]{:S(2)}) collective-permute-start(bf16[1,2,16,16,128]{4,3,2,1,0:T(8,128)(2,1)} %dynamic-slice_bitcast_fusion.15), channel_id=1, source_target_pairs={{0,16},{4,20},{8,24},{12,28},{16,0},{20,4},{24,8},{28,12},{1,17},{... | collective-permute-start | bytes 393224 | tf_op jit(solution)/shard_map/ppermute | solution.py:36
  382.6 22.1 %copy-start.18 = (bf16[2,2,16,2,16,128]{5,4,3,2,1,0:T(8,128)(2,1)S(1)}, bf16[2,2,16,2,16,128]{5,4,3,2,1,0:T(8,128)(2,1)}, u32[]{:S(2)}) copy-start(bf16[2,2,16,2,16,128]{5,4,3,2,1,0:T(8,128)(2,1)} %shard_map.147) | copy-start | bytes 1572868
  383.7 21.2 %copy-start.24 = (bf16[1,2,16,2,16,128]{5,4,3,2,1,0:T(8,128)(2,1)S(1)}, bf16[1,2,16,2,16,128]{5,4,3,2,1,0:T(8,128)(2,1)}, u32[]{:S(2)}) copy-start(bf16[1,2,16,2,16,128]{5,4,3,2,1,0:T(8,128)(2,1)} %shard_map.150) | copy-start | bytes 786436
  383.7 21.0 %collective-permute-start.21 = (bf16[2,2,16,16,128]{4,3,2,1,0:T(8,128)(2,1)S(1)}, bf16[2,2,16,16,128]{4,3,2,1,0:T(8,128)(2,1)S(1)}, u32[]{:S(2)}, u32[]{:S(2)}) collective-permute-start(bf16[2,2,16,16,128]{4,3,2,1,0:T(8,128)(2,1)S(1)} %dynamic-slice_bitcast_fusion.12), channel_id=1, source_target_pairs={{0,16},{4,20},{8,24},{12,28},{16,0},{20,4},{24,8},{28,12},{1,17},{... | collective-permute-start | bytes 786440 | tf_op jit(solution)/shard_map/ppermute | solution.py:36
  406.0 1.3 copy-start.6
  (1 other events, 1.0 us)

commit v6 on v5

--- a/solution.py
+++ b/solution.py
@@ -471,7 +471,7 @@
     first_sum, first_hop = exchanged_sum(first_part, "tp")
     ties = [None, grad_rows, first_hop]
     for level, result in early:
-        terms[level] = summed(result, orders[level % 2], [None, spread, grad_rows])[0]
+        terms[level] = summed(result, orders[level % 2])[0]
     result = across_terms(local, grad_above, spread_sent)
     terms[local] = summed(result, orders[local % 2], ties)[0]
     for top in range(local, 0, -2):

time: 410 us -> 399 us (0.973)
  waiting for transfers between devices: 198 us -> 180 us
  local copies, waits for them, and re-layouts: 31.7 us -> 38.1 us
    ppermute x28, waiting for transfers between devices: 171 us -> 154 us  [partner_2(): return lax.ppermute(value, axis, pairs)]
  transfers between devices with their start and end apart: 32 -> 32, of which waited for: 18 -> 17; matrix products, arithmetic and copies ran while one was open for 14% -> 16% of each run, Pallas kernels for 12% -> 12%
where the time goes in v6:
time: 399 us; the launch traced here: 397 us
  waiting for transfers between devices  180 us (45%)
  Pallas kernels  88 us (22%)
  starting transfers between devices  45 us (11%)
  local copies, waits for them, and re-layouts  38.1 us (10%)
  other arithmetic  33 us (8%)
  matrix products  11.6 us (3%)
    ppermute x28, waiting for transfers between devices, partner_2(): return lax.ppermute(value, axis, pairs)  154 us
    pallas_call x9, Pallas kernels, call(): pl.pallas_call(kernel, grid=(steps,), in_specs=in_specs, out_specs=out_sp...  88 us
    ppermute x28, starting transfers between devices, partner_2(): return lax.ppermute(value, axis, pairs)  26.4 us
    squeeze x16, local copies, waits for them, and re-layouts, halve(): give = lax.dynamic_index_in_dim(value, 1 - mine, at, keepdims=False)  22.1 us
    convert_element_type x10, other arithmetic, halved_sum(): value = total.astype(BF)  18.9 us
    all_to_all x1, waiting for transfers between devices, per_device(): lax.all_to_all(first_out, 'seq', split_axis=0, concat_axis=0, tiled=True)  13.1 us
    all_to_all x1, waiting for transfers between devices, per_device(): lax.all_to_all(mixed_part, 'seq', split_axis=0, concat_axis=0, tiled=True)  13.1 us
    dot_general x6, matrix products, dot(): lax.dot_general(left, right, (contract, ((), ())), preferred_element_type...  11.6 us
  transfers between devices with their start and end apart: 32, of which 17 were waited for; matrix products, arithmetic and copies ran while one was open for 16% of the time, Pallas kernels for 12%

profile of v6, /device:TPU:0, one launch (start us, length us, event | category | flops | bytes accessed | tf_op | source)
XLA Modules:
  0.0 397.1 jit_solution(11485802160324048191)
XLA Ops:
  1.7 2.3 convolution_convert_fusion.3
  4.0 7.3 %all-to-all-start = ((bf16[8,64,512]{2,1,0:T(8,128)(2,1)}), bf16[8,64,512]{2,1,0:T(8,128)(2,1)}, u32[]{:S(2)}, u32[]{:S(2)}) async-start(bf16[8,64,512]{2,1,0:T(8,128)(2,1)} %bitcast.2), calls=%async_computation | async-start | bytes 1048576 | tf_op jit(solution)/shard_map/all_to_all | solution.py:353
  12.7 13.1 %all-to-all-done = bf16[8,64,512]{2,1,0:T(8,128)(2,1)} async-done(((bf16[8,64,512]{2,1,0:T(8,128)(2,1)}), bf16[8,64,512]{2,1,0:T(8,128)(2,1)}, u32[]{:S(2)}, u32[]{:S(2)}) %all-to-all-start) | async-done | bytes 524320 | tf_op jit(solution)/shard_map/all_to_all | solution.py:353
  25.8 2.3 convolution_convert_fusion.2
  28.1 3.6 all-to-all-start.1
  31.7 1.6 collective-permute-start.4
  33.3 13.1 %all-to-all-done.1 = bf16[8,64,512]{2,1,0:T(8,128)(2,1)S(1)} async-done(((bf16[8,64,512]{2,1,0:T(8,128)(2,1)}), bf16[8,64,512]{2,1,0:T(8,128)(2,1)S(1)}, u32[]{:S(2)}, u32[]{:S(2)}) %all-to-all-start.1) | async-done | bytes 524320 | tf_op jit(solution)/shard_map/all_to_all | solution.py:355
  46.6 1.6 collective-permute-start
  48.2 11.0 %collective-permute-done = bf16[512,512]{1,0:T(8,128)(2,1)} collective-permute-done((bf16[512,512]{1,0:T(8,128)(2,1)S(1)}, bf16[512,512]{1,0:T(8,128)(2,1)}, u32[]{:S(2)}, u32[]{:S(2)}) %collective-permute-start) | collective-permute-done | bytes 524320 | tf_op jit(solution)/shard_map/ppermute | solution.py:36
  59.1 2.3 select_bitcast_fusion.5
  63.2 2.3 collective-permute-done.1
  67.1 1.6 copy.38
  68.7 13.9 %shard_map.136 = (bf16[512,2048]{1,0:T(8,128)(2,1)}, bf16[512,2048]{1,0:T(8,128)(2,1)}, bf16[512,2048]{1,0:T(8,128)(2,1)}, bf16[512,2048]{1,0:T(8,128)(2,1)}, bf16[512,2048]{1,0:T(8,128)(2,1)}) custom-call(s32[16,2]{1,0:T(8,128)} %copy.41.pairs, bf16[4,512,512]{2,1,0:T(8,128)(2,1)} %bitcast.208, bf16[16,2,128,128]{3,2,1,0:T(8,128)(2,1)} %w_up.3, ...), custom_call_target="tpu_custom_call" | custom-call | flops 2684354560 | bytes 16777344 | tf_op jit(solution)/shard_map/pallas_call | solution.py:289
  82.7 4.2 %collective-permute-done.2.partner = bf16[512,2048]{1,0:T(8,128)(2,1)S(1)} collective-permute-done((bf16[512,2048]{1,0:T(8,128)(2,1)}, bf16[512,2048]{1,0:T(8,128)(2,1)S(1)}, u32[]{:S(2)}, u32[]{:S(2)}) %collective-permute-start.2) | collective-permute-done | bytes 2097184 | tf_op jit(solution)/shard_map/ppermute | solution.py:36
  88.4 5.4 %shard_map.137.state = bf16[512,2048]{1,0:T(8,128)(2,1)} custom-call(bf16[512,2048]{1,0:T(8,128)(2,1)} %get-tuple-element.21.state, bf16[512,2048]{1,0:T(8,128)(2,1)} %copy-done.10, bf16[6,16,128,128]{3,2,1,0:T(8,128)(2,1)} %refs_3_.3, bf16[6,16,128,128]{3,2,1,0:T(8,128)(2,1)} %refs_7_.3), custom_call_target="tpu_custom_call" | custom-call | flops 536870912 | bytes 12582912 | tf_op jit(solution)/shard_map/pallas_call | solution.py:289
  93.8 1.5 collective-permute-start.3
  95.5 2.6 collective-permute-done.5
  98.5 1.5 copy.40
  100.0 41.7 %collective-permute-done.3.partner = bf16[512,2048]{1,0:T(8,128)(2,1)S(1)} collective-permute-done((bf16[512,2048]{1,0:T(8,128)(2,1)}, bf16[512,2048]{1,0:T(8,128)(2,1)S(1)}, u32[]{:S(2)}, u32[]{:S(2)}) %collective-permute-start.3) | collective-permute-done | bytes 2097184 | tf_op jit(solution)/shard_map/ppermute | solution.py:36
  143.0 14.4 %shard_map.138 = (bf16[4,512,512]{2,1,0:T(8,128)(2,1)}, bf16[512,2048]{1,0:T(8,128)(2,1)}, bf16[512,2048]{1,0:T(8,128)(2,1)}) custom-call(s32[16,2]{1,0:T(8,128)} %copy.41.pairs, bf16[512,2048]{1,0:T(8,128)(2,1)} %shard_map.137.state, bf16[512,2048]{1,0:T(8,128)(2,1)} %copy-done.11, bf16[6,16,128,128]{3,2,1,0:T(8,128)(2,1)} %refs_3_.3, ...), custom_call_target="tpu_custom_call" | custom-call | flops 1879048192 | bytes 13631616 | tf_op jit(solution)/shard_map/pallas_call | solution.py:289
  157.4 1.5 collective-permute-start.8
  158.9 6.7 %shard_map.139 = bf16[1,2,16,128,128]{4,3,2,1,0:T(8,128)(2,1)} custom-call(bf16[512,2048]{1,0:T(8,128)(2,1)} %shard_map.137.state, bf16[512,2048]{1,0:T(8,128)(2,1)} %copy-done.11, bf16[512,2048]{1,0:T(8,128)(2,1)} %get-tuple-element.23.grad, bf16[512,2048]{1,0:T(8,128)(2,1)} %get-tuple-element.24.after), custom_call_target="tpu_custom_call" | custom-call | flops 536870912 | bytes 9437184 | tf_op jit(solution)/shard_map/pallas_call | solution.py:289
  165.6 2.2 constant_dynamic-slice_fusion
  168.6 1.9 copy.44.after
  170.5 33.9 %collective-permute-done.8.incoming = bf16[512,2048]{1,0:T(8,128)(2,1)S(1)} collective-permute-done((bf16[512,2048]{1,0:T(8,128)(2,1)}, bf16[512,2048]{1,0:T(8,128)(2,1)S(1)}, u32[]{:S(2)}, u32[]{:S(2)}) %collective-permute-start.8) | collective-permute-done | bytes 2097184 | tf_op jit(solution)/shard_map/ppermute | solution.py:36
  205.8 6.4 %shard_map.140 = (bf16[512,2048]{1,0:T(8,128)(2,1)}, bf16[512,2048]{1,0:T(8,128)(2,1)}) custom-call(bf16[512,2048]{1,0:T(8,128)(2,1)} %get-tuple-element.23.grad, bf16[512,2048]{1,0:T(8,128)(2,1)} %copy-done.31, bf16[6,16,128,128]{3,2,1,0:T(8,128)(2,1)} %refs_3_.3, bf16[6,16,128,128]{3,2,1,0:T(8,128)(2,1)} %refs_7_.3, ...), custom_call_target="tpu_custom_call" | custom-call | flops 536870912 | bytes 14680064 | tf_op jit(solution)/shard_map/pallas_call | solution.py:289
  212.3 2.3 dynamic-slice_bitcast_fusion.3
  215.0 11.8 %collective-permute-done.25 = bf16[1,2,16,2,2,16,128]{6,5,2,1,3,4,0:T(8,128)(2,1)} collective-permute-done((bf16[1,2,16,2,2,16,128]{6,5,2,1,3,4,0:T(8,128)(2,1)}, bf16[1,2,16,2,2,16,128]{6,5,2,1,3,4,0:T(8,128)(2,1)}, u32[]{:S(2)}, u32[]{:S(2)}) %collective-permute-start.25) | collective-permute-done | bytes 524320 | tf_op jit(solution)/shard_map/ppermute | solution.py:36
  228.1 2.1 collective-permute-start.26
  231.6 18.8 %shard_map.141 = (bf16[512,2048]{1,0:T(8,128)(2,1)}, bf16[512,2048]{1,0:T(8,128)(2,1)}, bf16[512,2048]{1,0:T(8,128)(2,1)}, bf16[512,2048]{1,0:T(8,128)(2,1)}, bf...) custom-call(s32[16,2]{1,0:T(8,128)} %copy.41.pairs, bf16[512,2048]{1,0:T(8,128)(2,1)} %get-tuple-element.25.grad, ...), custom_call_target="tpu_custom_call" | custom-call | flops 2952790016 | bytes 19923072 | tf_op jit(solution)/shard_map/pallas_call | solution.py:289
  255.6 1.8 fusion.3
  258.3 1.6 collective-permute-start.7
  259.9 6.8 %shard_map.148 = bf16[1,2,16,128,128]{4,3,2,1,0:T(8,128)(2,1)} custom-call(bf16[512,2048]{1,0:T(8,128)(2,1)} %get-tuple-element.21.state, bf16[512,2048]{1,0:T(8,128)(2,1)} %copy-done.10, bf16[512,2048]{1,0:T(8,128)(2,1)} %get-tuple-element.25.grad, bf16[2,512,512]{2,1,0:T(8,128)(2,1)} %copy-done.19), custom_call_target="tpu_custom_call" | custom-call | flops 536870912 | bytes 8388608 | tf_op jit(solution)/shard_map/pallas_call | solution.py:289
  266.7 1.5 fusion.2.refs_4_
  269.1 7.9 %shard_map.142 = bf16[2,2,16,128,128]{4,3,2,1,0:T(8,128)(2,1)} custom-call(bf16[512,2048]{1,0:T(8,128)(2,1)} %get-tuple-element.28.refs_0_, bf16[512,2048]{1,0:T(8,128)(2,1)} %get-tuple-element.29.refs_1_, bf16[512,2048]{1,0:T(8,128)(2,1)} %get-tuple-element.30.refs_2_, bf16[512,2048]{1,0:T(8,128)(2,1)} %get-tuple-element.31.refs_3_, ...), custom_call_target="tpu_custom_call" | custom-call | flops 1073741824 | bytes 10485760 | tf_op jit(solution)/shard_map/pallas_call | solution.py:289
  277.1 2.5 dynamic-slice_bitcast_fusion.1
  279.5 1.7 collective-permute-start.16
  282.8 7.8 %shard_map.145 = bf16[2,2,16,128,128]{4,3,2,1,0:T(8,128)(2,1)} custom-call(bf16[512,2048]{1,0:T(8,128)(2,1)} %get-tuple-element.32.refs_0_, bf16[512,2048]{1,0:T(8,128)(2,1)} %get-tuple-element.33.refs_1_, bf16[512,2048]{1,0:T(8,128)(2,1)} %get-tuple-element.34.refs_2_, bf16[512,2048]{1,0:T(8,128)(2,1)} %get-tuple-element.35.refs_3_, ...), custom_call_target="tpu_custom_call" | custom-call | flops 1073741824 | bytes 10485760 | tf_op jit(solution)/shard_map/pallas_call | solution.py:289
  290.6 2.5 dynamic-slice_bitcast_fusion
  295.5 3.5 all-to-all-start.2
  299.1 2.2 fusion.11
  301.3 2.3 fusion.5.value
  303.6 7.2 %collective-permute-done.16 = bf16[2,2,16,2,2,16,128]{6,5,4,3,2,1,0:T(8,128)(2,1)} collective-permute-done((bf16[2,2,16,2,2,16,128]{6,5,4,3,2,1,0:T(8,128)(2,1)}, bf16[2,2,16,2,2,16,128]{6,5,4,3,2,1,0:T(8,128)(2,1)}, u32[]{:S(2)}, u32[]{:S(2)}) %collective-permute-start.16) | collective-permute-done | bytes 1048608 | tf_op jit(solution)/shard_map/ppermute | solution.py:36
  310.8 2.6 fusion.1.value
  313.4 9.6 %collective-permute-done.19 = bf16[2,2,16,2,2,16,128]{6,5,4,3,2,1,0:T(8,128)(2,1)} collective-permute-done((bf16[2,2,16,2,2,16,128]{6,5,4,3,2,1,0:T(8,128)(2,1)}, bf16[2,2,16,2,2,16,128]{6,5,4,3,2,1,0:T(8,128)(2,1)}, u32[]{:S(2)}, u32[]{:S(2)}) %collective-permute-start.19) | collective-permute-done | bytes 1048608 | tf_op jit(solution)/shard_map/ppermute | solution.py:36
  323.0 2.6 fusion.value
  326.9 4.2 %all-to-all-start.3 = ((bf16[8,64,512]{2,1,0:T(8,128)(2,1)}), bf16[8,64,512]{2,1,0:T(8,128)(2,1)}, u32[]{:S(2)}, u32[]{:S(2)}) async-start(bf16[8,64,512]{2,1,0:T(8,128)(2,1)} %bitcast.30), calls=%async_computation.3 | async-start | bytes 1048576 | tf_op jit(solution)/shard_map/all_to_all | solution.py:469
  331.1 1.8 multiply_reduce_fusion
  333.0 1.7 dynamic-slice_bitcast_fusion.10
  334.7 1.9 collective-permute-start.23
  336.6 1.9 dynamic-slice_bitcast_fusion.6
  340.9 1.9 dynamic-slice_bitcast_fusion.5
  344.5 1.5 convolution_convert_fusion
  346.9 1.8 fusion.14.value
  348.7 4.8 %collective-permute-done.17 = bf16[2,2,16,2,16,128]{5,4,3,2,1,0:T(8,128)(2,1)} collective-permute-done((bf16[2,2,16,2,16,128]{5,4,3,2,1,0:T(8,128)(2,1)}, bf16[2,2,16,2,16,128]{5,4,3,2,1,0:T(8,128)(2,1)}, u32[]{:S(2)}, u32[]{:S(2)}) %collective-permute-start.17) | collective-permute-done | bytes 524320 | tf_op jit(solution)/shard_map/ppermute | solution.py:36
  353.5 2.0 fusion.7.value
  355.5 2.5 collective-permute-done.20
  358.0 2.0 fusion.6.value
  362.0 1.5 collective-permute-start.18
  363.5 2.5 add_convert_fusion.1
  366.6 1.6 dynamic-slice_bitcast_fusion.14
  368.2 1.6 collective-permute-start.24
  372.3 12.8 %collective-permute-done.18 = bf16[2,2,16,16,128]{4,3,2,1,0:T(8,128)(2,1)S(1)} collective-permute-done((bf16[2,2,16,16,128]{4,3,2,1,0:T(8,128)(2,1)S(1)}, bf16[2,2,16,16,128]{4,3,2,1,0:T(8,128)(2,1)S(1)}, u32[]{:S(2)}, u32[]{:S(2)}) %collective-permute-start.18) | collective-permute-done | bytes 262176 | tf_op jit(solution)/shard_map/ppermute | solution.py:36
  385.1 8.2 %collective-permute-done.21 = bf16[2,2,16,16,128]{4,3,2,1,0:T(8,128)(2,1)S(1)} collective-permute-done((bf16[2,2,16,16,128]{4,3,2,1,0:T(8,128)(2,1)S(1)}, bf16[2,2,16,16,128]{4,3,2,1,0:T(8,128)(2,1)S(1)}, u32[]{:S(2)}, u32[]{:S(2)}) %collective-permute-start.21) | collective-permute-done | bytes 262176 | tf_op jit(solution)/shard_map/ppermute | solution.py:36
  (152 shorter events, 40.9 us)
Async XLA Ops:
  0.6 10.7 %copy-start.33 = (bf16[64,8,8]{0,2,1:T(8,128)(2,1)S(1)}, bf16[64,8,8]{0,2,1:T(8,128)(2,1)}, u32[]{:S(2)}) copy-start(bf16[64,8,8]{0,2,1:T(8,128)(2,1)} %param.11) | copy-start | bytes 24580
  4.0 21.8 %all-to-all-start = ((bf16[8,64,512]{2,1,0:T(8,128)(2,1)}), bf16[8,64,512]{2,1,0:T(8,128)(2,1)}, u32[]{:S(2)}, u32[]{:S(2)}) async-start(bf16[8,64,512]{2,1,0:T(8,128)(2,1)} %bitcast.2), calls=%async_computation | async-start | bytes 1048576 | tf_op jit(solution)/shard_map/all_to_all | solution.py:353
  12.1 19.6 %copy-start.23 = (bf16[512,512]{1,0:T(8,128)(2,1)S(1)}, bf16[512,512]{1,0:T(8,128)(2,1)}, u32[]{:S(2)}) copy-start(bf16[512,512]{1,0:T(8,128)(2,1)} %param.17) | copy-start | bytes 1572868
  12.1 34.3 %copy-start.12 = (bf16[512,512]{1,0:T(8,128)(2,1)S(1)}, bf16[512,512]{1,0:T(8,128)(2,1)}, u32[]{:S(2)}) copy-start(bf16[512,512]{1,0:T(8,128)(2,1)} %param.9) | copy-start | bytes 1572868
  12.7 33.8 %copy-start.25 = (bf16[512,512]{1,0:T(8,128)(2,1)}, bf16[512,512]{1,0:T(8,128)(2,1)S(1)}, u32[]{:S(2)}) copy-start(bf16[512,512]{1,0:T(8,128)(2,1)S(1)} %mul.56) | copy-start | bytes 1572868
  28.1 18.3 %all-to-all-start.1 = ((bf16[8,64,512]{2,1,0:T(8,128)(2,1)}), bf16[8,64,512]{2,1,0:T(8,128)(2,1)S(1)}, u32[]{:S(2)}, u32[]{:S(2)}) async-start(bf16[8,64,512]{2,1,0:T(8,128)(2,1)} %bitcast.4), calls=%async_computation.1 | async-start | bytes 1048576 | tf_op jit(solution)/shard_map/all_to_all | solution.py:355
  31.7 16.4 %collective-permute-start.4 = (bf16[512,512]{1,0:T(8,128)(2,1)S(1)}, bf16[512,512]{1,0:T(8,128)(2,1)}, u32[]{:S(2)}, u32[]{:S(2)}) collective-permute-start(bf16[512,512]{1,0:T(8,128)(2,1)S(1)} %copy-done.23), channel_id=1, source_target_pairs={{0,2},{1,3},{2,0},{3,1},{4,6},{5,7},{6,4},{7,5},{8,10},{9,11},{10,... | collective-permute-start | bytes 1572872 | tf_op jit(solution)/shard_map/ppermute | solution.py:36
  46.6 14.9 %copy-start.13 = (bf16[512,512]{1,0:T(8,128)(2,1)}, bf16[512,512]{1,0:T(8,128)(2,1)S(1)}, u32[]{:S(2)}) copy-start(bf16[512,512]{1,0:T(8,128)(2,1)S(1)} %fusion.12) | copy-start | bytes 1572868
  46.6 12.6 %collective-permute-start = (bf16[512,512]{1,0:T(8,128)(2,1)S(1)}, bf16[512,512]{1,0:T(8,128)(2,1)}, u32[]{:S(2)}, u32[]{:S(2)}) collective-permute-start(bf16[512,512]{1,0:T(8,128)(2,1)S(1)} %fusion.12), channel_id=1, source_target_pairs={{0,2},{1,3},{2,0},{3,1},{4,6},{5,7},{6,4},{7,5},{8,10},{9,11},{10,... | collective-permute-start | bytes 1572872 | tf_op jit(solution)/shard_map/ppermute | solution.py:36
  62.5 3.0 collective-permute-start.1
  82.5 12.8 %copy-start.15 = (bf16[1,512,512]{2,1,0:T(8,128)(2,1)S(1)}, bf16[1,512,512]{2,1,0:T(8,128)(2,1)}, u32[]{:S(2)}) copy-start(bf16[1,512,512]{2,1,0:T(8,128)(2,1)} %get-tuple-element.44) | copy-start | bytes 1572868
  82.5 12.8 %copy-start.16 = (bf16[1,512,512]{2,1,0:T(8,128)(2,1)S(1)}, bf16[1,512,512]{2,1,0:T(8,128)(2,1)}, u32[]{:S(2)}) copy-start(bf16[1,512,512]{2,1,0:T(8,128)(2,1)} %get-tuple-element.45) | copy-start | bytes 1572868
  82.5 4.4 %collective-permute-start.2 = (bf16[512,2048]{1,0:T(8,128)(2,1)}, bf16[512,2048]{1,0:T(8,128)(2,1)S(1)}, u32[]{:S(2)}, u32[]{:S(2)}) collective-permute-start(bf16[512,2048]{1,0:T(8,128)(2,1)} %get-tuple-element.21.state), channel_id=1, source_target_pairs={{0,1},{1,0},{2,3},{3,2},{4,5},{5,4},{6,7},{7,6},{8,9},{9,8},{10,11... | collective-permute-start | bytes 6291464 | tf_op jit(solution)/shard_map/ppermute | solution.py:36
  87.0 1.4 copy-start.10
  93.8 47.9 %collective-permute-start.3 = (bf16[512,2048]{1,0:T(8,128)(2,1)}, bf16[512,2048]{1,0:T(8,128)(2,1)S(1)}, u32[]{:S(2)}, u32[]{:S(2)}) collective-permute-start(bf16[512,2048]{1,0:T(8,128)(2,1)} %shard_map.137.state), channel_id=1, source_target_pairs={{0,2},{1,3},{2,0},{3,1},{4,6},{5,7},{6,4},{7,5},{8,10},{9,11},{10,... | collective-permute-start | bytes 6291464 | tf_op jit(solution)/shard_map/ppermute | solution.py:36
  95.4 2.7 collective-permute-start.5
  141.7 1.4 copy-start.11
  157.4 47.0 %collective-permute-start.8 = (bf16[512,2048]{1,0:T(8,128)(2,1)}, bf16[512,2048]{1,0:T(8,128)(2,1)S(1)}, u32[]{:S(2)}, u32[]{:S(2)}) collective-permute-start(bf16[512,2048]{1,0:T(8,128)(2,1)} %get-tuple-element.24.after), channel_id=1, source_target_pairs={{0,2},{1,3},{2,0},{3,1},{4,6},{5,7},{6,4},{7,5},{8,10},{9,11},{10,... | collective-permute-start | bytes 6291464 | tf_op jit(solution)/shard_map/ppermute | solution.py:36
  204.4 1.4 copy-start.31
  212.2 18.0 %collective-permute-start.9 = (bf16[512,2048]{1,0:T(8,128)(2,1)}, bf16[512,2048]{1,0:T(8,128)(2,1)S(1)}, u32[]{:S(2)}, u32[]{:S(2)}) collective-permute-start(bf16[512,2048]{1,0:T(8,128)(2,1)} %get-tuple-element.26), channel_id=1, source_target_pairs={{0,1},{1,0},{2,3},{3,2},{4,5},{5,4},{6,7},{7,6},{8,9},{9,8},{10,11... | collective-permute-start | bytes 6291464 | tf_op jit(solution)/shard_map/ppermute | solution.py:36
  212.2 14.7 %collective-permute-start.25 = (bf16[1,2,16,2,2,16,128]{6,5,2,1,3,4,0:T(8,128)(2,1)}, bf16[1,2,16,2,2,16,128]{6,5,2,1,3,4,0:T(8,128)(2,1)}, u32[]{:S(2)}, u32[]{:S(2)}) collective-permute-start(bf16[1,2,16,2,2,16,128]{6,5,2,1,3,4,0:T(8,128)(2,1)} %bitcast.198), channel_id=1, source_target_pairs={{0,8},{4,12},{8,0},{12,4},{16,24},{20,28},{24,16},{28,20},{1,9},{5... | collective-permute-start | bytes 1572872 | tf_op jit(solution)/shard_map/ppermute | solution.py:36
  212.3 14.6 %copy-start.30 = (bf16[1,2,16,2,1,2,16,128]{7,6,5,4,3,2,1,0:T(8,128)(2,1)S(1)}, bf16[1,2,16,2,1,2,16,128]{7,6,5,4,3,2,1,0:T(8,128)(2,1)}, u32[]{:S(2)}) copy-start(bf16[1,2,16,2,1,2,16,128]{7,6,5,4,3,2,1,0:T(8,128)(2,1)} %get-tuple-element.42) | copy-start | bytes 1572868
  214.6 41.0 %collective-permute-start.6 = (bf16[2,512,512]{2,1,0:T(8,128)(2,1)}, bf16[2,512,512]{2,1,0:T(8,128)(2,1)}, u32[]{:S(2)}, u32[]{:S(2)}) collective-permute-start(bf16[2,512,512]{2,1,0:T(8,128)(2,1)} %dynamic-slice_bitcast_fusion.3), channel_id=1, source_target_pairs={{0,1},{1,0},{2,3},{3,2},{4,5},{5,4},{6,7},{7,6},{8,9},{9,8},{10,11... | collective-permute-start | bytes 3145736 | tf_op jit(solution)/shard_map/ppermute | solution.py:36
  228.0 2.1 copy-start.27
  228.1 24.7 %collective-permute-start.26 = (bf16[1,2,16,2,16,128]{5,4,2,1,3,0:T(8,128)(2,1)S(1)}, bf16[1,2,16,2,16,128]{5,4,2,1,3,0:T(8,128)(2,1)}, u32[]{:S(2)}, u32[]{:S(2)}) collective-permute-start(bf16[1,2,16,2,16,128]{5,4,2,1,3,0:T(8,128)(2,1)S(1)} %dynamic-slice_bitcast_fusion.9), channel_id=1, source_target_pairs={{0,4},{4,0},{8,12},{12,8},{16,20},{20,16},{24,28},{28,24},{1,5},{5... | collective-permute-start | bytes 786440 | tf_op jit(solution)/shard_map/ppermute | solution.py:36
  230.1 1.4 copy-start.22
  250.3 2.4 copy-start.28
  251.7 5.8 %copy-start.19 = (bf16[2,512,512]{2,1,0:T(8,128)(2,1)}, bf16[2,512,512]{2,1,0:T(8,128)(2,1)S(1)}, u32[]{:S(2)}) copy-start(bf16[2,512,512]{2,1,0:T(8,128)(2,1)S(1)} %dynamic-slice_bitcast_fusion.2.after) | copy-start | bytes 3145732
  251.7 14.9 %collective-permute-start.10 = (bf16[2,512,512]{2,1,0:T(8,128)(2,1)S(1)}, bf16[2,512,512]{2,1,0:T(8,128)(2,1)}, u32[]{:S(2)}, u32[]{:S(2)}) collective-permute-start(bf16[2,512,512]{2,1,0:T(8,128)(2,1)S(1)} %dynamic-slice_bitcast_fusion.2.after), channel_id=1, source_target_pairs={{0,1},{1,0},{2,3},{3,2},{4,5},{5,4},{6,7},{7,6},{8,9},{9,8},{10,11... | collective-permute-start | bytes 3145736 | tf_op jit(solution)/shard_map/ppermute | solution.py:36
  254.4 140.0 %collective-permute-start.27 = (bf16[1,2,16,16,128]{4,3,2,1,0:T(8,128)(2,1)}, bf16[1,2,16,16,128]{4,3,2,1,0:T(8,128)(2,1)S(1)}, u32[]{:S(2)}, u32[]{:S(2)}) collective-permute-start(bf16[1,2,16,16,128]{4,3,2,1,0:T(8,128)(2,1)} %dynamic-slice_bitcast_fusion.13), channel_id=1, source_target_pairs={{0,16},{4,20},{8,24},{12,28},{16,0},{20,4},{24,8},{28,12},{1,17},{... | collective-permute-start | bytes 393224 | tf_op jit(solution)/shard_map/ppermute | solution.py:36
  258.3 8.3 %copy-start.29 = (bf16[4,512,512]{2,1,0:T(8,128)(2,1)S(1)}, bf16[4,512,512]{2,1,0:T(8,128)(2,1)}, u32[]{:S(2)}) copy-start(bf16[4,512,512]{2,1,0:T(8,128)(2,1)} %get-tuple-element.27) | copy-start | bytes 6291460
  258.3 40.7 %collective-permute-start.7 = (bf16[512,512]{1,0:T(8,128)(2,1)}, bf16[512,512]{1,0:T(8,128)(2,1)}, u32[]{:S(2)}, u32[]{:S(2)}) collective-permute-start(bf16[512,512]{1,0:T(8,128)(2,1)} %dynamic-slice_bitcast_fusion.8), channel_id=1, source_target_pairs={{0,2},{1,3},{2,0},{3,1},{4,6},{5,7},{6,4},{7,5},{8,10},{9,11},{10,... | collective-permute-start | bytes 1572872 | tf_op jit(solution)/shard_map/ppermute | solution.py:36
  268.2 25.0 %collective-permute-start.11 = (bf16[512,512]{1,0:T(8,128)(2,1)S(1)}, bf16[512,512]{1,0:T(8,128)(2,1)S(1)}, u32[]{:S(2)}, u32[]{:S(2)}) collective-permute-start(bf16[512,512]{1,0:T(8,128)(2,1)S(1)} %dynamic-slice_bitcast_fusion.7), channel_id=1, source_target_pairs={{0,2},{1,3},{2,0},{3,1},{4,6},{5,7},{6,4},{7,5},{8,10},{9,11},{10,... | collective-permute-start | bytes 1572872 | tf_op jit(solution)/shard_map/ppermute | solution.py:36
  277.1 4.2 %copy-start.20 = (bf16[1,2,16,128,128]{4,3,2,1,0:T(8,128)(2,1)S(1)}, bf16[1,2,16,128,128]{4,3,2,1,0:T(8,128)(2,1)}, u32[]{:S(2)}) copy-start(bf16[1,2,16,128,128]{4,3,2,1,0:T(8,128)(2,1)} %shard_map.148) | copy-start | bytes 3145732
  279.5 31.3 %collective-permute-start.16 = (bf16[2,2,16,2,2,16,128]{6,5,4,3,2,1,0:T(8,128)(2,1)}, bf16[2,2,16,2,2,16,128]{6,5,4,3,2,1,0:T(8,128)(2,1)}, u32[]{:S(2)}, u32[]{:S(2)}) collective-permute-start(bf16[2,2,16,2,2,16,128]{6,5,4,3,2,1,0:T(8,128)(2,1)} %dynamic-slice_bitcast_fusion.1), channel_id=1, source_target_pairs={{0,8},{4,12},{8,0},{12,4},{16,24},{20,28},{24,16},{28,20},{1,9},{5... | collective-permute-start | bytes 3145736 | tf_op jit(solution)/shard_map/ppermute | solution.py:36
  282.1 19.1 %collective-permute-start.22 = (bf16[1,2,16,2,2,16,128]{6,5,4,3,2,1,0:T(8,128)(2,1)}, bf16[1,2,16,2,2,16,128]{6,5,4,3,2,1,0:T(8,128)(2,1)}, u32[]{:S(2)}, u32[]{:S(2)}) collective-permute-start(bf16[1,2,16,2,2,16,128]{6,5,4,3,2,1,0:T(8,128)(2,1)} %dynamic-slice_bitcast_fusion.4), channel_id=1, source_target_pairs={{0,4},{4,0},{8,12},{12,8},{16,20},{20,16},{24,28},{28,24},{1,5},{5... | collective-permute-start | bytes 1572872 | tf_op jit(solution)/shard_map/ppermute | solution.py:36
  290.6 3.9 copy-start.2
  290.6 3.9 copy-start.24
  293.2 5.9 %copy-start.14 = (bf16[512,512]{1,0:T(8,128)(2,1)S(1)}, bf16[512,512]{1,0:T(8,128)(2,1)}, u32[]{:S(2)}) copy-start(bf16[512,512]{1,0:T(8,128)(2,1)} %copy-done.13) | copy-start | bytes 1572868
  293.2 29.8 %collective-permute-start.19 = (bf16[2,2,16,2,2,16,128]{6,5,4,3,2,1,0:T(8,128)(2,1)}, bf16[2,2,16,2,2,16,128]{6,5,4,3,2,1,0:T(8,128)(2,1)}, u32[]{:S(2)}, u32[]{:S(2)}) collective-permute-start(bf16[2,2,16,2,2,16,128]{6,5,4,3,2,1,0:T(8,128)(2,1)} %dynamic-slice_bitcast_fusion), channel_id=1, source_target_pairs={{0,4},{4,0},{8,12},{12,8},{16,20},{20,16},{24,28},{28,24},{1,5},{5... | collective-permute-start | bytes 3145736 | tf_op jit(solution)/shard_map/ppermute | solution.py:36
  295.5 30.1 %all-to-all-start.2 = ((bf16[8,64,512]{2,1,0:T(8,128)(2,1)}), bf16[8,64,512]{2,1,0:T(8,128)(2,1)S(1)}, u32[]{:S(2)}, u32[]{:S(2)}) async-start(bf16[8,64,512]{2,1,0:T(8,128)(2,1)} %bitcast.28), calls=%async_computation.2 | async-start | bytes 1048576 | tf_op jit(solution)/shard_map/all_to_all | solution.py:467
  299.0 11.8 %copy-start.8 = (bf16[2,2,16,128,128]{4,3,2,1,0:T(8,128)(2,1)S(1)}, bf16[2,2,16,128,128]{4,3,2,1,0:T(8,128)(2,1)}, u32[]{:S(2)}) copy-start(bf16[2,2,16,128,128]{4,3,2,1,0:T(8,128)(2,1)} %shard_map.142) | copy-start | bytes 6291460
  301.3 21.8 %copy-start.9 = (bf16[2,2,16,128,128]{4,3,2,1,0:T(8,128)(2,1)S(1)}, bf16[2,2,16,128,128]{4,3,2,1,0:T(8,128)(2,1)}, u32[]{:S(2)}) copy-start(bf16[2,2,16,128,128]{4,3,2,1,0:T(8,128)(2,1)} %shard_map.145) | copy-start | bytes 6291460
  313.4 12.3 %copy-start.26 = (bf16[512,512]{1,0:T(8,128)(2,1)S(1)}, bf16[512,512]{1,0:T(8,128)(2,1)}, u32[]{:S(2)}) copy-start(bf16[512,512]{1,0:T(8,128)(2,1)} %copy-done.25) | copy-start | bytes 1572868
  325.7 5.4 %copy-start.32 = (f32[64,64]{0,1:T(8,128)S(1)}, f32[64,64]{0,1:T(8,128)}, u32[]{:S(2)}) copy-start(f32[64,64]{0,1:T(8,128)} %fusion.30) | copy-start | bytes 49156
  325.7 7.2 %copy-start.7 = (bf16[8,64,512]{2,1,0:T(8,128)(2,1)}, bf16[8,64,512]{2,1,0:T(8,128)(2,1)S(1)}, u32[]{:S(2)}) copy-start(bf16[8,64,512]{2,1,0:T(8,128)(2,1)S(1)} %all-to-all-done.2) | copy-start | bytes 1572868
  326.9 17.6 %all-to-all-start.3 = ((bf16[8,64,512]{2,1,0:T(8,128)(2,1)}), bf16[8,64,512]{2,1,0:T(8,128)(2,1)}, u32[]{:S(2)}, u32[]{:S(2)}) async-start(bf16[8,64,512]{2,1,0:T(8,128)(2,1)} %bitcast.30), calls=%async_computation.3 | async-start | bytes 1048576 | tf_op jit(solution)/shard_map/all_to_all | solution.py:469
  332.9 7.0 %collective-permute-start.14 = (f32[64,8,8]{0,2,1:T(8,128)S(1)}, f32[64,8,8]{0,2,1:T(8,128)S(1)}, u32[]{:S(2)}, u32[]{:S(2)}) collective-permute-start(f32[64,8,8]{0,2,1:T(8,128)S(1)} %bitcast.216), channel_id=1, source_target_pairs={{0,1},{1,0},{2,3},{3,2},{4,5},{5,4},{6,7},{7,6},{8,9},{9,8},{10,11... | collective-permute-start | bytes 49160 | tf_op jit(solution)/shard_map/ppermute | solution.py:36
  334.7 12.2 %collective-permute-start.23 = (bf16[1,2,16,2,16,128]{5,4,3,2,1,0:T(8,128)(2,1)}, bf16[1,2,16,2,16,128]{5,4,3,2,1,0:T(8,128)(2,1)}, u32[]{:S(2)}, u32[]{:S(2)}) collective-permute-start(bf16[1,2,16,2,16,128]{5,4,3,2,1,0:T(8,128)(2,1)} %dynamic-slice_bitcast_fusion.10), channel_id=1, source_target_pairs={{0,8},{4,12},{8,0},{12,4},{16,24},{20,28},{24,16},{28,20},{1,9},{5... | collective-permute-start | bytes 786440 | tf_op jit(solution)/shard_map/ppermute | solution.py:36
  338.4 15.1 %collective-permute-start.17 = (bf16[2,2,16,2,16,128]{5,4,3,2,1,0:T(8,128)(2,1)}, bf16[2,2,16,2,16,128]{5,4,3,2,1,0:T(8,128)(2,1)}, u32[]{:S(2)}, u32[]{:S(2)}) collective-permute-start(bf16[2,2,16,2,16,128]{5,4,3,2,1,0:T(8,128)(2,1)} %dynamic-slice_bitcast_fusion.6), channel_id=1, source_target_pairs={{0,4},{4,0},{8,12},{12,8},{16,20},{20,16},{24,28},{28,24},{1,5},{5... | collective-permute-start | bytes 1572872 | tf_op jit(solution)/shard_map/ppermute | solution.py:36
  339.9 13.6 %copy-start.6 = (bf16[2,2,16,2,2,16,128]{6,5,4,3,2,1,0:T(8,128)(2,1)S(1)}, bf16[2,2,16,2,2,16,128]{6,5,4,3,2,1,0:T(8,128)(2,1)}, u32[]{:S(2)}) copy-start(bf16[2,2,16,2,2,16,128]{6,5,4,3,2,1,0:T(8,128)(2,1)} %shard_map.143) | copy-start | bytes 3145732
  339.9 4.0 %collective-permute-start.15 = (f32[64,8,8]{0,2,1:T(8,128)S(1)}, f32[64,8,8]{0,2,1:T(8,128)S(1)}, u32[]{:S(2)}, u32[]{:S(2)}) collective-permute-start(f32[64,8,8]{0,2,1:T(8,128)S(1)} %bitcast_add_fusion), channel_id=1, source_target_pairs={{0,2},{1,3},{2,0},{3,1},{4,6},{5,7},{6,4},{7,5},{8,10},{9,11},{10,... | collective-permute-start | bytes 49160 | tf_op jit(solution)/shard_map/ppermute | solution.py:36
  342.8 15.2 %copy-start.5 = (bf16[2,2,16,2,2,16,128]{6,5,4,3,2,1,0:T(8,128)(2,1)S(1)}, bf16[2,2,16,2,2,16,128]{6,5,4,3,2,1,0:T(8,128)(2,1)}, u32[]{:S(2)}) copy-start(bf16[2,2,16,2,2,16,128]{6,5,4,3,2,1,0:T(8,128)(2,1)} %shard_map.146) | copy-start | bytes 3145732
  342.8 15.2 %collective-permute-start.20 = (bf16[2,2,16,2,16,128]{5,4,3,2,1,0:T(8,128)(2,1)}, bf16[2,2,16,2,16,128]{5,4,3,2,1,0:T(8,128)(2,1)}, u32[]{:S(2)}, u32[]{:S(2)}) collective-permute-start(bf16[2,2,16,2,16,128]{5,4,3,2,1,0:T(8,128)(2,1)} %dynamic-slice_bitcast_fusion.5), channel_id=1, source_target_pairs={{0,8},{4,12},{8,0},{12,4},{16,24},{20,28},{24,16},{28,20},{1,9},{5... | collective-permute-start | bytes 1572872 | tf_op jit(solution)/shard_map/ppermute | solution.py:36
  346.1 14.0 %collective-permute-start.12 = (bf16[512,512]{1,0:T(8,128)(2,1)S(1)}, bf16[512,512]{1,0:T(8,128)(2,1)S(1)}, u32[]{:S(2)}, u32[]{:S(2)}) collective-permute-start(bf16[512,512]{1,0:T(8,128)(2,1)S(1)} %convolution_convert_fusion), channel_id=1, source_target_pairs={{0,1},{1,0},{2,3},{3,2},{4,5},{5,4},{6,7},{7,6},{8,9},{9,8},{10,11... | collective-permute-start | bytes 1572872 | tf_op jit(solution)/shard_map/ppermute | solution.py:36
  361.0 5.1 %copy-start.3 = (bf16[512,512]{1,0:T(8,128)(2,1)S(1)}, bf16[512,512]{1,0:T(8,128)(2,1)}, u32[]{:S(2)}) copy-start(bf16[512,512]{1,0:T(8,128)(2,1)} %add_convert_fusion.tie) | copy-start | bytes 1572868
  362.0 23.0 %collective-permute-start.18 = (bf16[2,2,16,16,128]{4,3,2,1,0:T(8,128)(2,1)S(1)}, bf16[2,2,16,16,128]{4,3,2,1,0:T(8,128)(2,1)S(1)}, u32[]{:S(2)}, u32[]{:S(2)}) collective-permute-start(bf16[2,2,16,16,128]{4,3,2,1,0:T(8,128)(2,1)S(1)} %dynamic-slice_bitcast_fusion.12), channel_id=1, source_target_pairs={{0,16},{4,20},{8,24},{12,28},{16,0},{20,4},{24,8},{28,12},{1,17},{... | collective-permute-start | bytes 786440 | tf_op jit(solution)/shard_map/ppermute | solution.py:36
  366.0 19.0 %copy-start.18 = (bf16[2,2,16,2,16,128]{5,4,3,2,1,0:T(8,128)(2,1)S(1)}, bf16[2,2,16,2,16,128]{5,4,3,2,1,0:T(8,128)(2,1)}, u32[]{:S(2)}) copy-start(bf16[2,2,16,2,16,128]{5,4,3,2,1,0:T(8,128)(2,1)} %shard_map.144) | copy-start | bytes 1572868
  366.0 29.9 %collective-permute-start.13 = (bf16[512,512]{1,0:T(8,128)(2,1)S(1)}, bf16[512,512]{1,0:T(8,128)(2,1)S(1)}, u32[]{:S(2)}, u32[]{:S(2)}) collective-permute-start(bf16[512,512]{1,0:T(8,128)(2,1)S(1)} %copy-done.3), channel_id=1, source_target_pairs={{0,2},{1,3},{2,0},{3,1},{4,6},{5,7},{6,4},{7,5},{8,10},{9,11},{10,... | collective-permute-start | bytes 1572872 | tf_op jit(solution)/shard_map/ppermute | solution.py:36
  368.2 25.3 %collective-permute-start.24 = (bf16[1,2,16,16,128]{4,3,2,1,0:T(8,128)(2,1)}, bf16[1,2,16,16,128]{4,3,2,1,0:T(8,128)(2,1)}, u32[]{:S(2)}, u32[]{:S(2)}) collective-permute-start(bf16[1,2,16,16,128]{4,3,2,1,0:T(8,128)(2,1)} %dynamic-slice_bitcast_fusion.14), channel_id=1, source_target_pairs={{0,16},{4,20},{8,24},{12,28},{16,0},{20,4},{24,8},{28,12},{1,17},{... | collective-permute-start | bytes 393224 | tf_op jit(solution)/shard_map/ppermute | solution.py:36
  369.8 23.5 %copy-start.17 = (bf16[2,2,16,2,16,128]{5,4,3,2,1,0:T(8,128)(2,1)S(1)}, bf16[2,2,16,2,16,128]{5,4,3,2,1,0:T(8,128)(2,1)}, u32[]{:S(2)}) copy-start(bf16[2,2,16,2,16,128]{5,4,3,2,1,0:T(8,128)(2,1)} %shard_map.147) | copy-start | bytes 1572868
  370.9 22.6 %copy-start.21 = (bf16[1,2,16,2,16,128]{5,4,3,2,1,0:T(8,128)(2,1)S(1)}, bf16[1,2,16,2,16,128]{5,4,3,2,1,0:T(8,128)(2,1)}, u32[]{:S(2)}) copy-start(bf16[1,2,16,2,16,128]{5,4,3,2,1,0:T(8,128)(2,1)} %shard_map.150) | copy-start | bytes 786436
  370.9 22.5 %collective-permute-start.21 = (bf16[2,2,16,16,128]{4,3,2,1,0:T(8,128)(2,1)S(1)}, bf16[2,2,16,16,128]{4,3,2,1,0:T(8,128)(2,1)S(1)}, u32[]{:S(2)}, u32[]{:S(2)}) collective-permute-start(bf16[2,2,16,16,128]{4,3,2,1,0:T(8,128)(2,1)S(1)} %dynamic-slice_bitcast_fusion.11), channel_id=1, source_target_pairs={{0,16},{4,20},{8,24},{12,28},{16,0},{20,4},{24,8},{28,12},{1,17},{... | collective-permute-start | bytes 786440 | tf_op jit(solution)/shard_map/ppermute | solution.py:36
  394.6 1.3 copy-start.4
  (3 other events, 3.1 us)
